TPU v7x, 128 devices: a whole 4x4x4 slice. The times are simulated.
128 devices in a mesh: gx: 16 (over x, z), gy: 8 (over y, core).
Axes of the slice: x: 4, y: 4, z: 4, core: 2. Of those that a mesh axis runs over, the one named last changes fastest.
Arguments:
- particle_data: float32 [5, 128, 128, 3072], P(None, ('gx', 'gy')), as said below
- particle_cells: int32 [2, 128, 128, 3072], P(None, ('gx', 'gy')), may hold values from 0 to 1023, as said below
- slot_counts: int32 [128, 128], P(('gx', 'gy')), may hold values from 0 to 3072, as said below
- fluid_velocity: float32 [3, 64, 128, 1024], P(None, None, 'gx', 'gy'), may hold values from -6 to 6
Outputs:
- pressure: float32 [64, 128, 1024], P(None, 'gx', 'gy')
- drag_force: float32 [3, 128, 128, 3072], P(None, ('gx', 'gy'))
Inputs may be any that keep to these rules, and one draw needn't show every extreme that they name: `slot_counts`: holder h has live particles only in the fluid boxes whose length position differs from box h's by at most 2 and whose width position differs by at most 1; elsewhere its counts are 0. In those boxes its counts are at least 384 and vary with a density level of the fluid box, from one to four; one of those boxes is full to 3072. `particle_data`: volumes lie between 0.5 and 3, drag coefficients between 0.5 and 5; velocities are of order one. `particle_cells`: row 0 holds heights 0 to 63, row 1 columns 0 to 1023.
All inputs are finite; a program needn't handle non-finite values.
Results may differ from a plain program's by a relative error of at most 0.0001.
Values sent between devices are 32-bit elements; how exact they have to be, the bound alone decides.
No kernel may reach another device: no remote copies, remote signals or barrier semaphores. Data moves between devices by JAX's collectives and lax.ppermute only.
A program may use at most 192 MiB of HBM per device.

v0:
```python
import jax
import jax.numpy as jnp
from jax import lax
from jax.sharding import PartitionSpec as P

ITERS = 3


TIME_STEP = 0.1
SHIFT = 0.05
REACH_X = (-2, -1, 0, 1, 2)
REACH_Y = (-1, 0, 1)


def extended(block, sides, width):
    for axis, dim in sides:
        count = lax.axis_size(axis)
        forward = [(i, i + 1) for i in range(count - 1)]
        backward = [(target, source) for source, target in forward]
        low = lax.ppermute(
            lax.slice_in_dim(block, block.shape[dim] - width, None, axis=dim), axis, forward
        )
        high = lax.ppermute(lax.slice_in_dim(block, 0, width, axis=dim), axis, backward)
        block = jnp.concatenate([low, block, high], axis=dim)
    return block


def passed_along(shard, axis, by):
    count = lax.axis_size(axis)
    pairs = [(i, i + by) for i in range(count) if 0 <= i + by < count]
    return lax.ppermute(shard, axis, pairs)


def neighbours(padded):
    return [
        padded[2:, 1:-1, 1:-1],
        padded[:-2, 1:-1, 1:-1],
        padded[1:-1, 2:, 1:-1],
        padded[1:-1, :-2, 1:-1],
        padded[1:-1, 1:-1, 2:],
        padded[1:-1, 1:-1, :-2],
    ]


def face_weights(padded_eps):
    center = padded_eps[1:-1, 1:-1, 1:-1]
    return [2.0 * center * around / (center + around) for around in neighbours(padded_eps)]


def apply_operator(padded, weights, diagonal):
    result = diagonal * padded[1:-1, 1:-1, 1:-1]
    for weight_face, value_face in zip(weights, neighbours(padded)):
        result = result - weight_face * value_face
    return result


def differences(padded):
    along_z = (padded[2:, 1:-1, 1:-1] - padded[:-2, 1:-1, 1:-1]) * 0.5
    along_x = (padded[1:-1, 2:, 1:-1] - padded[1:-1, :-2, 1:-1]) * 0.5
    along_y = (padded[1:-1, 1:-1, 2:] - padded[1:-1, 1:-1, :-2]) * 0.5
    return (along_x, along_y, along_z)


def pad_depth(field):
    return jnp.pad(field, ((1, 1), (0, 0), (0, 0)))


def direction_rim(field):
    return pad_depth(extended(field, (("gx", 1), ("gy", 2)), 1))


def global_norm(residual, scaled):
    return lax.psum(jnp.sum(residual * scaled), ("gx", "gy"))


def locate(step_x, step_y):
    width_x = lax.axis_size("gx")
    width_y = lax.axis_size("gy")
    target_x = lax.axis_index("gx") + step_x
    target_y = lax.axis_index("gy") + step_y
    valid = (target_x >= 0) & (target_x < width_x) & (target_y >= 0) & (target_y < width_y)
    column = jnp.clip(target_x * width_y + target_y, 0, width_x * width_y - 1)
    return (column, valid.astype(jnp.float32))


def pick_block(outgoing, step_x, step_y):
    column, valid = locate(step_x, step_y)
    return lax.dynamic_index_in_dim(outgoing, column, 1, keepdims=False) * valid


def place_block(result, block, step_x, step_y):
    column, valid = locate(step_x, step_y)
    return result.at[:, column].add(block * valid)


def per_device(particle_data, particle_cells, slot_counts, fluid_velocity):
    device_count = lax.axis_size(("gx", "gy"))
    width_y = lax.axis_size("gy")
    capacity = particle_data.shape[3]
    depth, rows_x, rows_y = fluid_velocity.shape[1:]
    occupied = (
        lax.broadcasted_iota(jnp.int32, (device_count, capacity), 1) < slot_counts[0][:, None]
    ).astype(jnp.float32)
    cell_flat = particle_cells[0, 0] * (rows_x * rows_y) + particle_cells[1, 0]
    outgoing = (
        jnp.concatenate([particle_data[:, 0], cell_flat.astype(jnp.float32)[None]], axis=0)
        * occupied[None]
    )
    arrived = []
    for step_x in REACH_X:
        for step_y in REACH_Y:
            block = pick_block(outgoing, step_x, step_y)
            arrived.append(passed_along(block, ("gx", "gy"), step_x * width_y + step_y))
    incoming = jnp.stack(arrived, axis=1)
    blocks_in = incoming.shape[1]
    cell_index = incoming[5].reshape(-1).astype(jnp.int32)
    volume = incoming[0]
    coefficient = incoming[1]
    velocity = incoming[2:5]
    deposit_terms = jnp.stack(
        [
            volume,
            coefficient,
            coefficient * velocity[0],
            coefficient * velocity[1],
            coefficient * velocity[2],
        ]
    ).reshape(5, -1)
    deposited = (
        jnp.zeros((5, depth * rows_x * rows_y), jnp.float32).at[:, cell_index].add(deposit_terms)
    )
    deposited = deposited.reshape(5, depth, rows_x, rows_y)
    fraction = deposited[0]
    porosity = 1.0 / (1.0 + fraction)
    predicted = fluid_velocity + TIME_STEP * (1.0 + fraction)[None] * (
        deposited[2:5] - deposited[1][None] * fluid_velocity
    )
    fluxes = porosity[None] * predicted
    stacked = jnp.stack([porosity, fluxes[0], fluxes[1]])
    rimmed = extended(stacked, (("gx", 2), ("gy", 3)), 1)
    rimmed = jnp.pad(rimmed, ((0, 0), (1, 1), (0, 0), (0, 0)))
    weights = face_weights(rimmed[0])
    diagonal = SHIFT * porosity
    for weight_face in weights:
        diagonal = diagonal + weight_face
    source_term = -(
        differences(rimmed[1])[0]
        + differences(rimmed[2])[1]
        + differences(jnp.pad(fluxes[2], 1))[2]
    )
    pressure = jnp.zeros_like(porosity)
    residual = source_term
    scaled = residual / diagonal
    direction = scaled
    norm_now = global_norm(residual, scaled)
    for iteration in range(ITERS):
        product_field = apply_operator(direction_rim(direction), weights, diagonal)
        step_length = norm_now / lax.psum(jnp.sum(direction * product_field), ("gx", "gy"))
        pressure = pressure + step_length * direction
        if iteration + 1 < ITERS:
            residual = residual - step_length * product_field
            scaled = residual / diagonal
            norm_next = global_norm(residual, scaled)
            direction = scaled + norm_next / norm_now * direction
            norm_now = norm_next
    pressure_padded = pad_depth(extended(pressure, (("gx", 1), ("gy", 2)), 1))
    gradient = differences(pressure_padded)
    cell_table = jnp.stack(
        [predicted[0], predicted[1], predicted[2], gradient[0], gradient[1], gradient[2]]
    ).reshape(6, -1)
    at_particles = cell_table[:, cell_index].reshape(6, blocks_in, capacity)
    forces = coefficient[None] * (at_particles[0:3] - velocity) - volume[None] * at_particles[3:6]
    returned = jnp.zeros((3, device_count, capacity), jnp.float32)
    position = 0
    for step_x in REACH_X:
        for step_y in REACH_Y:
            back = passed_along(forces[:, position], ("gx", "gy"), -(step_x * width_y + step_y))
            returned = place_block(returned, back, step_x, step_y)
            position = position + 1
    return (pressure, returned[:, None])


def solution(mesh):
    return jax.shard_map(
        per_device,
        mesh=mesh,
        in_specs=(
            P(None, ("gx", "gy"), None, None),
            P(None, ("gx", "gy"), None, None),
            P(("gx", "gy"), None),
            P(None, None, "gx", "gy"),
        ),
        out_specs=(P(None, "gx", "gy"), P(None, ("gx", "gy"), None, None)),
        check_vma=False,
    )
```

profile of v0, /device:TPU:10, one launch (start us, length us, event | category | flops | bytes accessed | tf_op | source)
XLA Modules:
  0.0 1262.0 jit_solution(265473428970808231)
XLA Ops:
  2.9 8.1 copy.64
  21.5 5.1 collective-permute-start
  44.1 4.8 collective-permute-start.9
  55.5 9.9 collective-permute-start.12
  69.0 5.0 collective-permute-start.14
  80.9 10.9 copy.34
  92.0 301.8 %scatter_custom_fusion = f32[5,65536]{0,1:T(8,128)} fusion(s32[46080]{0:T(1024)S(1)} %bitcast.198, f32[46080,5]{1,0:T(8,128)} %copy.34, f32[]{:T(128)} %constant.375.clone.1), kind=kCustom, calls=%fused_computation.6 | custom fusion | flops 230400 | bytes 1311232 | tf_op jit(solution)/shard_map/scatter-add | solution.py:130
  393.8 25.2 %slice.734 = f32[3,65536]{0,1:T(8,128)} slice(f32[5,65536]{0,1:T(8,128)} %scatter_custom_fusion), slice={[2:5], [0:65536]} | slice | bytes 1572864 | tf_op jit(solution)/shard_map/slice | solution.py:136
  419.0 41.2 %multiply_reduce_fusion = (f32[65536]{0:T(1024)S(1)}, f32[65536]{0:T(1024)S(1)}, f32[65536]{0:T(1024)S(1)}) fusion(f32[5,65536]{0,1:T(8,128)} %scatter_custom_fusion), kind=kLoop, calls=%fused_computation.4 | loop fusion | flops 196608 | bytes 1310720 | tf_op jit(solution)/shard_map/mul | solution.py:135
  460.2 18.0 %copy.35 = f32[3,64,8,128]{3,2,1,0:T(8,128)S(1)} copy(f32[3,64,8,128]{0,3,2,1:T(8,128)} %bitcast.181) | data formatting | bytes 1572864 | tf_op jit(solution)/shard_map/slice | solution.py:136
  481.4 6.0 collective-permute-start.16
  493.4 11.0 collective-permute-start.17
  504.9 9.9 collective-permute-start.18
  523.9 5.0 collective-permute-start.19
  540.6 4.9 collective-permute-done.21
  549.3 68.3 %all-reduce.6 = (f32[]{:T(128)}, f32[]{:T(128)}) all-reduce(f32[]{:T(128)} %get-tuple-element.186, f32[]{:T(128)} %get-tuple-element.185), channel_id=1, replica_groups=mesh['gx'=16,'gy'=8] {'gx','gy'}, use_global_device_ids=true, to_apply=%region_2.3 | all-reduce | flops 2 | bytes 16 | tf_op jit(solution)/shard_map/psum | solution.py:73
  619.6 64.2 %psum.44 = f32[]{:T(128)} all-reduce(f32[]{:T(128)} %get-tuple-element.205), channel_id=1, replica_groups=mesh['gx'=16,'gy'=8] {'gx','gy'}, use_global_device_ids=true, to_apply=%region_6.7 | all-reduce | flops 1 | bytes 8 | tf_op jit(solution)/shard_map/psum | solution.py:73
  687.2 6.0 collective-permute-start.24
  700.7 4.9 collective-permute-done.25
  709.3 66.8 %psum.45 = f32[]{:T(128)} all-reduce(f32[]{:T(128)} %get-tuple-element.203), channel_id=1, replica_groups=mesh['gx'=16,'gy'=8] {'gx','gy'}, use_global_device_ids=true, to_apply=%region_8.9 | all-reduce | flops 1 | bytes 8 | tf_op jit(solution)/shard_map/psum | solution.py:158
  778.1 61.9 %psum.46 = f32[]{:T(128)} all-reduce(f32[]{:T(128)} %multiply_reduce_fusion.1), channel_id=1, replica_groups=mesh['gx'=16,'gy'=8] {'gx','gy'}, use_global_device_ids=true, to_apply=%region_10.11 | all-reduce | flops 1 | bytes 8 | tf_op jit(solution)/shard_map/psum | solution.py:73
  844.3 5.1 collective-permute-start.28
  866.3 66.3 %psum.47 = f32[]{:T(128)} all-reduce(f32[]{:T(128)} %fusion.21), channel_id=1, replica_groups=mesh['gx'=16,'gy'=8] {'gx','gy'}, use_global_device_ids=true, to_apply=%region_12.13 | all-reduce | flops 1 | bytes 8 | tf_op jit(solution)/shard_map/psum | solution.py:158
  940.7 5.9 collective-permute-done.32
  962.0 16.8 %copy.40 = f32[6,65536]{0,1:T(8,128)} copy(f32[6,65536]{1,0:T(8,128)S(1)} %pad_maximum_fusion) | data formatting | bytes 3145728 | tf_op jit(solution)/shard_map/stack | solution.py:168
  978.8 162.7 %gather_fusion = f32[46080,6]{1,0:T(8,128)} fusion(f32[6,65536]{0,1:T(8,128)} %copy.40, s32[46080]{0:T(1024)S(1)} %broadcast_clamp_fusion), kind=kCustom, calls=%fused_computation | custom fusion | bytes 2396160 | tf_op jit(solution)/shard_map/gather | solution.py:171
  1141.4 32.3 %fusion.71 = (f32[3,46080]{0,1:T(8,128)}, f32[3,46080]{0,1:T(8,128)}) fusion(f32[6,46080]{0,1:T(8,128)} %bitcast.182), kind=kLoop, calls=%fused_computation.296 | loop fusion | bytes 2211840 | tf_op jit(solution)/shard_map/slice | solution.py:172
  1173.8 12.3 copy.41
  1186.1 12.4 copy.42
  1206.1 4.9 collective-permute-start.37
  1215.2 5.2 collective-permute-start.40
  1254.3 4.9 copy.44
  (206 shorter events, 185.0 us)
Async XLA Ops:
  21.5 15.2 %collective-permute-start = (f32[6,3072]{1,0:T(8,128)S(1)}, f32[6,3072]{1,0:T(8,128)S(1)}, u32[]{:S(2)}, u32[]{:S(2)}) collective-permute-start(f32[6,3072]{1,0:T(8,128)S(1)} %get-tuple-element.234), channel_id=1, source_target_pairs={{17,0},{18,1},{19,2},{20,3},{21,4},{22,5},{23,6},{24,7},{25,8},{26... | collective-permute-start | bytes 221192 | tf_op jit(solution)/shard_map/ppermute | solution.py:31
  26.6 12.2 collective-permute-start.1
  29.2 12.8 %collective-permute-start.2 = (f32[6,3072]{1,0:T(8,128)S(1)}, f32[6,3072]{1,0:T(8,128)S(1)}, u32[]{:S(2)}, u32[]{:S(2)}) collective-permute-start(f32[6,3072]{1,0:T(8,128)S(1)} %get-tuple-element.232), channel_id=1, source_target_pairs={{15,0},{16,1},{17,2},{18,3},{19,4},{20,5},{21,6},{22,7},{23,8},{24... | collective-permute-start | bytes 221192 | tf_op jit(solution)/shard_map/ppermute | solution.py:31
  31.2 11.0 collective-permute-start.3
  33.4 10.7 collective-permute-start.4
  36.8 12.2 collective-permute-start.5
  38.8 14.4 %collective-permute-start.6 = (f32[6,3072]{1,0:T(8,128)S(1)}, f32[6,3072]{1,0:T(8,128)S(1)}, u32[]{:S(2)}, u32[]{:S(2)}) collective-permute-start(f32[6,3072]{1,0:T(8,128)S(1)} %get-tuple-element.228), channel_id=1, source_target_pairs={{1,0},{2,1},{3,2},{4,3},{5,4},{6,5},{7,6},{8,7},{9,8},{10,9},{11,1... | collective-permute-start | bytes 221192 | tf_op jit(solution)/shard_map/ppermute | solution.py:31
  42.1 13.4 %collective-permute-start.7 = (f32[6,3072]{1,0:T(8,128)S(1)}, f32[6,3072]{1,0:T(8,128)S(1)}, u32[]{:S(2)}, u32[]{:S(2)}) collective-permute-start(f32[6,3072]{1,0:T(8,128)S(1)} %get-tuple-element.227), channel_id=1, source_target_pairs={{0,0},{1,1},{2,2},{3,3},{4,4},{5,5},{6,6},{7,7},{8,8},{9,9},{10,10... | collective-permute-start | bytes 221192 | tf_op jit(solution)/shard_map/ppermute | solution.py:31
  42.1 23.3 %collective-permute-start.8 = (f32[6,3072]{1,0:T(8,128)S(1)}, f32[6,3072]{1,0:T(8,128)S(1)}, u32[]{:S(2)}, u32[]{:S(2)}) collective-permute-start(f32[6,3072]{1,0:T(8,128)S(1)} %get-tuple-element.226), channel_id=1, source_target_pairs={{0,1},{1,2},{2,3},{3,4},{4,5},{5,6},{6,7},{7,8},{8,9},{9,10},{10,1... | collective-permute-start | bytes 221192 | tf_op jit(solution)/shard_map/ppermute | solution.py:31
  44.1 24.9 %collective-permute-start.9 = (f32[6,3072]{1,0:T(8,128)S(1)}, f32[6,3072]{1,0:T(8,128)S(1)}, u32[]{:S(2)}, u32[]{:S(2)}) collective-permute-start(f32[6,3072]{1,0:T(8,128)S(1)} %get-tuple-element.225), channel_id=1, source_target_pairs={{0,7},{1,8},{2,9},{3,10},{4,11},{5,12},{6,13},{7,14},{8,15},{9,16}... | collective-permute-start | bytes 221192 | tf_op jit(solution)/shard_map/ppermute | solution.py:31
  49.0 25.0 %collective-permute-start.10 = (f32[6,3072]{1,0:T(8,128)S(1)}, f32[6,3072]{1,0:T(8,128)S(1)}, u32[]{:S(2)}, u32[]{:S(2)}) collective-permute-start(f32[6,3072]{1,0:T(8,128)S(1)} %get-tuple-element.224), channel_id=1, source_target_pairs={{0,8},{1,9},{2,10},{3,11},{4,12},{5,13},{6,14},{7,15},{8,16},{9,17... | collective-permute-start | bytes 221192 | tf_op jit(solution)/shard_map/ppermute | solution.py:31
  53.2 20.8 %collective-permute-start.11 = (f32[6,3072]{1,0:T(8,128)S(1)}, f32[6,3072]{1,0:T(8,128)S(1)}, u32[]{:S(2)}, u32[]{:S(2)}) collective-permute-start(f32[6,3072]{1,0:T(8,128)S(1)} %get-tuple-element.223), channel_id=1, source_target_pairs={{0,9},{1,10},{2,11},{3,12},{4,13},{5,14},{6,15},{7,16},{8,17},{9,1... | collective-permute-start | bytes 221192 | tf_op jit(solution)/shard_map/ppermute | solution.py:31
  55.5 18.6 %collective-permute-start.12 = (f32[6,3072]{1,0:T(8,128)S(1)}, f32[6,3072]{1,0:T(8,128)S(1)}, u32[]{:S(2)}, u32[]{:S(2)}) collective-permute-start(f32[6,3072]{1,0:T(8,128)S(1)} %get-tuple-element.222), channel_id=1, source_target_pairs={{0,15},{1,16},{2,17},{3,18},{4,19},{5,20},{6,21},{7,22},{8,23},{9,... | collective-permute-start | bytes 221192 | tf_op jit(solution)/shard_map/ppermute | solution.py:31
  493.4 21.4 %collective-permute-start.17 = (f32[3,64,10,1]{1,3,2,0:T(1,128)S(1)}, f32[3,64,10,1]{1,3,2,0:T(1,128)S(1)}, u32[]{:S(2)}, u32[]{:S(2)}) collective-permute-start(f32[3,64,10,1]{1,3,2,0:T(1,128)S(1)} %copy.36), channel_id=1, source_target_pairs={{0,1},{1,2},{2,3},{3,4},{4,5},{5,6},{6,7},{8,9},{9,10},{10,11},{11... | collective-permute-start | bytes 23048 | tf_op jit(solution)/shard_map/ppermute | solution.py:20
  504.9 11.3 collective-permute-start.18
  535.0 10.5 collective-permute-start.21
  536.9 10.3 collective-permute-start.22
  695.1 10.5 collective-permute-start.25
  851.3 10.5 collective-permute-start.29
  949.0 10.6 collective-permute-start.34
  1199.2 16.0 %collective-permute-start.35 = (f32[3,3072]{1,0:T(4,128)S(1)}, f32[3,3072]{1,0:T(4,128)S(1)}, u32[]{:S(2)}, u32[]{:S(2)}) collective-permute-start(f32[3,3072]{1,0:T(4,128)S(1)} %get-tuple-element.266), channel_id=1, source_target_pairs={{0,17},{1,18},{2,19},{3,20},{4,21},{5,22},{6,23},{7,24},{8,25},{9,... | collective-permute-start | bytes 110600 | tf_op jit(solution)/shard_map/ppermute | solution.py:31
  1202.0 20.8 %collective-permute-start.36 = (f32[3,3072]{1,0:T(4,128)S(1)}, f32[3,3072]{1,0:T(4,128)S(1)}, u32[]{:S(2)}, u32[]{:S(2)}) collective-permute-start(f32[3,3072]{1,0:T(4,128)S(1)} %get-tuple-element.265), channel_id=1, source_target_pairs={{0,16},{1,17},{2,18},{3,19},{4,20},{5,21},{6,22},{7,23},{8,24},{9,... | collective-permute-start | bytes 110600 | tf_op jit(solution)/shard_map/ppermute | solution.py:31
  1206.1 19.2 %collective-permute-start.37 = (f32[3,3072]{1,0:T(4,128)S(1)}, f32[3,3072]{1,0:T(4,128)S(1)}, u32[]{:S(2)}, u32[]{:S(2)}) collective-permute-start(f32[3,3072]{1,0:T(4,128)S(1)} %get-tuple-element.264), channel_id=1, source_target_pairs={{0,15},{1,16},{2,17},{3,18},{4,19},{5,20},{6,21},{7,22},{8,23},{9,... | collective-permute-start | bytes 110600 | tf_op jit(solution)/shard_map/ppermute | solution.py:31
  1211.0 15.0 %collective-permute-start.38 = (f32[3,3072]{1,0:T(4,128)S(1)}, f32[3,3072]{1,0:T(4,128)S(1)}, u32[]{:S(2)}, u32[]{:S(2)}) collective-permute-start(f32[3,3072]{1,0:T(4,128)S(1)} %get-tuple-element.263), channel_id=1, source_target_pairs={{0,9},{1,10},{2,11},{3,12},{4,13},{5,14},{6,15},{7,16},{8,17},{9,1... | collective-permute-start | bytes 110600 | tf_op jit(solution)/shard_map/ppermute | solution.py:31
  1212.9 17.4 %collective-permute-start.39 = (f32[3,3072]{1,0:T(4,128)S(1)}, f32[3,3072]{1,0:T(4,128)S(1)}, u32[]{:S(2)}, u32[]{:S(2)}) collective-permute-start(f32[3,3072]{1,0:T(4,128)S(1)} %get-tuple-element.262), channel_id=1, source_target_pairs={{0,8},{1,9},{2,10},{3,11},{4,12},{5,13},{6,14},{7,15},{8,16},{9,17... | collective-permute-start | bytes 110600 | tf_op jit(solution)/shard_map/ppermute | solution.py:31
  1215.2 20.2 %collective-permute-start.40 = (f32[3,3072]{1,0:T(4,128)S(1)}, f32[3,3072]{1,0:T(4,128)S(1)}, u32[]{:S(2)}, u32[]{:S(2)}) collective-permute-start(f32[3,3072]{1,0:T(4,128)S(1)} %get-tuple-element.261), channel_id=1, source_target_pairs={{0,7},{1,8},{2,9},{3,10},{4,11},{5,12},{6,13},{7,14},{8,15},{9,16}... | collective-permute-start | bytes 110600 | tf_op jit(solution)/shard_map/ppermute | solution.py:31
  1222.7 16.6 %collective-permute-start.41 = (f32[3,3072]{1,0:T(4,128)S(1)}, f32[3,3072]{1,0:T(4,128)S(1)}, u32[]{:S(2)}, u32[]{:S(2)}) collective-permute-start(f32[3,3072]{1,0:T(4,128)S(1)} %get-tuple-element.260), channel_id=1, source_target_pairs={{0,1},{1,2},{2,3},{3,4},{4,5},{5,6},{6,7},{7,8},{8,9},{9,10},{10,1... | collective-permute-start | bytes 110600 | tf_op jit(solution)/shard_map/ppermute | solution.py:31
  1225.3 17.9 %collective-permute-start.42 = (f32[3,3072]{1,0:T(4,128)S(1)}, f32[3,3072]{1,0:T(4,128)S(1)}, u32[]{:S(2)}, u32[]{:S(2)}) collective-permute-start(f32[3,3072]{1,0:T(4,128)S(1)} %get-tuple-element.259), channel_id=1, source_target_pairs={{0,0},{1,1},{2,2},{3,3},{4,4},{5,5},{6,6},{7,7},{8,8},{9,9},{10,10... | collective-permute-start | bytes 110600 | tf_op jit(solution)/shard_map/ppermute | solution.py:31
  1226.0 19.8 %collective-permute-start.43 = (f32[3,3072]{1,0:T(4,128)S(1)}, f32[3,3072]{1,0:T(4,128)S(1)}, u32[]{:S(2)}, u32[]{:S(2)}) collective-permute-start(f32[3,3072]{1,0:T(4,128)S(1)} %get-tuple-element.258), channel_id=1, source_target_pairs={{1,0},{2,1},{3,2},{4,3},{5,4},{6,5},{7,6},{8,7},{9,8},{10,9},{11,1... | collective-permute-start | bytes 110600 | tf_op jit(solution)/shard_map/ppermute | solution.py:31
  1230.3 18.6 %collective-permute-start.44 = (f32[3,3072]{1,0:T(4,128)S(1)}, f32[3,3072]{1,0:T(4,128)S(1)}, u32[]{:S(2)}, u32[]{:S(2)}) collective-permute-start(f32[3,3072]{1,0:T(4,128)S(1)} %get-tuple-element.257), channel_id=1, source_target_pairs={{7,0},{8,1},{9,2},{10,3},{11,4},{12,5},{13,6},{14,7},{15,8},{16,9}... | collective-permute-start | bytes 110600 | tf_op jit(solution)/shard_map/ppermute | solution.py:31
  1235.4 16.2 %collective-permute-start.45 = (f32[3,3072]{1,0:T(4,128)S(1)}, f32[3,3072]{1,0:T(4,128)S(1)}, u32[]{:S(2)}, u32[]{:S(2)}) collective-permute-start(f32[3,3072]{1,0:T(4,128)S(1)} %get-tuple-element.256), channel_id=1, source_target_pairs={{8,0},{9,1},{10,2},{11,3},{12,4},{13,5},{14,6},{15,7},{16,8},{17,9... | collective-permute-start | bytes 110600 | tf_op jit(solution)/shard_map/ppermute | solution.py:31
  1239.3 13.1 %collective-permute-start.46 = (f32[3,3072]{1,0:T(4,128)S(1)}, f32[3,3072]{1,0:T(4,128)S(1)}, u32[]{:S(2)}, u32[]{:S(2)}) collective-permute-start(f32[3,3072]{1,0:T(4,128)S(1)} %get-tuple-element.255), channel_id=1, source_target_pairs={{9,0},{10,1},{11,2},{12,3},{13,4},{14,5},{15,6},{16,7},{17,8},{18,... | collective-permute-start | bytes 110600 | tf_op jit(solution)/shard_map/ppermute | solution.py:31
  (32 other events, 777.2 us)
where the time goes:
time: 1280 us; the launch traced here: 1260 us
  other arithmetic  383 us (30%)
  blocking collectives  328 us (26%)
  local copies, waits for them, and re-layouts  323 us (25%)
  starting transfers between devices  175 us (14%)
  waiting for transfers between devices  44.9 us (4%)
    scatter-add x1, other arithmetic, per_device(): jnp.zeros((5, depth * rows_x * rows_y), jnp.float32).at[:, cell_index]  302 us
    psum x3, blocking collectives, global_norm(): return lax.psum(jnp.sum(residual * scaled), ('gx', 'gy'))  194 us
    gather x1, local copies, waits for them, and re-layouts, per_device(): at_particles = cell_table[:, cell_index].reshape(6, blocks_in, capacity)  163 us
    psum x2, blocking collectives, per_device(): lax.psum(jnp.sum(direction * product_field), ('gx', 'gy'))  133 us
    ppermute x30, starting transfers between devices, passed_along(): return lax.ppermute(shard, axis, pairs)  94 us
    ppermute x10, starting transfers between devices, extended(): lax.ppermute(lax.slice_in_dim(block, 0, width, axis=dim), axis, backward)  47.7 us
    slice x2, local copies, waits for them, and re-layouts, per_device(): at_particles[3:6]  44.8 us
    slice x2, local copies, waits for them, and re-layouts, per_device(): deposited[2:5] - deposited[1][None] * fluid_velocity  43.2 us
  transfers between devices with their start and end apart: 50, of which 17 were waited for; matrix products, arithmetic and copies ran while one was open for 2% of the time, Pallas kernels for 0%

commit v1 on v0

v1 whole, which is shorter than its diff:
```python
import functools
import jax
import jax.numpy as jnp
from jax import lax
from jax.experimental import pallas as pl
from jax.experimental.pallas import tpu as pltpu
from jax.sharding import PartitionSpec as P

f32, bf16, i32 = jnp.float32, jnp.bfloat16, jnp.int32
CH = 24
BR = 152
WL = 16
NW = 32
SPAN = WL * 128
VM = pltpu.CompilerParams(vmem_limit_bytes=56 * 1024 * 1024)


def sort_network(x):
    lane = lax.broadcasted_iota(i32, (1, 8, 128), 2)
    flipped = None
    for merge in range(1, 13):
        if merge < 12:
            if merge >= 5:
                want = (lane >> (merge - 5)) & 1
                mask = -want
            else:
                mask = jnp.asarray(-((lax.broadcasted_iota(i32, (32, 8, 128), 0) >> merge) & 1))
        else:
            mask = None
        if mask is not None:
            x = x ^ mask
        for bit in range(merge - 1, -1, -1):
            if bit < 5:
                step = 1 << bit
                y = x.reshape(32 // (2 * step), 2, step, 8, 128)
                a, b = y[:, 0], y[:, 1]
                x = jnp.stack([jnp.minimum(a, b), jnp.maximum(a, b)], axis=1).reshape(32, 8, 128)
            else:
                step = 1 << (bit - 5)
                up = (lane & step) != 0
                other = jnp.where(up, pltpu.roll(x, step, 2), pltpu.roll(x, 128 - step, 2))
                x = jnp.where(up, jnp.maximum(x, other), jnp.minimum(x, other))
        if mask is not None:
            x = x ^ mask
    return x


def lanes_to_chunks(x):
    lane = lax.broadcasted_iota(i32, (1, 8, 128), 2)
    for bit in range(5):
        step = 1 << bit
        y = x.reshape(32 // (2 * step), 2, step, 8, 128)
        a, b = y[:, 0], y[:, 1]
        up = ((lane & step) != 0)[:, None]
        na = jnp.where(up, pltpu.roll(b, step, 3), a)
        nb = jnp.where(up, b, pltpu.roll(a, 128 - step, 3))
        x = jnp.stack([na, nb], axis=1).reshape(32, 8, 128)
    for bit in range(2):
        step, far = 1 << bit, 32 << bit
        y = x.reshape(32 // (2 * step), 2, step, 8, 128)
        a, b = y[:, 0], y[:, 1]
        up = ((lane & far) != 0)[:, None]
        na = jnp.where(up, pltpu.roll(b, far, 3), a)
        nb = jnp.where(up, b, pltpu.roll(a, 128 - far, 3))
        x = jnp.stack([na, nb], axis=1).reshape(32, 8, 128)
    return jnp.stack([x[(c % 8) * 4 + c // 8] for c in range(32)], axis=0)


GROUPS = (((-2, -1, 0, 3), (2, -1, 3, 3), (0, -1, 6, 2)), ((-1, -1, 0, 3), (1, -1, 3, 3), (0, 1, 6, 1)))
NGX, NGY = 16, 8


def row_mask(first, count):
    row = lax.broadcasted_iota(i32, (8, 128), 0)
    return (row >= first) & (row < first + count)


def sort_kernel(runs, n_out, data_ref, cells_ref, counts_ref, *rest):
    outs, pos_ref = rest[:n_out], rest[n_out]
    data_v, cells_v, key_s, pay_s, out_s, sems = rest[n_out + 1:]
    hx, hy = lax.axis_index("gx"), lax.axis_index("gy")
    copies = []
    for t, (dx, _, _, _) in enumerate(runs):
        tile = pl.ds(pl.multiple_of(jnp.clip(hx + dx, 0, NGX - 1) * 8, 8), 8)
        copies.append(pltpu.make_async_copy(data_ref.at[:, 0, tile, :], data_v.at[t], sems.at[2 * t]))
        copies.append(pltpu.make_async_copy(cells_ref.at[:, 0, tile, :], cells_v.at[t], sems.at[2 * t + 1]))
    for copy in copies:
        copy.start()
    lane = lax.broadcasted_iota(i32, (8, 128), 1)
    row = lax.broadcasted_iota(i32, (8, 128), 0)
    counts = jnp.zeros((8, 128), i32)
    for dx, dy0, first, count in runs:
        for i in range(count):
            bx, by = hx + dx, hy + dy0 + i
            valid = (bx >= 0) & (bx < NGX) & (by >= 0) & (by < NGY)
            n = counts_ref[0, jnp.clip(bx * NGY + by, 0, NGX * NGY - 1)]
            counts = jnp.where(row == first + i, jnp.where(valid, n, 0), counts)
    shifts = [lax.rem(first - (hy + dy0) + 16, 8) for _, dy0, first, _ in runs]
    masks = [row_mask(first, count) for _, _, first, count in runs]
    for copy in copies:
        copy.wait()

    def gathered(ref, f, c):
        got = None
        for t in range(len(runs)):
            x = pltpu.roll(ref[t, f, :, c * 128:(c + 1) * 128], shifts[t], 0)
            got = x if got is None else jnp.where(masks[t], x, got)
        return got

    rows = []
    for c in range(32):
        slot = lane + c * 128
        if c < CH:
            h, col = gathered(cells_v, 0, c), gathered(cells_v, 1, c)
            live = slot < counts
            cell = (((col >> 7) * 64 + h) << 7) + (col & 127)
            cell = jnp.where(live, cell, 65536)
            for f in range(5):
                pay_s[f, c] = jnp.where(live, gathered(data_v, f, c), 0.0)
            rows.append((cell << 12) + slot)
        else:
            rows.append((1 << 29) + slot)
    keys = lanes_to_chunks(sort_network(jnp.stack(rows, axis=0)))
    key_s[...] = keys[:CH]
    place = lax.broadcasted_iota(i32, (32, 8, 128), 0) * 128 + lax.broadcasted_iota(i32, (32, 8, 128), 2)
    pad = lax.broadcasted_iota(i32, (32, 8, 128), 0) >= CH
    back = jnp.where(pad, (1 << 29) + place, ((keys & 4095) << 12) + place)
    back = lanes_to_chunks(sort_network(back))
    pos_ref[...] = back[:CH] & 4095

    def chunk(c, _):
        k = key_s[c]
        slot = k & 4095
        at, src = slot & 127, slot >> 7
        acc = [jnp.zeros((8, 128), f32) for _ in range(5)]
        for v in range(CH):
            here = src == v
            for f in range(5):
                got = jnp.take_along_axis(pay_s[f, v], at, axis=1)
                acc[f] = jnp.where(here, got, acc[f])
        for f in range(5):
            out_s[pl.ds(f * CH + c, 8, stride=BR), :] = acc[f]
        out_s[pl.ds(5 * CH + c, 8, stride=BR), :] = (k >> 12).astype(f32)
        return 0
    lax.fori_loop(0, CH, chunk, 0)
    low = lane < 64
    bound = jnp.where(low, lane, lane - 63) * SPAN
    total = jnp.zeros((8, 128), i32)
    for c in range(CH):
        cell = key_s[c] >> 12
        last = jnp.broadcast_to(cell[:, 127:128], (8, 128))
        start = jnp.broadcast_to(cell[:, 0:1], (8, 128))
        total = total + jnp.where(jnp.where(low, last, start) < bound, 1, 0)
    for r in range(8):
        out_s[pl.ds(6 * CH + r, 8, stride=BR), :] = total.astype(f32)
    for out, (_, _, first, count) in zip(outs, runs):
        out[...] = out_s[first * BR:(first + count) * BR, :]


def sort_blocks(runs, data, cells, counts):
    shapes = [jax.ShapeDtypeStruct((count * BR, 128), f32) for _, _, _, count in runs]
    shapes.append(jax.ShapeDtypeStruct((CH, 8, 128), i32))
    n = len(runs)
    return pl.pallas_call(
        functools.partial(sort_kernel, runs, n),
        out_shape=tuple(shapes),
        in_specs=[pl.BlockSpec(memory_space=pl.ANY)] * 2 + [pl.BlockSpec(memory_space=pltpu.SMEM)],
        out_specs=(pl.BlockSpec(memory_space=pltpu.VMEM),) * (n + 1),
        scratch_shapes=[
            pltpu.VMEM((n, 5, 8, 3072), f32),
            pltpu.VMEM((n, 2, 8, 3072), i32),
            pltpu.VMEM((CH, 8, 128), i32),
            pltpu.VMEM((5, CH, 8, 128), f32),
            pltpu.VMEM((8 * BR, 128), f32),
            pltpu.SemaphoreType.DMA((2 * n,)),
        ],
        compiler_params=VM,
        name="sort_blocks",
    )(data, cells, counts)


def load_offsets(refs, off_v, off_s, sem):
    for j, (ref, base) in enumerate(refs):
        off_v[j:j + 1, :] = ref[base + 6 * CH:base + 6 * CH + 1, :].astype(i32)
    copy = pltpu.make_async_copy(off_v, off_s, sem)
    copy.start()
    copy.wait()


def wide(row, rows):
    return jnp.broadcast_to(row, (rows, 128))


def split_cell(cell):
    line = jnp.floor(cell * (1.0 / 128.0))
    return line, cell - line * 128.0


def width_onehot(wid, iota):
    w16 = wide(wid, 16).astype(bf16)
    w = jnp.concatenate([w16] * 8, axis=0)
    return jnp.where(w == iota, jnp.asarray(1.0, bf16), jnp.asarray(0.0, bf16))


def deposit_kernel(nref, per, use_acc, *refs):
    bases = per
    blocks = [(refs[i], b) for i in range(nref) for b in bases]
    nb = len(blocks)
    rest = refs[nref:]
    if use_acc:
        prev, rest = rest[0], rest[1:]
    out, pre, off_v, off_s, sem = rest
    load_offsets(blocks, off_v, off_s, sem)
    for j, (ref, base) in enumerate(blocks):
        vol = ref[base:base + CH, :]
        coef = ref[base + CH:base + 2 * CH, :]
        vals = [vol, coef] + [coef * ref[base + (2 + d) * CH:base + (3 + d) * CH, :] for d in range(3)]
        for k, v in enumerate(vals):
            hi = v.astype(bf16).astype(f32)
            pre[j, k] = hi
            pre[j, 5 + k] = v - hi
        line, wid = split_cell(ref[base + 5 * CH:base + 6 * CH, :])
        pre[j, 10] = line
        pre[j, 11] = wid
    iota = lax.broadcasted_iota(i32, (128, 128), 0).astype(f32).astype(bf16)
    iota16 = lax.broadcasted_iota(i32, (16, 128), 0).astype(f32).astype(bf16)
    zero = jnp.zeros((16, 128), bf16)

    def operands(j, c, w):
        rel = jnp.clip(pre[j, 10, pl.ds(c, 1), :] - (w * WL).astype(f32), -1.0, 16.0)
        mask = wide(rel, 16).astype(bf16) == iota16
        a = jnp.concatenate(
            [jnp.where(mask, wide(pre[j, k, pl.ds(c, 1), :], 16).astype(bf16), zero) for k in range(10)], axis=0)
        return a, width_onehot(pre[j, 11, pl.ds(c, 1), :], iota)

    def product(a, b):
        return lax.dot_general(a, b, (((1,), (1,)), ((), ())), preferred_element_type=f32)

    def window(w, _):
        total = None
        more = 0
        for j in range(nb):
            first = jnp.minimum(off_s[j, w], CH - 2)
            more = jnp.maximum(more, off_s[j, 64 + w] - first)
            a0, b0 = operands(j, first, w)
            a1, b1 = operands(j, first + 1, w)
            p = product(jnp.concatenate([a0, a1], axis=1), jnp.concatenate([b0, b1], axis=1))
            total = p if total is None else total + p
        total = (total[:80] + total[80:]).reshape(5, WL, 128)
        rows = pl.ds(pl.multiple_of(w * WL, WL), WL)
        if use_acc:
            total = total + prev[:, rows, :]
        out[:, rows, :] = total

        @pl.when(more > 2)
        def _():
            def block(j, _):
                def step(c, _):
                    a, b = operands(j, c, w)
                    p = product(a, b)
                    out[:, rows, :] += (p[:80] + p[80:]).reshape(5, WL, 128)
                    return 0
                return lax.fori_loop(jnp.minimum(off_s[j, w], CH - 2) + 2, off_s[j, 64 + w], step, 0)
            lax.fori_loop(0, nb, block, 0)
        return 0
    lax.fori_loop(0, NW, window, 0)


def deposit(arrays, bases, prev=None):
    nb = len(arrays) * len(bases)
    args = list(arrays) + ([] if prev is None else [prev])
    return pl.pallas_call(
        functools.partial(deposit_kernel, len(arrays), bases, prev is not None),
        out_shape=jax.ShapeDtypeStruct((5, 512, 128), f32),
        in_specs=[pl.BlockSpec(memory_space=pltpu.VMEM)] * len(args),
        out_specs=pl.BlockSpec(memory_space=pltpu.VMEM),
        scratch_shapes=[
            pltpu.VMEM((nb, 12, CH, 128), f32),
            pltpu.VMEM((nb, 128), i32),
            pltpu.SMEM((nb, 128), i32),
            pltpu.SemaphoreType.DMA,
        ],
        compiler_params=VM,
        name="deposit",
    )(*args)


def interp_kernel(nref, bases, *refs):
    blocks = [(refs[i], b) for i in range(nref) for b in bases]
    nb = len(blocks)
    table, out, pre, acc, off_v, off_s, sem = refs[nref:]
    load_offsets(blocks, off_v, off_s, sem)
    for j, (ref, base) in enumerate(blocks):
        line, wid = split_cell(ref[base + 5 * CH:base + 6 * CH, :])
        pre[j, 0] = line
        pre[j, 1] = wid
    acc[...] = jnp.zeros_like(acc)
    iota = lax.broadcasted_iota(i32, (128, 128), 0).astype(f32).astype(bf16)
    iota16 = lax.broadcasted_iota(i32, (16, 128), 0).astype(f32)

    def visit(j, c, w, width, tab):
        masks, hots = [], []
        for i in range(width):
            rel = pre[j, 0, pl.ds(c + i, 1), :] - (w * WL).astype(f32)
            masks.append(wide(rel, 16) == iota16)
            b = width_onehot(pre[j, 1, pl.ds(c + i, 1), :], iota)
            hots.append(jnp.concatenate([b, b], axis=0))
        hot = hots[0] if width == 1 else jnp.concatenate(hots, axis=1)
        g = jnp.dot(tab, hot, preferred_element_type=f32)
        for i in range(width):
            for k in range(3):
                part = jnp.where(masks[i], g[k * 16:k * 16 + 16, i * 128:(i + 1) * 128], 0.0)
                acc[j, c + i, k] += part[:8] + part[8:]

    def window(w, _):
        tab = table[w]
        more = 0
        for j in range(nb):
            first = jnp.minimum(off_s[j, w], CH - 2)
            more = jnp.maximum(more, off_s[j, 64 + w] - first)
            visit(j, first, w, 2, tab)

        @pl.when(more > 2)
        def _():
            def block(j, _):
                def step(c, _):
                    visit(j, c, w, 1, tab)
                    return 0
                return lax.fori_loop(jnp.minimum(off_s[j, w], CH - 2) + 2, off_s[j, 64 + w], step, 0)
            lax.fori_loop(0, nb, block, 0)
        return 0
    lax.fori_loop(0, NW, window, 0)
    def fin(j, _):
        for k in range(3):
            out[j, k] = jnp.sum(acc[j, :, k], axis=1)
        return 0
    lax.fori_loop(0, nb, fin, 0)


def interp(arrays, bases, table):
    nb = len(arrays) * len(bases)
    args = list(arrays) + [table]
    return pl.pallas_call(
        functools.partial(interp_kernel, len(arrays), bases),
        out_shape=jax.ShapeDtypeStruct((nb, 3, CH, 128), f32),
        in_specs=[pl.BlockSpec(memory_space=pltpu.VMEM)] * len(args),
        out_specs=pl.BlockSpec(memory_space=pltpu.VMEM),
        scratch_shapes=[
            pltpu.VMEM((nb, 2, CH, 128), f32),
            pltpu.VMEM((nb, CH, 3, 8, 128), f32),
            pltpu.VMEM((nb, 128), i32),
            pltpu.SMEM((nb, 128), i32),
            pltpu.SemaphoreType.DMA,
        ],
        compiler_params=VM,
        name="interp",
    )(*args)


TIME_STEP = 0.1
SHIFT = 0.05
VSPEC = pl.BlockSpec(memory_space=pltpu.VMEM)
S = jax.ShapeDtypeStruct


def put_table(table, k, x, values):
    hi = values.astype(bf16)
    lo = (values - hi.astype(f32)).astype(bf16)
    for q in range(4):
        table[4 * x + q, k * 16:k * 16 + 16, 0:128] = hi[16 * q:16 * q + 16]
        table[4 * x + q, k * 16:k * 16 + 16, 128:256] = lo[16 * q:16 * q + 16]


def fields_kernel(acc, fluid, table, low, high):
    for x in range(8):
        at = slice(x * 64, x * 64 + 64)
        fraction = acc[0, at, :]
        drag = acc[1, at, :]
        porosity = 1.0 / (1.0 + fraction)
        out, r = (low, x) if x < 4 else (high, x - 4)
        out[0, r] = porosity
        for d in range(3):
            fluid_d = fluid[d, pl.ds(x, 64, stride=8), :]
            predicted = fluid_d + TIME_STEP * (1.0 + fraction) * (acc[2 + d, at, :] - drag * fluid_d)
            put_table(table, d, x, predicted)
            out[1 + d, r] = porosity * predicted


def fields(acc, fluid):
    return pl.pallas_call(
        fields_kernel,
        out_shape=(S((NW, 48, 256), bf16), S((4, 4, 64, 128), f32), S((4, 4, 64, 128), f32)),
        in_specs=[VSPEC] * 2,
        out_specs=(VSPEC,) * 3,
        compiler_params=VM,
        name="fields",
    )(acc, fluid)


def pack_kernel(left, low, high, right, out):
    lane = lax.broadcasted_iota(i32, (64, 128), 1)
    for f in range(4):
        got = jnp.zeros((64, 128), f32)
        for r in range(16):
            src = (left, low, high, right)[r // 4][f, r % 4]
            place = lax.rem(lane + 132 - 8 * r, 128) < 8
            got = jnp.where(place, src if r == 0 else pltpu.roll(src, 8 * r, 1), got)
        out[f] = got


def pack_edges(left, low, high, right):
    return pl.pallas_call(
        pack_kernel,
        out_shape=S((4, 64, 128), f32),
        in_specs=[VSPEC] * 4,
        out_specs=VSPEC,
        compiler_params=VM,
        name="pack_edges",
    )(left, low, high, right)


def up_z(x):
    return jnp.concatenate([x[1:], jnp.zeros_like(x[:1])], axis=0)


def down_z(x):
    return jnp.concatenate([jnp.zeros_like(x[:1]), x[:-1]], axis=0)


def up_y(x):
    return pltpu.roll(x, x.shape[1] - 1, 1)


def down_y(x):
    return pltpu.roll(x, 1, 1)


def face(e, n):
    return 2.0 * e * n / jnp.maximum(e + n, 1e-30)


def sweeps_kernel(left, low, high, right, from_left, from_right, vs, moments, ext, wx, wy, wz, diag, inv, src, more):
    lane = lax.broadcasted_iota(i32, (64, 128), 1)
    even = (lane & 7) < 4
    keep = (lane < 4) | (lane >= 124)
    for f in range(4):
        both = jnp.where(even, from_right[f], from_left[f])
        for r in range(16):
            ext[f, r, :, 0:128] = (left, low, high, right)[r // 4][f, r % 4]
            ext[f, r, :, 128:256] = jnp.where(keep, both if r == 0 else pltpu.roll(both, 128 - 8 * r, 1), 0.0)

    def faces(r, _):
        e = ext[0, r]
        wx[r] = face(e, ext[0, jnp.minimum(r + 1, 15)])
        wy[r] = face(e, up_y(e))
        wz[r] = face(e, up_z(e))
        return 0
    lax.fori_loop(0, 16, faces, 0)

    def sources(r, _):
        e = ext[0, r]
        y, z = wy[r], wz[r]
        d = SHIFT * e + wz[r] + down_z(z) + wx[r] + wx[r - 1] + y + down_y(y)
        outside = e == 0.0
        i = jnp.where(outside, 0.0, 1.0 / jnp.where(outside, 1.0, d))
        fy, fz = ext[2, r], ext[3, r]
        b = -0.5 * ((ext[1, r + 1] - ext[1, r - 1]) + (up_y(fy) - down_y(fy)) + (up_z(fz) - down_z(fz)))
        diag[r] = d
        inv[r] = i
        vs[0, r] = b * i
        return 0
    lax.fori_loop(1, 15, sources, 0)

    def spread(k, r):
        v = vs[k, r]
        y, z = wy[r], wz[r]
        total = wx[r] * vs[k, r + 1] + wx[r - 1] * vs[k, r - 1]
        total = total + y * up_y(v) + down_y(y * v)
        total = total + z * up_z(v) + down_z(z * v)
        return (diag[r] * v - total) * inv[r]

    for k, (lo, hi) in ((0, (2, 14)), (1, (3, 13))):
        def image(r, _, k=k):
            vs[k + 1, r] = spread(k, r)
            return 0
        lax.fori_loop(lo, hi, image, 0)

    def sums(r, total):
        d = diag[r][:, 0:128]
        v0, v1, v2 = (vs[k, r][:, 0:128] for k in range(3))
        v3 = spread(2, r)[:, 0:128]
        d0, d1, d2 = d * v0, d * v1, d * v2
        terms = (d0 * v0, d0 * v1, d1 * v1, d1 * v2, d2 * v2, d2 * v3)
        return tuple(t + jnp.sum(x.reshape(8, 8, 128), axis=0) for t, x in zip(total, terms))
    total = lax.fori_loop(4, 12, sums, tuple(jnp.zeros((8, 128), f32) for _ in range(6)))
    for k in range(6):
        moments[k:k + 1, :] = jnp.sum(total[k], axis=0, keepdims=True)
    moments[6:8, :] = jnp.zeros((2, 128), f32)


def sweeps(left, low, high, right, from_left, from_right):
    big = pltpu.VMEM((16, 64, 256), f32)
    return pl.pallas_call(
        sweeps_kernel,
        out_shape=(S((3, 16, 64, 256), f32), S((8, 128), f32)),
        in_specs=[VSPEC] * 6,
        out_specs=(VSPEC,) * 2,
        scratch_shapes=[pltpu.VMEM((4, 16, 64, 256), f32)] + [big] * 7,
        compiler_params=VM,
        name="sweeps",
    )(left, low, high, right, from_left, from_right)


def coefficients(mu):
    def form(a, b, shift):
        return sum(a[i] * b[j] * mu[i + j + shift] for i in range(len(a)) for j in range(len(b)))
    zero = jnp.zeros_like(mu[0])
    one = jnp.ones_like(mu[0])
    pressure = [zero, zero, zero]
    scaled, direction = [one], [one]
    norm = mu[0]
    for sweep in range(3):
        step = norm / form(direction, direction, 1)
        for i, c in enumerate(direction):
            pressure[i] = pressure[i] + step * c
        if sweep < 2:
            moved = [zero] + direction
            old = scaled + [zero] * (len(moved) - len(scaled))
            scaled = [a - step * b for a, b in zip(old, moved)]
            following = form(scaled, scaled, 0)
            ratio = following / norm
            direction = [a + ratio * b for a, b in zip(scaled, direction + [zero])]
            norm = following
    return pressure


def gradient_kernel(all_moments, vs, pressure, table, p):
    summed = jnp.sum(all_moments[...], axis=0)
    mu = [jnp.broadcast_to(jnp.sum(summed[k:k + 1, :], axis=1, keepdims=True), (8, 256)) for k in range(6)]
    coef = [jnp.broadcast_to(c[:1], (64, 256)) for c in coefficients(mu)]

    def combine(r, _):
        p[r] = coef[0] * vs[0, r] + coef[1] * vs[1, r] + coef[2] * vs[2, r]
        return 0
    lax.fori_loop(3, 13, combine, 0)
    for x in range(8):
        here = p[x + 4]
        core = here[:, 0:128]
        pressure[pl.ds(x, 64, stride=8), :] = core
        put_table(table, 0, x, 0.5 * (p[x + 5][:, 0:128] - p[x + 3][:, 0:128]))
        put_table(table, 1, x, 0.5 * (up_y(here) - down_y(here))[:, 0:128])
        put_table(table, 2, x, 0.5 * (up_z(core) - down_z(core)))


def gradients(all_moments, vs):
    return pl.pallas_call(
        gradient_kernel,
        out_shape=(S((512, 128), f32), S((NW, 48, 256), bf16)),
        in_specs=[VSPEC] * 2,
        out_specs=(VSPEC,) * 2,
        scratch_shapes=[pltpu.VMEM((16, 64, 256), f32)],
        compiler_params=VM,
        name="gradients",
    )(all_moments, vs)


PR = 3 * CH


def place_kernel(back_refs, groups, *refs):
    n = back_refs
    backs, (pos_a, pos_b), out = refs[:n], refs[n:n + 2], refs[n + 2]
    stage, found, tiles, zeros, sem_zero, sem_tile = refs[n + 3:]
    hx, hy = lax.axis_index("gx"), lax.axis_index("gy")
    zeros[...] = jnp.zeros_like(zeros)

    def tile_at(t):
        return out.at[:, 0, pl.ds(pl.multiple_of(t * 8, 8), 8), :]

    def far(t):
        return jnp.abs(t - hx) > 2
    for t in range(16):
        @pl.when(far(t))
        def _():
            pltpu.make_async_copy(zeros, tile_at(t), sem_zero.at[t]).start()
    where = {-2: 0, -1: 1, 0: 2, 1: 3, 2: 4}
    for g, runs in enumerate(groups):
        for dx, dy0, first, count in runs:
            for i in range(count):
                src = (dy0 + i + 1) * PR
                stage[(first + i) * PR:(first + i + 1) * PR, :] = backs[where[dx]][src:src + PR, :]
        if g == 1:
            stage[7 * PR:8 * PR, :] = jnp.zeros((PR, 128), f32)
        pos_ref = (pos_a, pos_b)[g]

        def chunk(c, _):
            k = pos_ref[c]
            at, src = k & 127, k >> 7
            acc = [jnp.zeros((8, 128), f32) for _ in range(3)]
            for v in range(CH):
                here = src == v
                for f in range(3):
                    got = jnp.take_along_axis(stage[pl.ds(f * CH + v, 8, stride=PR), :], at, axis=1)
                    acc[f] = jnp.where(here, got, acc[f])
            for f in range(3):
                found[g, f, c] = acc[f]
            return 0
        lax.fori_loop(0, CH, chunk, 0)
    row = lax.broadcasted_iota(i32, (8, 128), 0)
    for dx in (-2, -1, 0, 1, 2):
        pieces = [(g, run) for g, runs in enumerate(groups) for run in runs if run[0] == dx]
        turned = []
        for g, (_, dy0, first, count) in pieces:
            shift = lax.rem(hy + dy0 - first + 16, 8)
            low = hy + dy0
            turned.append((g, shift, (row >= low) & (row < low + count)))
        for f in range(3):
            for c in range(CH):
                got = jnp.zeros((8, 128), f32)
                for g, shift, mask in turned:
                    got = jnp.where(mask, pltpu.roll(found[g, f, c], shift, 0), got)
                tiles[where[dx], f, :, c * 128:(c + 1) * 128] = got

        @pl.when((hx + dx >= 0) & (hx + dx < NGX))
        def _():
            pltpu.make_async_copy(tiles.at[where[dx]], tile_at(hx + dx), sem_tile.at[where[dx]]).start()
    for t in range(16):
        @pl.when(far(t))
        def _():
            pltpu.make_async_copy(zeros, tile_at(t), sem_zero.at[t]).wait()
    for dx in (-2, -1, 0, 1, 2):
        @pl.when((hx + dx >= 0) & (hx + dx < NGX))
        def _():
            pltpu.make_async_copy(tiles.at[where[dx]], tile_at(hx + dx), sem_tile.at[where[dx]]).wait()


def place_forces(backs, pos):
    return pl.pallas_call(
        functools.partial(place_kernel, len(backs), GROUPS),
        out_shape=S((3, 1, 128, 3072), f32),
        in_specs=[VSPEC] * (len(backs) + 2),
        out_specs=pl.BlockSpec(memory_space=pl.ANY),
        scratch_shapes=[
            pltpu.VMEM((8 * PR, 128), f32),
            pltpu.VMEM((2, 3, CH, 8, 128), f32),
            pltpu.VMEM((5, 3, 8, 3072), f32),
            pltpu.VMEM((3, 8, 3072), f32),
            pltpu.SemaphoreType.DMA((16,)),
            pltpu.SemaphoreType.DMA((5,)),
        ],
        compiler_params=VM,
        name="place_forces",
    )(*backs, *pos)


def force_kernel(nref, bases, *refs):
    blocks = [(refs[i], b) for i in range(nref) for b in bases]
    at_pred, at_grad, out = refs[nref:]
    for j, (ref, base) in enumerate(blocks):
        volume = ref[base:base + CH, :]
        coef = ref[base + CH:base + 2 * CH, :]
        for d in range(3):
            vel = ref[base + (2 + d) * CH:base + (3 + d) * CH, :]
            out[j * PR + d * CH:j * PR + (d + 1) * CH, :] = coef * (at_pred[j, d] - vel) - volume * at_grad[j, d]


def block_forces(arrays, bases, at_pred, at_grad):
    nb = len(arrays) * len(bases)
    return pl.pallas_call(
        functools.partial(force_kernel, len(arrays), bases),
        out_shape=S((nb * PR, 128), f32),
        in_specs=[VSPEC] * (len(arrays) + 2),
        out_specs=VSPEC,
        compiler_params=VM,
        name="block_forces",
    )(*arrays, at_pred, at_grad)


def pairs(count, by):
    return [(i, i + by) for i in range(count) if 0 <= i + by < count]


def shift_x(x, by):
    return lax.ppermute(x, "gx", pairs(NGX, by))


def shift_y(x, by):
    return lax.ppermute(x, "gy", pairs(NGY, by))


def per_device(particle_data, particle_cells, slot_counts, fluid_velocity):
    m2, p2, zero_a, pos_a = sort_blocks(GROUPS[0], particle_data, particle_cells, slot_counts)
    m1, p1, zero_b, pos_b = sort_blocks(GROUPS[1], particle_data, particle_cells, slot_counts)
    along = [
        shift_x(m2, -2),
        shift_x(m1, -1),
        jnp.concatenate([zero_a, zero_b], axis=0),
        shift_x(p1, 1),
        shift_x(p2, 2),
    ]
    parts = [jnp.concatenate([a[d * BR:(d + 1) * BR] for a in along], axis=0) for d in range(3)]
    mine = parts[1]
    sides = [shift_y(parts[0], -1), shift_y(parts[2], 1)]
    bases = tuple(range(0, 5 * BR, BR))
    acc = deposit([mine], bases)
    acc = deposit(sides, bases, acc)
    table, low, high = fields(acc, fluid_velocity.reshape(3, 512, 128))
    left, right = shift_x(high, 1), shift_x(low, -1)
    packed = pack_edges(left, low, high, right)
    from_left, from_right = shift_y(packed, 1), shift_y(packed, -1)
    vs, moments = sweeps(left, low, high, right, from_left, from_right)
    everyone = lax.all_to_all(jnp.broadcast_to(moments[None], (NGX * NGY, 8, 128)), ("gx", "gy"), 0, 0)
    blocks = [sides[0], mine, sides[1]]
    at_pred = [interp([b], bases, table) for b in blocks]
    pressure, slopes = gradients(everyone, vs)
    at_grad = [interp([b], bases, slopes) for b in blocks]
    forces = [block_forces([b], bases, p, g) for b, p, g in zip(blocks, at_pred, at_grad)]
    forces = [shift_y(forces[0], 1), forces[1], shift_y(forces[2], -1)]
    backs = []
    for i, dx in enumerate((-2, -1, 0, 1, 2)):
        block = jnp.concatenate([f[i * PR:(i + 1) * PR] for f in forces], axis=0)
        backs.append(block if dx == 0 else shift_x(block, -dx))
    drag = place_forces(backs, [pos_a, pos_b])
    return pressure.reshape(64, 8, 128), drag


def solution(mesh):
    return jax.shard_map(
        per_device,
        mesh=mesh,
        in_specs=(
            P(None, ("gx", "gy"), None, None),
            P(None, ("gx", "gy"), None, None),
            P(("gx", "gy"), None),
            P(None, None, "gx", "gy"),
        ),
        out_specs=(P(None, "gx", "gy"), P(None, ("gx", "gy"), None, None)),
        check_vma=False,
    )
```

time: 1280 us -> 270 us (0.21); the launches traced: 1260 us -> 268 us
  other arithmetic: 383 us -> 0.7 us
  blocking collectives: 328 us -> 0 us
  local copies, waits for them, and re-layouts: 323 us -> 7.76 us
  Pallas kernels: 0 us -> 163 us
  starting transfers between devices: 175 us -> 64.1 us
  waiting for transfers between devices: 44.9 us -> 31.5 us
    psum x5 -> x0, blocking collectives: 328 us -> none  [the longest x3 194 us: global_norm(): return lax.psum(jnp.sum(residual * scaled), ('gx', 'gy'))]
    scatter-add x15 -> x0, other arithmetic: 311 us -> none  [the longest x1 302 us: per_device(): jnp.zeros((5, depth * rows_x * rows_y), jnp.float32).at[:, cell_index]]
    pallas_call x0 -> x18, Pallas kernels: none -> 163 us  [the longest x6 67.8 us: interp(): pl.pallas_call(functools.partial(interp_kernel, len(arrays), bases), out_...]
    gather x1 -> x0, local copies, waits for them, and re-layouts: 163 us -> none  [per_device(): at_particles = cell_table[:, cell_index].reshape(6, blocks_in, capacity)]
    ppermute x50 -> x16, starting transfers between devices: 175 us -> 53.5 us  [the longest x10 37.9 us: shift_x(): return lax.ppermute(x, 'gx', pairs(NGX, by))]
    slice x19 -> x3, local copies, waits for them, and re-layouts: 108 us -> 0.88 us  [per_device(): block = jnp.concatenate([f[i * PR:(i + 1) * PR] for f in forces], axis=0)]
    mul x7 -> x0, other arithmetic: 46.7 us -> none  [the longest x1 41.2 us: per_device(): TIME_STEP * (1.0 + fraction)[None]]
    another operation x4 -> x0, local copies, waits for them, and re-layouts: 27.7 us -> none  [the longest x1 16.8 us: per_device(): jnp.stack([predicted[0], predicted[1], predicted[2], gradient[0], gradien...]
  transfers between devices with their start and end apart: 50 -> 17, of which waited for: 17 -> 10; matrix products, arithmetic and copies ran while one was open for 2% -> 1% of each run, Pallas kernels for 0% -> 29%
where the time goes in v1:
time: 270 us; the launch traced here: 268 us
  Pallas kernels  163 us (60%)
  starting transfers between devices  64.1 us (24%)
  waiting for transfers between devices  31.5 us (12%)
  local copies, waits for them, and re-layouts  7.76 us (3%)
    pallas_call x6, Pallas kernels, interp(): pl.pallas_call(functools.partial(interp_kernel, len(arrays), bases), out_...  67.8 us
    ppermute x10, starting transfers between devices, shift_x(): return lax.ppermute(x, 'gx', pairs(NGX, by))  37.9 us
    pallas_call x2, Pallas kernels, sort_blocks(): pl.pallas_call(functools.partial(sort_kernel, runs, n), out_shape=tuple(s...  32.1 us
    pallas_call x2, Pallas kernels, deposit(): pl.pallas_call(functools.partial(deposit_kernel, len(arrays), bases, prev...  28 us
    ppermute x10, waiting for transfers between devices, shift_x(): return lax.ppermute(x, 'gx', pairs(NGX, by))  26.7 us
    ppermute x6, starting transfers between devices, shift_y(): return lax.ppermute(x, 'gy', pairs(NGY, by))  15.6 us
    pallas_call x1, Pallas kernels, sweeps(): pl.pallas_call(sweeps_kernel, out_shape=(S((3, 16, 64, 256), f32), S((8,...  10.8 us
    all_to_all x1, starting transfers between devices, per_device(): lax.all_to_all(jnp.broadcast_to(moments[None], (NGX * NGY, 8, 128)), ('gx...  10.6 us
  transfers between devices with their start and end apart: 17, of which 10 were waited for; matrix products, arithmetic and copies ran while one was open for 1% of the time, Pallas kernels for 29%

profile of v1, /device:TPU:10, one launch (start us, length us, event | category | flops | bytes accessed | tf_op | source)
XLA Modules:
  0.0 268.3 jit_solution(6000884564421001982)
XLA Ops:
  0.6 16.0 %sort_blocks.2 = (f32[456,128]{1,0:T(8,128)}, f32[456,128]{1,0:T(8,128)}, f32[304,128]{1,0:T(8,128)}, s32[24,8,128]{2,1,0:T(8,128)}) custom-call(f32[5,1,128,3072]{3,2,1,0:T(8,128)} %data_ref.3, s32[2,1,128,3072]{3,2,1,0:T(8,128)} %cells_ref.3, s32[1,128]{1,0:T(1,128)} %counts_ref.3), custom_call_target="tpu_custom_call" | custom-call | tf_op jit(solution)/shard_map/sort_blocks/pallas_call | solution.py:164
  16.7 5.9 %collective-permute-start = (f32[456,128]{1,0:T(8,128)}, f32[456,128]{1,0:T(8,128)S(1)}, u32[]{:S(2)}, u32[]{:S(2)}) collective-permute-start(f32[456,128]{1,0:T(8,128)} %get-tuple-element.17), channel_id=1, source_target_pairs={{16,0},{24,8},{32,16},{40,24},{48,32},{56,40},{64,48},{72,56},{80,... | collective-permute-start | bytes 700424 | tf_op jit(solution)/shard_map/ppermute | solution.py:684
  22.6 16.0 %sort_blocks.3 = (f32[456,128]{1,0:T(8,128)}, f32[456,128]{1,0:T(8,128)}, f32[152,128]{1,0:T(8,128)}, s32[24,8,128]{2,1,0:T(8,128)}) custom-call(f32[5,1,128,3072]{3,2,1,0:T(8,128)} %data_ref.3, s32[2,1,128,3072]{3,2,1,0:T(8,128)} %cells_ref.3, s32[1,128]{1,0:T(1,128)} %counts_ref.3), custom_call_target="tpu_custom_call" | custom-call | tf_op jit(solution)/shard_map/sort_blocks/pallas_call | solution.py:164
  38.6 2.6 collective-permute-start.1
  41.2 3.2 %collective-permute-start.2 = (f32[456,128]{1,0:T(8,128)}, f32[456,128]{1,0:T(8,128)S(1)}, u32[]{:S(2)}, u32[]{:S(2)}) collective-permute-start(f32[456,128]{1,0:T(8,128)} %get-tuple-element.20), channel_id=1, source_target_pairs={{0,8},{8,16},{16,24},{24,32},{32,40},{40,48},{48,56},{56,64},{64,7... | collective-permute-start | bytes 700424 | tf_op jit(solution)/shard_map/ppermute | solution.py:684
  44.5 3.0 %collective-permute-start.3 = (f32[456,128]{1,0:T(8,128)S(1)}, f32[456,128]{1,0:T(8,128)S(1)}, u32[]{:S(2)}, u32[]{:S(2)}) collective-permute-start(f32[456,128]{1,0:T(8,128)S(1)} %copy-done.13), channel_id=1, source_target_pairs={{0,16},{8,24},{16,32},{24,40},{32,48},{40,56},{48,64},{56,72},{64,... | collective-permute-start | bytes 700424 | tf_op jit(solution)/shard_map/ppermute | solution.py:684
  48.8 6.4 %collective-permute-done.2 = f32[456,128]{1,0:T(8,128)S(1)} collective-permute-done((f32[456,128]{1,0:T(8,128)}, f32[456,128]{1,0:T(8,128)S(1)}, u32[]{:S(2)}, u32[]{:S(2)}) %collective-permute-start.2) | collective-permute-done | bytes 233504 | tf_op jit(solution)/shard_map/ppermute | solution.py:684
  59.3 3.8 %collective-permute-start.4 = (f32[760,128]{1,0:T(8,128)S(1)}, f32[760,128]{1,0:T(8,128)S(1)}, u32[]{:S(2)}, u32[]{:S(2)}) collective-permute-start(f32[760,128]{1,0:T(8,128)S(1)} %get-tuple-element.34), channel_id=1, source_target_pairs={{1,0},{2,1},{3,2},{4,3},{5,4},{6,5},{7,6},{9,8},{10,9},{11,10},{12... | collective-permute-start | bytes 1167368 | tf_op jit(solution)/shard_map/ppermute | solution.py:688
  63.1 12.1 %deposit.2.refs_2_ = f32[5,512,128]{2,1,0:T(8,128)} custom-call(f32[760,128]{1,0:T(8,128)} %copy-done), custom_call_target="tpu_custom_call" | custom-call | tf_op jit(solution)/shard_map/deposit/pallas_call | solution.py:272
  76.8 15.8 %deposit.3.acc = f32[5,512,128]{2,1,0:T(8,128)} custom-call(f32[760,128]{1,0:T(8,128)} %copy-done.2, f32[760,128]{1,0:T(8,128)} %copy-done.1, f32[5,512,128]{2,1,0:T(8,128)} %deposit.2.refs_2_), custom_call_target="tpu_custom_call" | custom-call | tf_op jit(solution)/shard_map/deposit/pallas_call | solution.py:272
  92.6 2.9 %fields.1 = (bf16[32,48,256]{2,1,0:T(8,128)(2,1)}, f32[4,4,64,128]{3,2,1,0:T(8,128)}, f32[4,4,64,128]{3,2,1,0:T(8,128)}) custom-call(f32[5,512,128]{2,1,0:T(8,128)} %deposit.3.acc, f32[3,512,128]{2,1,0:T(8,128)} %bitcast.2), custom_call_target="tpu_custom_call" | custom-call | tf_op jit(solution)/shard_map/fields/pallas_call | solution.py:390
  95.5 2.7 %collective-permute-start.6 = (f32[4,4,64,128]{3,2,1,0:T(8,128)}, f32[4,4,64,128]{3,2,1,0:T(8,128)S(1)}, u32[]{:S(2)}, u32[]{:S(2)}) collective-permute-start(f32[4,4,64,128]{3,2,1,0:T(8,128)} %get-tuple-element.23.high), channel_id=1, source_target_pairs={{0,8},{8,16},{16,24},{24,32},{32,40},{40,48},{48,56},{56,64},{64,7... | collective-permute-start | bytes 1572872 | tf_op jit(solution)/shard_map/ppermute | solution.py:684
  98.2 5.2 %collective-permute-start.7 = (f32[4,4,64,128]{3,2,1,0:T(8,128)}, f32[4,4,64,128]{3,2,1,0:T(8,128)S(1)}, u32[]{:S(2)}, u32[]{:S(2)}) collective-permute-start(f32[4,4,64,128]{3,2,1,0:T(8,128)} %get-tuple-element.24.low), channel_id=1, source_target_pairs={{8,0},{16,8},{24,16},{32,24},{40,32},{48,40},{56,48},{64,56},{72,6... | collective-permute-start | bytes 1572872 | tf_op jit(solution)/shard_map/ppermute | solution.py:684
  103.5 10.0 %collective-permute-done.6.left = f32[4,4,64,128]{3,2,1,0:T(8,128)S(1)} collective-permute-done((f32[4,4,64,128]{3,2,1,0:T(8,128)}, f32[4,4,64,128]{3,2,1,0:T(8,128)S(1)}, u32[]{:S(2)}, u32[]{:S(2)}) %collective-permute-start.6) | collective-permute-done | bytes 524320 | tf_op jit(solution)/shard_map/ppermute | solution.py:684
  115.6 2.7 %pack_edges.1 = f32[4,64,128]{2,1,0:T(8,128)} custom-call(f32[4,4,64,128]{3,2,1,0:T(8,128)} %copy-done.4, f32[4,4,64,128]{3,2,1,0:T(8,128)} %get-tuple-element.24.low, f32[4,4,64,128]{3,2,1,0:T(8,128)} %get-tuple-element.23.high, f32[4,4,64,128]{3,2,1,0:T(8,128)} %copy-done.5), custom_call_target="tpu_custom_call" | custom-call | tf_op jit(solution)/shard_map/pack_edges/pallas_call | solution.py:412
  120.2 2.4 collective-permute-start.8
  123.1 3.7 %collective-permute-done.8.from_left = f32[4,64,128]{2,1,0:T(8,128)S(1)} collective-permute-done((f32[4,64,128]{2,1,0:T(8,128)}, f32[4,64,128]{2,1,0:T(8,128)S(1)}, u32[]{:S(2)}, u32[]{:S(2)}) %collective-permute-start.8) | collective-permute-done | bytes 131104 | tf_op jit(solution)/shard_map/ppermute | solution.py:688
  127.4 10.8 %sweeps.1 = (f32[3,16,64,256]{3,2,1,0:T(8,128)}, f32[8,128]{1,0:T(8,128)}) custom-call(f32[4,4,64,128]{3,2,1,0:T(8,128)} %copy-done.4, f32[4,4,64,128]{3,2,1,0:T(8,128)} %get-tuple-element.24.low, f32[4,4,64,128]{3,2,1,0:T(8,128)} %get-tuple-element.23.high, f32[4,4,64,128]{3,2,1,0:T(8,128)} %copy-done.5, f32[4,64,128]{2,1,0:T(8,128)} %copy-done.8, ...), custom_call_target="tpu_custom_call" | custom-call | tf_op jit(solution)/shard_map/sweeps/pallas_call | solution.py:503
  139.7 10.6 %all-to-all-start = ((f32[128,8,128]{2,1,0:T(8,128)}), f32[128,8,128]{2,1,0:T(8,128)S(1)}, u32[]{:S(2)}, u32[]{:S(2)}) async-start(f32[128,8,128]{2,1,0:T(8,128)} %broadcast_in_dim.2), calls=%async_computation | async-start | bytes 1048576 | tf_op jit(solution)/shard_map/all_to_all | solution.py:712
  150.3 11.3 %interp.8.refs_1_ = f32[5,3,24,128]{3,2,1,0:T(8,128)} custom-call(f32[760,128]{1,0:T(8,128)} %copy-done, bf16[32,48,256]{2,1,0:T(8,128)(2,1)} %get-tuple-element.28.refs_1_), custom_call_target="tpu_custom_call" | custom-call | tf_op jit(solution)/shard_map/interp/pallas_call | solution.py:343
  161.6 11.3 %interp.10.refs_1_ = f32[5,3,24,128]{3,2,1,0:T(8,128)} custom-call(f32[760,128]{1,0:T(8,128)} %copy-done.1, bf16[32,48,256]{2,1,0:T(8,128)(2,1)} %get-tuple-element.28.refs_1_), custom_call_target="tpu_custom_call" | custom-call | tf_op jit(solution)/shard_map/interp/pallas_call | solution.py:343
  172.9 11.3 %interp.6.refs_1_ = f32[5,3,24,128]{3,2,1,0:T(8,128)} custom-call(f32[760,128]{1,0:T(8,128)} %copy-done.2, bf16[32,48,256]{2,1,0:T(8,128)(2,1)} %get-tuple-element.28.refs_1_), custom_call_target="tpu_custom_call" | custom-call | tf_op jit(solution)/shard_map/interp/pallas_call | solution.py:343
  185.0 3.8 %gradients.1 = (f32[512,128]{1,0:T(8,128)}, bf16[32,48,256]{2,1,0:T(8,128)(2,1)}) custom-call(f32[128,8,128]{2,1,0:T(8,128)} %copy-done.3, f32[3,16,64,256]{3,2,1,0:T(8,128)} %get-tuple-element.26.vs), custom_call_target="tpu_custom_call" | custom-call | tf_op jit(solution)/shard_map/gradients/pallas_call | solution.py:556
  188.8 11.3 %interp.9.refs_2_ = f32[5,3,24,128]{3,2,1,0:T(8,128)} custom-call(f32[760,128]{1,0:T(8,128)} %copy-done, bf16[32,48,256]{2,1,0:T(8,128)(2,1)} %get-tuple-element.29.refs_1_), custom_call_target="tpu_custom_call" | custom-call | tf_op jit(solution)/shard_map/interp/pallas_call | solution.py:343
  200.0 11.3 %interp.7.refs_2_ = f32[5,3,24,128]{3,2,1,0:T(8,128)} custom-call(f32[760,128]{1,0:T(8,128)} %copy-done.2, bf16[32,48,256]{2,1,0:T(8,128)(2,1)} %get-tuple-element.29.refs_1_), custom_call_target="tpu_custom_call" | custom-call | tf_op jit(solution)/shard_map/interp/pallas_call | solution.py:343
  215.3 11.3 %interp.11.refs_2_ = f32[5,3,24,128]{3,2,1,0:T(8,128)} custom-call(f32[760,128]{1,0:T(8,128)} %copy-done.1, bf16[32,48,256]{2,1,0:T(8,128)(2,1)} %get-tuple-element.29.refs_1_), custom_call_target="tpu_custom_call" | custom-call | tf_op jit(solution)/shard_map/interp/pallas_call | solution.py:343
  228.4 3.5 %collective-permute-start.11 = (f32[360,128]{1,0:T(8,128)}, f32[360,128]{1,0:T(8,128)S(1)}, u32[]{:S(2)}, u32[]{:S(2)}) collective-permute-start(f32[360,128]{1,0:T(8,128)} %block_forces.5), channel_id=1, source_target_pairs={{1,0},{2,1},{3,2},{4,3},{5,4},{6,5},{7,6},{9,8},{10,9},{11,10},{12... | collective-permute-start | bytes 552968 | tf_op jit(solution)/shard_map/ppermute | solution.py:688
  235.3 5.3 %collective-permute-start.12 = (f32[216,128]{1,0:T(8,128)S(1)}, f32[216,128]{1,0:T(8,128)S(1)}, u32[]{:S(2)}, u32[]{:S(2)}) collective-permute-start(f32[216,128]{1,0:T(8,128)S(1)} %pad_maximum_fusion), channel_id=1, source_target_pairs={{0,16},{8,24},{16,32},{24,40},{32,48},{40,56},{48,64},{56,72},{64,... | collective-permute-start | bytes 331784 | tf_op jit(solution)/shard_map/ppermute | solution.py:684
  240.6 2.7 %collective-permute-start.13 = (f32[216,128]{1,0:T(8,128)S(1)}, f32[216,128]{1,0:T(8,128)S(1)}, u32[]{:S(2)}, u32[]{:S(2)}) collective-permute-start(f32[216,128]{1,0:T(8,128)S(1)} %pad_maximum_fusion.1), channel_id=1, source_target_pairs={{0,8},{8,16},{16,24},{24,32},{32,40},{40,48},{48,56},{56,64},{64,7... | collective-permute-start | bytes 331784 | tf_op jit(solution)/shard_map/ppermute | solution.py:684
  243.4 5.2 %collective-permute-start.14 = (f32[216,128]{1,0:T(8,128)S(1)}, f32[216,128]{1,0:T(8,128)S(1)}, u32[]{:S(2)}, u32[]{:S(2)}) collective-permute-start(f32[216,128]{1,0:T(8,128)S(1)} %pad_maximum_fusion.3), channel_id=1, source_target_pairs={{8,0},{16,8},{24,16},{32,24},{40,32},{48,40},{56,48},{64,56},{72,6... | collective-permute-start | bytes 331784 | tf_op jit(solution)/shard_map/ppermute | solution.py:684
  251.9 6.0 %collective-permute-done.15.refs_4_ = f32[216,128]{1,0:T(8,128)S(1)} collective-permute-done((f32[216,128]{1,0:T(8,128)S(1)}, f32[216,128]{1,0:T(8,128)S(1)}, u32[]{:S(2)}, u32[]{:S(2)}) %collective-permute-start.15) | collective-permute-done | bytes 110624 | tf_op jit(solution)/shard_map/ppermute | solution.py:684
  258.5 9.7 %place_forces.1 = f32[3,1,128,3072]{3,2,1,0:T(8,128)} custom-call(f32[216,128]{1,0:T(8,128)} %copy-done.9, f32[216,128]{1,0:T(8,128)} %copy-done.10, f32[216,128]{1,0:T(8,128)} %pad_maximum_fusion.2.refs_2_, f32[216,128]{1,0:T(8,128)} %copy-done.11, f32[216,128]{1,0:T(8,128)} %copy-done.12, s32[24,8,128]{2,1,0:T(8,128)} %get-tuple-element.30.refs_5_, ...), custom_call_target="tpu_custom_call" | custom-call | tf_op jit(solution)/shard_map/place_forces/pallas_call | solution.py:638
  (63 shorter events, 27.2 us)
Async XLA Ops:
  16.7 27.8 %copy-start.13 = (f32[456,128]{1,0:T(8,128)S(1)}, f32[456,128]{1,0:T(8,128)}, u32[]{:S(2)}) copy-start(f32[456,128]{1,0:T(8,128)} %get-tuple-element.21) | copy-start | bytes 700420
  16.7 31.2 %copy-start.6 = (f32[304,128]{1,0:T(8,128)S(1)}, f32[304,128]{1,0:T(8,128)}, u32[]{:S(2)}) copy-start(f32[304,128]{1,0:T(8,128)} %get-tuple-element.19) | copy-start | bytes 466948
  16.7 30.8 %collective-permute-start = (f32[456,128]{1,0:T(8,128)}, f32[456,128]{1,0:T(8,128)S(1)}, u32[]{:S(2)}, u32[]{:S(2)}) collective-permute-start(f32[456,128]{1,0:T(8,128)} %get-tuple-element.17), channel_id=1, source_target_pairs={{16,0},{24,8},{32,16},{40,24},{48,32},{56,40},{64,48},{72,56},{80,... | collective-permute-start | bytes 700424 | tf_op jit(solution)/shard_map/ppermute | solution.py:684
  38.6 9.3 %collective-permute-start.1 = (f32[456,128]{1,0:T(8,128)}, f32[456,128]{1,0:T(8,128)S(1)}, u32[]{:S(2)}, u32[]{:S(2)}) collective-permute-start(f32[456,128]{1,0:T(8,128)} %get-tuple-element.18), channel_id=1, source_target_pairs={{8,0},{16,8},{24,16},{32,24},{40,32},{48,40},{56,48},{64,56},{72,6... | collective-permute-start | bytes 700424 | tf_op jit(solution)/shard_map/ppermute | solution.py:684
  41.2 14.0 %collective-permute-start.2 = (f32[456,128]{1,0:T(8,128)}, f32[456,128]{1,0:T(8,128)S(1)}, u32[]{:S(2)}, u32[]{:S(2)}) collective-permute-start(f32[456,128]{1,0:T(8,128)} %get-tuple-element.20), channel_id=1, source_target_pairs={{0,8},{8,16},{16,24},{24,32},{32,40},{40,48},{48,56},{56,64},{64,7... | collective-permute-start | bytes 700424 | tf_op jit(solution)/shard_map/ppermute | solution.py:684
  44.5 12.8 %collective-permute-start.3 = (f32[456,128]{1,0:T(8,128)S(1)}, f32[456,128]{1,0:T(8,128)S(1)}, u32[]{:S(2)}, u32[]{:S(2)}) collective-permute-start(f32[456,128]{1,0:T(8,128)S(1)} %copy-done.13), channel_id=1, source_target_pairs={{0,16},{8,24},{16,32},{24,40},{32,48},{40,56},{48,64},{56,72},{64,... | collective-permute-start | bytes 700424 | tf_op jit(solution)/shard_map/ppermute | solution.py:684
  57.4 5.8 %copy-start = (f32[760,128]{1,0:T(8,128)}, f32[760,128]{1,0:T(8,128)S(1)}, u32[]{:S(2)}) copy-start(f32[760,128]{1,0:T(8,128)S(1)} %get-tuple-element.32.refs_0_) | copy-start | bytes 1167364
  57.4 17.9 %collective-permute-start.5 = (f32[760,128]{1,0:T(8,128)S(1)}, f32[760,128]{1,0:T(8,128)S(1)}, u32[]{:S(2)}, u32[]{:S(2)}) collective-permute-start(f32[760,128]{1,0:T(8,128)S(1)} %get-tuple-element.33), channel_id=1, source_target_pairs={{0,1},{1,2},{2,3},{3,4},{4,5},{5,6},{6,7},{8,9},{9,10},{10,11},{11... | collective-permute-start | bytes 1167368 | tf_op jit(solution)/shard_map/ppermute | solution.py:688
  59.3 16.0 %collective-permute-start.4 = (f32[760,128]{1,0:T(8,128)S(1)}, f32[760,128]{1,0:T(8,128)S(1)}, u32[]{:S(2)}, u32[]{:S(2)}) collective-permute-start(f32[760,128]{1,0:T(8,128)S(1)} %get-tuple-element.34), channel_id=1, source_target_pairs={{1,0},{2,1},{3,2},{4,3},{5,4},{6,5},{7,6},{9,8},{10,9},{11,10},{12... | collective-permute-start | bytes 1167368 | tf_op jit(solution)/shard_map/ppermute | solution.py:688
  75.3 0.7 copy-start.1
  76.0 0.8 copy-start.2
  95.5 17.9 %collective-permute-start.6 = (f32[4,4,64,128]{3,2,1,0:T(8,128)}, f32[4,4,64,128]{3,2,1,0:T(8,128)S(1)}, u32[]{:S(2)}, u32[]{:S(2)}) collective-permute-start(f32[4,4,64,128]{3,2,1,0:T(8,128)} %get-tuple-element.23.high), channel_id=1, source_target_pairs={{0,8},{8,16},{16,24},{24,32},{32,40},{40,48},{48,56},{56,64},{64,7... | collective-permute-start | bytes 1572872 | tf_op jit(solution)/shard_map/ppermute | solution.py:684
  98.2 16.5 %collective-permute-start.7 = (f32[4,4,64,128]{3,2,1,0:T(8,128)}, f32[4,4,64,128]{3,2,1,0:T(8,128)S(1)}, u32[]{:S(2)}, u32[]{:S(2)}) collective-permute-start(f32[4,4,64,128]{3,2,1,0:T(8,128)} %get-tuple-element.24.low), channel_id=1, source_target_pairs={{8,0},{16,8},{24,16},{32,24},{40,32},{48,40},{56,48},{64,56},{72,6... | collective-permute-start | bytes 1572872 | tf_op jit(solution)/shard_map/ppermute | solution.py:684
  113.5 1.3 copy-start.4
  114.8 0.8 copy-start.5
  118.3 4.7 %collective-permute-start.9 = (f32[4,64,128]{2,1,0:T(8,128)}, f32[4,64,128]{2,1,0:T(8,128)S(1)}, u32[]{:S(2)}, u32[]{:S(2)}) collective-permute-start(f32[4,64,128]{2,1,0:T(8,128)} %pack_edges.1), channel_id=1, source_target_pairs={{1,0},{2,1},{3,2},{4,3},{5,4},{6,5},{7,6},{9,8},{10,9},{11,10},{12... | collective-permute-start | bytes 393224 | tf_op jit(solution)/shard_map/ppermute | solution.py:688
  120.2 6.5 %collective-permute-start.8 = (f32[4,64,128]{2,1,0:T(8,128)}, f32[4,64,128]{2,1,0:T(8,128)S(1)}, u32[]{:S(2)}, u32[]{:S(2)}) collective-permute-start(f32[4,64,128]{2,1,0:T(8,128)} %pack_edges.1), channel_id=1, source_target_pairs={{0,1},{1,2},{2,3},{3,4},{4,5},{5,6},{6,7},{8,9},{9,10},{10,11},{11... | collective-permute-start | bytes 393224 | tf_op jit(solution)/shard_map/ppermute | solution.py:688
  123.1 3.7 %copy-start.7 = (f32[4,64,128]{2,1,0:T(8,128)}, f32[4,64,128]{2,1,0:T(8,128)S(1)}, u32[]{:S(2)}) copy-start(f32[4,64,128]{2,1,0:T(8,128)S(1)} %collective-permute-done.9.from_right) | copy-start | bytes 393220
  126.7 0.7 copy-start.8
  139.7 44.5 %all-to-all-start = ((f32[128,8,128]{2,1,0:T(8,128)}), f32[128,8,128]{2,1,0:T(8,128)S(1)}, u32[]{:S(2)}, u32[]{:S(2)}) async-start(f32[128,8,128]{2,1,0:T(8,128)} %broadcast_in_dim.2), calls=%async_computation | async-start | bytes 1048576 | tf_op jit(solution)/shard_map/all_to_all | solution.py:712
  184.2 0.8 copy-start.3
  213.2 21.4 %collective-permute-start.10 = (f32[360,128]{1,0:T(8,128)}, f32[360,128]{1,0:T(8,128)S(1)}, u32[]{:S(2)}, u32[]{:S(2)}) collective-permute-start(f32[360,128]{1,0:T(8,128)} %block_forces.3), channel_id=1, source_target_pairs={{0,1},{1,2},{2,3},{3,4},{4,5},{5,6},{6,7},{8,9},{9,10},{10,11},{11... | collective-permute-start | bytes 552968 | tf_op jit(solution)/shard_map/ppermute | solution.py:688
  228.4 6.9 %collective-permute-start.11 = (f32[360,128]{1,0:T(8,128)}, f32[360,128]{1,0:T(8,128)S(1)}, u32[]{:S(2)}, u32[]{:S(2)}) collective-permute-start(f32[360,128]{1,0:T(8,128)} %block_forces.5), channel_id=1, source_target_pairs={{1,0},{2,1},{3,2},{4,3},{5,4},{6,5},{7,6},{9,8},{10,9},{11,10},{12... | collective-permute-start | bytes 552968 | tf_op jit(solution)/shard_map/ppermute | solution.py:688
  235.3 16.0 %collective-permute-start.12 = (f32[216,128]{1,0:T(8,128)S(1)}, f32[216,128]{1,0:T(8,128)S(1)}, u32[]{:S(2)}, u32[]{:S(2)}) collective-permute-start(f32[216,128]{1,0:T(8,128)S(1)} %pad_maximum_fusion), channel_id=1, source_target_pairs={{0,16},{8,24},{16,32},{24,40},{32,48},{40,56},{48,64},{56,72},{64,... | collective-permute-start | bytes 331784 | tf_op jit(solution)/shard_map/ppermute | solution.py:684
  240.6 10.6 %collective-permute-start.13 = (f32[216,128]{1,0:T(8,128)S(1)}, f32[216,128]{1,0:T(8,128)S(1)}, u32[]{:S(2)}, u32[]{:S(2)}) collective-permute-start(f32[216,128]{1,0:T(8,128)S(1)} %pad_maximum_fusion.1), channel_id=1, source_target_pairs={{0,8},{8,16},{16,24},{24,32},{32,40},{40,48},{48,56},{56,64},{64,7... | collective-permute-start | bytes 331784 | tf_op jit(solution)/shard_map/ppermute | solution.py:684
  243.4 8.5 %collective-permute-start.14 = (f32[216,128]{1,0:T(8,128)S(1)}, f32[216,128]{1,0:T(8,128)S(1)}, u32[]{:S(2)}, u32[]{:S(2)}) collective-permute-start(f32[216,128]{1,0:T(8,128)S(1)} %pad_maximum_fusion.3), channel_id=1, source_target_pairs={{8,0},{16,8},{24,16},{32,24},{40,32},{48,40},{56,48},{64,56},{72,6... | collective-permute-start | bytes 331784 | tf_op jit(solution)/shard_map/ppermute | solution.py:684
  248.6 9.2 %collective-permute-start.15 = (f32[216,128]{1,0:T(8,128)S(1)}, f32[216,128]{1,0:T(8,128)S(1)}, u32[]{:S(2)}, u32[]{:S(2)}) collective-permute-start(f32[216,128]{1,0:T(8,128)S(1)} %pad_maximum_fusion.4), channel_id=1, source_target_pairs={{16,0},{24,8},{32,16},{40,24},{48,32},{56,40},{64,48},{72,56},{80,... | collective-permute-start | bytes 331784 | tf_op jit(solution)/shard_map/ppermute | solution.py:684
  251.2 6.6 %copy-start.9 = (f32[216,128]{1,0:T(8,128)}, f32[216,128]{1,0:T(8,128)S(1)}, u32[]{:S(2)}) copy-start(f32[216,128]{1,0:T(8,128)S(1)} %collective-permute-done.12.refs_0_) | copy-start | bytes 331780
  251.2 6.6 %copy-start.10 = (f32[216,128]{1,0:T(8,128)}, f32[216,128]{1,0:T(8,128)S(1)}, u32[]{:S(2)}) copy-start(f32[216,128]{1,0:T(8,128)S(1)} %collective-permute-done.13.refs_1_) | copy-start | bytes 331780
  251.9 6.0 %copy-start.11 = (f32[216,128]{1,0:T(8,128)}, f32[216,128]{1,0:T(8,128)S(1)}, u32[]{:S(2)}) copy-start(f32[216,128]{1,0:T(8,128)S(1)} %collective-permute-done.14.refs_3_) | copy-start | bytes 331780
  257.9 0.6 copy-start.12

commit v2 on v1

--- a/solution.py
+++ b/solution.py
@@ -12,7 +12,11 @@
 WL = 16
 NW = 32
 SPAN = WL * 128
+PR = 3 * CH
 VM = pltpu.CompilerParams(vmem_limit_bytes=56 * 1024 * 1024)
+VSPEC = pl.BlockSpec(memory_space=pltpu.VMEM)
+S = jax.ShapeDtypeStruct
+TOKEN = S((8, 128), f32)
 
 
 def sort_network(x):
@@ -38,7 +42,7 @@
             else:
                 step = 1 << (bit - 5)
                 up = (lane & step) != 0
-                other = jnp.where(up, pltpu.roll(x, step, 2), pltpu.roll(x, 128 - step, 2))
+                other = jnp.take_along_axis(x, jnp.broadcast_to(lane ^ step, x.shape), axis=2)
                 x = jnp.where(up, jnp.maximum(x, other), jnp.minimum(x, other))
         if mask is not None:
             x = x ^ mask
@@ -122,11 +126,7 @@
             rows.append((1 << 29) + slot)
     keys = lanes_to_chunks(sort_network(jnp.stack(rows, axis=0)))
     key_s[...] = keys[:CH]
-    place = lax.broadcasted_iota(i32, (32, 8, 128), 0) * 128 + lax.broadcasted_iota(i32, (32, 8, 128), 2)
-    pad = lax.broadcasted_iota(i32, (32, 8, 128), 0) >= CH
-    back = jnp.where(pad, (1 << 29) + place, ((keys & 4095) << 12) + place)
-    back = lanes_to_chunks(sort_network(back))
-    pos_ref[...] = back[:CH] & 4095
+    pos_ref[...] = keys[:CH]
 
     def chunk(c, _):
         k = key_s[c]
@@ -153,8 +153,33 @@
         total = total + jnp.where(jnp.where(low, last, start) < bound, 1, 0)
     for r in range(8):
         out_s[pl.ds(6 * CH + r, 8, stride=BR), :] = total.astype(f32)
-    for out, (_, _, first, count) in zip(outs, runs):
-        out[...] = out_s[first * BR:(first + count) * BR, :]
+    side = lax.rem(hx // abs(runs[0][0]), 2) == 0
+    for out, first in ((outs[0], jnp.where(side, 3 * BR, 0)), (outs[1], jnp.where(side, 0, 3 * BR))):
+        out[...] = out_s[pl.ds(pl.multiple_of(first, 8), 3 * BR), :]
+    _, _, first, count = runs[2]
+    outs[2][...] = out_s[first * BR:(first + count) * BR, :]
+
+
+def inverse_kernel(keys_a, keys_b, after, pos_a, pos_b, token):
+    token[...] = after[...]
+    place = lax.broadcasted_iota(i32, (CH, 8, 128), 0) * 128 + lax.broadcasted_iota(i32, (CH, 8, 128), 2)
+    rest = jnp.full((32 - CH, 8, 128), 1 << 29, i32)
+    for keys, pos in ((keys_a, pos_a), (keys_b, pos_b)):
+        back = jnp.concatenate([((keys[...] & 4095) << 12) + place, rest], axis=0)
+        pos[...] = lanes_to_chunks(sort_network(back))[:CH] & 4095
+
+
+def inverse(keys_a, keys_b, after):
+    shape = jax.ShapeDtypeStruct((CH, 8, 128), i32)
+    return pl.pallas_call(
+        inverse_kernel,
+        out_shape=(shape, shape, TOKEN),
+        in_specs=[VSPEC] * 3,
+        out_specs=(VSPEC,) * 3,
+        compiler_params=VM,
+        cost_estimate=pl.CostEstimate(flops=10**9, bytes_accessed=2 * 10**7, transcendentals=0),
+        name="inverse",
+    )(keys_a, keys_b, after)
 
 
 def sort_blocks(runs, data, cells, counts):
@@ -202,14 +227,14 @@
     return jnp.where(w == iota, jnp.asarray(1.0, bf16), jnp.asarray(0.0, bf16))
 
 
-def deposit_kernel(nref, per, use_acc, *refs):
-    bases = per
+def deposit_kernel(nref, bases, unroll, use_acc, *refs):
     blocks = [(refs[i], b) for i in range(nref) for b in bases]
     nb = len(blocks)
     rest = refs[nref:]
     if use_acc:
-        prev, rest = rest[0], rest[1:]
-    out, pre, off_v, off_s, sem = rest
+        prev, fluid, table, own_0, own_1, token, out, pre, off_v, off_s, sem = rest
+    else:
+        out, pre, off_v, off_s, sem = rest
     load_offsets(blocks, off_v, off_s, sem)
     for j, (ref, base) in enumerate(blocks):
         vol = ref[base:base + CH, :]
@@ -234,133 +259,165 @@
         return a, width_onehot(pre[j, 11, pl.ds(c, 1), :], iota)
 
     def product(a, b):
-        return lax.dot_general(a, b, (((1,), (1,)), ((), ())), preferred_element_type=f32)
-
-    def window(w, _):
-        total = None
-        more = 0
-        for j in range(nb):
-            first = jnp.minimum(off_s[j, w], CH - 2)
-            more = jnp.maximum(more, off_s[j, 64 + w] - first)
-            a0, b0 = operands(j, first, w)
-            a1, b1 = operands(j, first + 1, w)
-            p = product(jnp.concatenate([a0, a1], axis=1), jnp.concatenate([b0, b1], axis=1))
-            total = p if total is None else total + p
-        total = (total[:80] + total[80:]).reshape(5, WL, 128)
-        rows = pl.ds(pl.multiple_of(w * WL, WL), WL)
-        if use_acc:
-            total = total + prev[:, rows, :]
-        out[:, rows, :] = total
-
-        @pl.when(more > 2)
-        def _():
+        p = lax.dot_general(a, b, (((1,), (1,)), ((), ())), preferred_element_type=f32)
+        return p
+
+    def halves(p):
+        return (p[:80] + p[80:]).reshape(5, WL, 128)
+
+    def windows(i, more):
+        for u in range(unroll):
+            w = i * unroll + u
+            total = None
+            for j in range(nb):
+                first = jnp.minimum(off_s[j, w], CH - 2)
+                more = jnp.maximum(more, off_s[j, 64 + w] - first)
+                a0, b0 = operands(j, first, w)
+                a1, b1 = operands(j, first + 1, w)
+                p = product(jnp.concatenate([a0, a1], axis=1), jnp.concatenate([b0, b1], axis=1))
+                total = p if total is None else total + p
+            total = halves(total)
+            rows = pl.ds(pl.multiple_of(w * WL, WL), WL)
+            if use_acc:
+                total = total + prev[:, rows, :]
+            out[:, rows, :] = total
+        return more
+    more = lax.fori_loop(0, NW // unroll, windows, jnp.int32(0))
+
+    @pl.when(more > 2)
+    def _():
+        def window(w, _):
+            rows = pl.ds(pl.multiple_of(w * WL, WL), WL)
+
             def block(j, _):
                 def step(c, _):
                     a, b = operands(j, c, w)
-                    p = product(a, b)
-                    out[:, rows, :] += (p[:80] + p[80:]).reshape(5, WL, 128)
+                    out[:, rows, :] += halves(product(a, b))
                     return 0
                 return lax.fori_loop(jnp.minimum(off_s[j, w], CH - 2) + 2, off_s[j, 64 + w], step, 0)
-            lax.fori_loop(0, nb, block, 0)
-        return 0
-    lax.fori_loop(0, NW, window, 0)
-
-
-def deposit(arrays, bases, prev=None):
+            return lax.fori_loop(0, nb, block, 0)
+        lax.fori_loop(0, NW, window, 0)
+
+
+    if use_acc:
+        fields(out, fluid, table, own_0, own_1)
+        token[...] = jnp.zeros_like(token)
+
+
+def deposit(arrays, bases, unroll, prev=None, fluid=None):
     nb = len(arrays) * len(bases)
-    args = list(arrays) + ([] if prev is None else [prev])
-    return pl.pallas_call(
-        functools.partial(deposit_kernel, len(arrays), bases, prev is not None),
-        out_shape=jax.ShapeDtypeStruct((5, 512, 128), f32),
-        in_specs=[pl.BlockSpec(memory_space=pltpu.VMEM)] * len(args),
-        out_specs=pl.BlockSpec(memory_space=pltpu.VMEM),
-        scratch_shapes=[
-            pltpu.VMEM((nb, 12, CH, 128), f32),
-            pltpu.VMEM((nb, 128), i32),
-            pltpu.SMEM((nb, 128), i32),
-            pltpu.SemaphoreType.DMA,
-        ],
-        compiler_params=VM,
+    args = list(arrays) + ([] if prev is None else [prev, fluid])
+    total = S((5, 512, 128), f32)
+    shapes = (S((NW, 48, 256), bf16), S((4, 4, 64, 128), f32), S((4, 4, 64, 128), f32), TOKEN)
+    scratch = [
+        pltpu.VMEM((nb, 12, CH, 128), f32),
+        pltpu.VMEM((nb, 128), i32),
+        pltpu.SMEM((nb, 128), i32),
+        pltpu.SemaphoreType.DMA,
+    ]
+    if prev is not None:
+        scratch = [pltpu.VMEM((5, 512, 128), f32)] + scratch
+    return pl.pallas_call(
+        functools.partial(deposit_kernel, len(arrays), bases, unroll, prev is not None),
+        out_shape=total if prev is None else shapes,
+        in_specs=[VSPEC] * len(args),
+        out_specs=VSPEC if prev is None else (VSPEC,) * 4,
+        scratch_shapes=scratch,
+        compiler_params=VM,
+        cost_estimate=pl.CostEstimate(flops=10**9 * nb, bytes_accessed=3 * 10**6 * nb, transcendentals=0),
         name="deposit",
     )(*args)
 
 
-def interp_kernel(nref, bases, *refs):
+def interp_kernel(nref, bases, unroll, *refs):
     blocks = [(refs[i], b) for i in range(nref) for b in bases]
     nb = len(blocks)
-    table, out, pre, acc, off_v, off_s, sem = refs[nref:]
+    fast, slope, _ = refs[nref:nref + 3]
+    outs = refs[nref + 3:-6]
+    token, pre, acc, off_v, off_s, sem = refs[-6:]
+    each = nb // len(outs)
+    token[...] = jnp.zeros_like(token)
     load_offsets(blocks, off_v, off_s, sem)
     for j, (ref, base) in enumerate(blocks):
         line, wid = split_cell(ref[base + 5 * CH:base + 6 * CH, :])
         pre[j, 0] = line
         pre[j, 1] = wid
+        pre[j, 2] = ref[base + CH:base + 2 * CH, :]
+        pre[j, 3] = -ref[base:base + CH, :]
     acc[...] = jnp.zeros_like(acc)
     iota = lax.broadcasted_iota(i32, (128, 128), 0).astype(f32).astype(bf16)
     iota16 = lax.broadcasted_iota(i32, (16, 128), 0).astype(f32)
 
     def visit(j, c, w, width, tab):
-        masks, hots = [], []
+        scales, hots = [], []
         for i in range(width):
-            rel = pre[j, 0, pl.ds(c + i, 1), :] - (w * WL).astype(f32)
-            masks.append(wide(rel, 16) == iota16)
-            b = width_onehot(pre[j, 1, pl.ds(c + i, 1), :], iota)
+            at = pl.ds(c + i, 1)
+            mask = wide(pre[j, 0, at, :] - (w * WL).astype(f32), 16) == iota16
+            scales.append([jnp.where(mask, wide(pre[j, 2 + s, at, :], 16), 0.0) for s in range(2)])
+            b = width_onehot(pre[j, 1, at, :], iota)
             hots.append(jnp.concatenate([b, b], axis=0))
         hot = hots[0] if width == 1 else jnp.concatenate(hots, axis=1)
         g = jnp.dot(tab, hot, preferred_element_type=f32)
         for i in range(width):
             for k in range(3):
-                part = jnp.where(masks[i], g[k * 16:k * 16 + 16, i * 128:(i + 1) * 128], 0.0)
+                lanes = slice(i * 128, (i + 1) * 128)
+                part = scales[i][0] * g[k * 16:k * 16 + 16, lanes]
+                part = part + scales[i][1] * g[48 + k * 16:64 + k * 16, lanes]
                 acc[j, c + i, k] += part[:8] + part[8:]
 
-    def window(w, _):
-        tab = table[w]
-        more = 0
-        for j in range(nb):
-            first = jnp.minimum(off_s[j, w], CH - 2)
-            more = jnp.maximum(more, off_s[j, 64 + w] - first)
-            visit(j, first, w, 2, tab)
-
-        @pl.when(more > 2)
-        def _():
+    def windows(i, more):
+        for u in range(unroll):
+            w = i * unroll + u
+            tab = jnp.concatenate([fast[w], slope[w]], axis=0)
+            for j in range(nb):
+                first = jnp.minimum(off_s[j, w], CH - 2)
+                more = jnp.maximum(more, off_s[j, 64 + w] - first)
+                visit(j, first, w, 2, tab)
+        return more
+    more = lax.fori_loop(0, NW // unroll, windows, jnp.int32(0))
+
+    @pl.when(more > 2)
+    def _():
+        def window(w, _):
+            tab = jnp.concatenate([fast[w], slope[w]], axis=0)
+
             def block(j, _):
                 def step(c, _):
                     visit(j, c, w, 1, tab)
                     return 0
                 return lax.fori_loop(jnp.minimum(off_s[j, w], CH - 2) + 2, off_s[j, 64 + w], step, 0)
-            lax.fori_loop(0, nb, block, 0)
-        return 0
-    lax.fori_loop(0, NW, window, 0)
-    def fin(j, _):
+            return lax.fori_loop(0, nb, block, 0)
+        lax.fori_loop(0, NW, window, 0)
+    for j, (ref, base) in enumerate(blocks):
+        coef = ref[base + CH:base + 2 * CH, :]
         for k in range(3):
-            out[j, k] = jnp.sum(acc[j, :, k], axis=1)
-        return 0
-    lax.fori_loop(0, nb, fin, 0)
-
-
-def interp(arrays, bases, table):
+            vel = ref[base + (2 + k) * CH:base + (3 + k) * CH, :]
+            at = (j % each) * PR + k * CH
+            outs[j // each][at:at + CH, :] = jnp.sum(acc[j, :, k], axis=1) - coef * vel
+
+
+def interp(arrays, bases, fast, slope, unroll, after, n_out):
     nb = len(arrays) * len(bases)
-    args = list(arrays) + [table]
-    return pl.pallas_call(
-        functools.partial(interp_kernel, len(arrays), bases),
-        out_shape=jax.ShapeDtypeStruct((nb, 3, CH, 128), f32),
-        in_specs=[pl.BlockSpec(memory_space=pltpu.VMEM)] * len(args),
-        out_specs=pl.BlockSpec(memory_space=pltpu.VMEM),
+    args = list(arrays) + [fast, slope, after]
+    return pl.pallas_call(
+        functools.partial(interp_kernel, len(arrays), bases, unroll),
+        out_shape=(S((nb // n_out * PR, 128), f32),) * n_out + (TOKEN,),
+        in_specs=[VSPEC] * len(args),
+        out_specs=(VSPEC,) * (n_out + 1),
         scratch_shapes=[
-            pltpu.VMEM((nb, 2, CH, 128), f32),
+            pltpu.VMEM((nb, 4, CH, 128), f32),
             pltpu.VMEM((nb, CH, 3, 8, 128), f32),
             pltpu.VMEM((nb, 128), i32),
             pltpu.SMEM((nb, 128), i32),
             pltpu.SemaphoreType.DMA,
         ],
         compiler_params=VM,
+        cost_estimate=pl.CostEstimate(flops=10**9 * nb, bytes_accessed=3 * 10**6 * nb, transcendentals=0),
         name="interp",
     )(*args)
 
-
 TIME_STEP = 0.1
 SHIFT = 0.05
-VSPEC = pl.BlockSpec(memory_space=pltpu.VMEM)
-S = jax.ShapeDtypeStruct
 
 
 def put_table(table, k, x, values):
@@ -371,52 +428,57 @@
         table[4 * x + q, k * 16:k * 16 + 16, 128:256] = lo[16 * q:16 * q + 16]
 
 
-def fields_kernel(acc, fluid, table, low, high):
-    for x in range(8):
-        at = slice(x * 64, x * 64 + 64)
-        fraction = acc[0, at, :]
-        drag = acc[1, at, :]
-        porosity = 1.0 / (1.0 + fraction)
-        out, r = (low, x) if x < 4 else (high, x - 4)
-        out[0, r] = porosity
-        for d in range(3):
-            fluid_d = fluid[d, pl.ds(x, 64, stride=8), :]
-            predicted = fluid_d + TIME_STEP * (1.0 + fraction) * (acc[2 + d, at, :] - drag * fluid_d)
-            put_table(table, d, x, predicted)
-            out[1 + d, r] = porosity * predicted
-
-
-def fields(acc, fluid):
-    return pl.pallas_call(
-        fields_kernel,
-        out_shape=(S((NW, 48, 256), bf16), S((4, 4, 64, 128), f32), S((4, 4, 64, 128), f32)),
-        in_specs=[VSPEC] * 2,
-        out_specs=(VSPEC,) * 3,
-        compiler_params=VM,
-        name="fields",
-    )(acc, fluid)
-
-
-def pack_kernel(left, low, high, right, out):
+def fields(acc, fluid, table, own_0, own_1):
+    even = lax.rem(lax.axis_index("gx"), 2) == 0
+    for r in range(4):
+        made = []
+        for x in (r, r + 4):
+            at = slice(x * 64, x * 64 + 64)
+            fraction = acc[0, at, :]
+            drag = acc[1, at, :]
+            porosity = 1.0 / (1.0 + fraction)
+            values = [porosity]
+            for d in range(3):
+                fluid_d = fluid[d, pl.ds(x, 64, stride=8), :]
+                predicted = fluid_d + TIME_STEP * (1.0 + fraction) * (acc[2 + d, at, :] - drag * fluid_d)
+                put_table(table, d, x, predicted)
+                values.append(porosity * predicted)
+            made.append(values)
+        for f in range(4):
+            low, high = made[0][f], made[1][f]
+            own_0[f, r] = jnp.where(even, high, low)
+            own_1[f, r] = jnp.where(even, low, high)
+
+
+def extended_row(rows, f, r, even):
+    own_0, own_1, got_0, got_1 = rows
+    first, second = ((got_1, got_0), (own_1, own_0), (own_0, own_1), (got_0, got_1))[r // 4]
+    return jnp.where(even, first[f, r % 4], second[f, r % 4])
+
+
+def pack_kernel(own_0, own_1, got_0, got_1, after, out):
+    del after
+    even = lax.rem(lax.axis_index("gx"), 2) == 0
+    rows = (own_0, own_1, got_0, got_1)
     lane = lax.broadcasted_iota(i32, (64, 128), 1)
     for f in range(4):
         got = jnp.zeros((64, 128), f32)
         for r in range(16):
-            src = (left, low, high, right)[r // 4][f, r % 4]
+            src = extended_row(rows, f, r, even)
             place = lax.rem(lane + 132 - 8 * r, 128) < 8
             got = jnp.where(place, src if r == 0 else pltpu.roll(src, 8 * r, 1), got)
         out[f] = got
 
 
-def pack_edges(left, low, high, right):
+def pack_edges(rows, after):
     return pl.pallas_call(
         pack_kernel,
         out_shape=S((4, 64, 128), f32),
-        in_specs=[VSPEC] * 4,
+        in_specs=[VSPEC] * 5,
         out_specs=VSPEC,
         compiler_params=VM,
         name="pack_edges",
-    )(left, low, high, right)
+    )(*rows, after)
 
 
 def up_z(x):
@@ -439,14 +501,17 @@
     return 2.0 * e * n / jnp.maximum(e + n, 1e-30)
 
 
-def sweeps_kernel(left, low, high, right, from_left, from_right, vs, moments, ext, wx, wy, wz, diag, inv, src, more):
+def sweeps_kernel(own_0, own_1, got_0, got_1, edge_0, edge_1, vs, moments, ext, wx, wy, wz, diag, inv, src, more):
     lane = lax.broadcasted_iota(i32, (64, 128), 1)
     even = (lane & 7) < 4
     keep = (lane < 4) | (lane >= 124)
+    even_x = lax.rem(lax.axis_index("gx"), 2) == 0
+    even_y = lax.rem(lax.axis_index("gy"), 2) == 0
+    rows = (own_0, own_1, got_0, got_1)
     for f in range(4):
-        both = jnp.where(even, from_right[f], from_left[f])
+        both = jnp.where(even == even_y, edge_0[f], edge_1[f])
         for r in range(16):
-            ext[f, r, :, 0:128] = (left, low, high, right)[r // 4][f, r % 4]
+            ext[f, r, :, 0:128] = extended_row(rows, f, r, even_x)
             ext[f, r, :, 128:256] = jnp.where(keep, both if r == 0 else pltpu.roll(both, 128 - 8 * r, 1), 0.0)
 
     def faces(r, _):
@@ -493,22 +558,24 @@
         terms = (d0 * v0, d0 * v1, d1 * v1, d1 * v2, d2 * v2, d2 * v3)
         return tuple(t + jnp.sum(x.reshape(8, 8, 128), axis=0) for t, x in zip(total, terms))
     total = lax.fori_loop(4, 12, sums, tuple(jnp.zeros((8, 128), f32) for _ in range(6)))
+    row = jnp.zeros((1, 128), f32)
+    first = lax.broadcasted_iota(i32, (1, 128), 1)
     for k in range(6):
-        moments[k:k + 1, :] = jnp.sum(total[k], axis=0, keepdims=True)
-    moments[6:8, :] = jnp.zeros((2, 128), f32)
-
-
-def sweeps(left, low, high, right, from_left, from_right):
+        row = jnp.where(first == k, jnp.sum(total[k]), row)
+    moments[...] = jnp.broadcast_to(row[:, None, :], moments.shape)
+
+
+def sweeps(rows, edge_0, edge_1):
     big = pltpu.VMEM((16, 64, 256), f32)
     return pl.pallas_call(
         sweeps_kernel,
-        out_shape=(S((3, 16, 64, 256), f32), S((8, 128), f32)),
+        out_shape=(S((3, 16, 64, 256), f32), S((NGX * NGY, 1, 128), f32)),
         in_specs=[VSPEC] * 6,
         out_specs=(VSPEC,) * 2,
         scratch_shapes=[pltpu.VMEM((4, 16, 64, 256), f32)] + [big] * 7,
         compiler_params=VM,
         name="sweeps",
-    )(left, low, high, right, from_left, from_right)
+    )(*rows, edge_0, edge_1)
 
 
 def coefficients(mu):
@@ -536,7 +603,7 @@
 
 def gradient_kernel(all_moments, vs, pressure, table, p):
     summed = jnp.sum(all_moments[...], axis=0)
-    mu = [jnp.broadcast_to(jnp.sum(summed[k:k + 1, :], axis=1, keepdims=True), (8, 256)) for k in range(6)]
+    mu = [jnp.broadcast_to(summed[:, k:k + 1], (8, 256)) for k in range(6)]
     coef = [jnp.broadcast_to(c[:1], (64, 256)) for c in coefficients(mu)]
 
     def combine(r, _):
@@ -564,7 +631,21 @@
     )(all_moments, vs)
 
 
-PR = 3 * CH
+def arrange_kernel(*refs):
+    for i, out in enumerate(refs[3:]):
+        for d in range(3):
+            out[d * PR:(d + 1) * PR, :] = refs[d][i * PR:(i + 1) * PR, :]
+
+
+def arrange(*arrays):
+    return pl.pallas_call(
+        arrange_kernel,
+        out_shape=(S((3 * PR, 128), f32),) * 5,
+        in_specs=[VSPEC] * 3,
+        out_specs=(VSPEC,) * 5,
+        compiler_params=VM,
+        name="arrange",
+    )(*arrays)
 
 
 def place_kernel(back_refs, groups, *refs):
@@ -585,10 +666,18 @@
             pltpu.make_async_copy(zeros, tile_at(t), sem_zero.at[t]).start()
     where = {-2: 0, -1: 1, 0: 2, 1: 3, 2: 4}
     for g, runs in enumerate(groups):
-        for dx, dy0, first, count in runs:
-            for i in range(count):
-                src = (dy0 + i + 1) * PR
-                stage[(first + i) * PR:(first + i + 1) * PR, :] = backs[where[dx]][src:src + PR, :]
+        side = lax.rem(hx // abs(runs[0][0]), 2) == 0
+        pair = (backs[0], backs[1]) if g == 0 else (backs[3], backs[4])
+        up = lax.rem(hy, 2) == 0
+        sources = (jnp.where(up, 2 * PR, 0), PR, jnp.where(up, 0, 2 * PR))
+        for ref, first in zip(pair, (jnp.where(side, 3 * PR, 0), jnp.where(side, 0, 3 * PR))):
+            for d in range(3):
+                to = pl.multiple_of(first + d * PR, 8)
+                stage[pl.ds(to, PR), :] = ref[pl.ds(pl.multiple_of(sources[d], 8), PR), :]
+        _, dy0, first, count = runs[2]
+        for d in range(count):
+            src = pl.multiple_of(sources[dy0 + 1 + d], 8)
+            stage[(first + d) * PR:(first + d + 1) * PR, :] = backs[2][pl.ds(src, PR), :]
         if g == 1:
             stage[7 * PR:8 * PR, :] = jnp.zeros((PR, 128), f32)
         pos_ref = (pos_a, pos_b)[g]
@@ -653,74 +742,40 @@
     )(*backs, *pos)
 
 
-def force_kernel(nref, bases, *refs):
-    blocks = [(refs[i], b) for i in range(nref) for b in bases]
-    at_pred, at_grad, out = refs[nref:]
-    for j, (ref, base) in enumerate(blocks):
-        volume = ref[base:base + CH, :]
-        coef = ref[base + CH:base + 2 * CH, :]
-        for d in range(3):
-            vel = ref[base + (2 + d) * CH:base + (3 + d) * CH, :]
-            out[j * PR + d * CH:j * PR + (d + 1) * CH, :] = coef * (at_pred[j, d] - vel) - volume * at_grad[j, d]
-
-
-def block_forces(arrays, bases, at_pred, at_grad):
-    nb = len(arrays) * len(bases)
-    return pl.pallas_call(
-        functools.partial(force_kernel, len(arrays), bases),
-        out_shape=S((nb * PR, 128), f32),
-        in_specs=[VSPEC] * (len(arrays) + 2),
-        out_specs=VSPEC,
-        compiler_params=VM,
-        name="block_forces",
-    )(*arrays, at_pred, at_grad)
-
-
-def pairs(count, by):
-    return [(i, i + by) for i in range(count) if 0 <= i + by < count]
-
-
-def shift_x(x, by):
-    return lax.ppermute(x, "gx", pairs(NGX, by))
-
-
-def shift_y(x, by):
-    return lax.ppermute(x, "gy", pairs(NGY, by))
+def exchange(x, axis, by, which):
+    count = {"gx": NGX, "gy": NGY}[axis]
+    pairs = [(i, i + by) for i in range(count - by) if (i // by) % 2 == which]
+    return lax.ppermute(x, axis, pairs + [(j, i) for i, j in pairs])
 
 
 def per_device(particle_data, particle_cells, slot_counts, fluid_velocity):
-    m2, p2, zero_a, pos_a = sort_blocks(GROUPS[0], particle_data, particle_cells, slot_counts)
-    m1, p1, zero_b, pos_b = sort_blocks(GROUPS[1], particle_data, particle_cells, slot_counts)
-    along = [
-        shift_x(m2, -2),
-        shift_x(m1, -1),
-        jnp.concatenate([zero_a, zero_b], axis=0),
-        shift_x(p1, 1),
-        shift_x(p2, 2),
+    two_0, two_1, zero_a, keys_a = sort_blocks(GROUPS[0], particle_data, particle_cells, slot_counts)
+    two_0, two_1 = exchange(two_0, "gx", 2, 0), exchange(two_1, "gx", 2, 1)
+    one_0, one_1, zero_b, keys_b = sort_blocks(GROUPS[1], particle_data, particle_cells, slot_counts)
+    one_0, one_1 = exchange(one_0, "gx", 1, 0), exchange(one_1, "gx", 1, 1)
+    along = [two_0, two_1, jnp.concatenate([zero_a, zero_b], axis=0), one_0, one_1]
+    below, mine, above = [jnp.concatenate([a[d * BR:(d + 1) * BR] for a in along], axis=0) for d in range(3)]
+    up = lax.rem(lax.axis_index("gy"), 2) == 0
+    sides = [
+        exchange(jnp.where(up, above, below), "gy", 1, 0),
+        exchange(jnp.where(up, below, above), "gy", 1, 1),
     ]
-    parts = [jnp.concatenate([a[d * BR:(d + 1) * BR] for a in along], axis=0) for d in range(3)]
-    mine = parts[1]
-    sides = [shift_y(parts[0], -1), shift_y(parts[2], 1)]
     bases = tuple(range(0, 5 * BR, BR))
-    acc = deposit([mine], bases)
-    acc = deposit(sides, bases, acc)
-    table, low, high = fields(acc, fluid_velocity.reshape(3, 512, 128))
-    left, right = shift_x(high, 1), shift_x(low, -1)
-    packed = pack_edges(left, low, high, right)
-    from_left, from_right = shift_y(packed, 1), shift_y(packed, -1)
-    vs, moments = sweeps(left, low, high, right, from_left, from_right)
-    everyone = lax.all_to_all(jnp.broadcast_to(moments[None], (NGX * NGY, 8, 128)), ("gx", "gy"), 0, 0)
-    blocks = [sides[0], mine, sides[1]]
-    at_pred = [interp([b], bases, table) for b in blocks]
+    acc = deposit([mine], bases, 8)
+    table, own_0, own_1, token = deposit(sides, bases, 4, acc, fluid_velocity.reshape(3, 512, 128))
+    rows = (own_0, own_1, exchange(own_0, "gx", 1, 0), exchange(own_1, "gx", 1, 1))
+    *pos, token = inverse(keys_a, keys_b, token)
+    packed = pack_edges(rows, token)
+    vs, moments = sweeps(rows, exchange(packed, "gy", 1, 0), exchange(packed, "gy", 1, 1))
+    everyone = lax.all_to_all(moments, ("gx", "gy"), 0, 0)
     pressure, slopes = gradients(everyone, vs)
-    at_grad = [interp([b], bases, slopes) for b in blocks]
-    forces = [block_forces([b], bases, p, g) for b, p, g in zip(blocks, at_pred, at_grad)]
-    forces = [shift_y(forces[0], 1), forces[1], shift_y(forces[2], -1)]
-    backs = []
-    for i, dx in enumerate((-2, -1, 0, 1, 2)):
-        block = jnp.concatenate([f[i * PR:(i + 1) * PR] for f in forces], axis=0)
-        backs.append(block if dx == 0 else shift_x(block, -dx))
-    drag = place_forces(backs, [pos_a, pos_b])
+    far_0, far_1, token = interp(sides, bases, table, slopes, 4, token, 2)
+    back = [exchange(far_0, "gy", 1, 0), exchange(far_1, "gy", 1, 1)]
+    near, _ = interp([mine], bases, table, slopes, 8, token, 1)
+    blocks = list(arrange(back[0], near, back[1]))
+    for i, (by, which) in ((0, (2, 0)), (1, (2, 1)), (3, (1, 0)), (4, (1, 1))):
+        blocks[i] = exchange(blocks[i], "gx", by, which)
+    drag = place_forces(blocks, pos)
     return pressure.reshape(64, 8, 128), drag
 
 

time: 270 us -> 179 us (0.66)
  Pallas kernels: 163 us -> 94.3 us
  starting transfers between devices: 64.1 us -> 40 us
  blocking collectives: 0 us -> 16.9 us
  waiting for transfers between devices: 31.5 us -> 21.1 us
    pallas_call x13 -> x7, Pallas kernels: 115 us -> 55.8 us  [the longest x2 19.1 us: deposit(): pl.pallas_call(functools.partial(deposit_kernel, len(arrays), bases, unro...]
    all_to_all x0 -> x1, blocking collectives: none -> 16.9 us  [per_device(): everyone = lax.all_to_all(moments, ('gx', 'gy'), 0, 0)]
    ppermute x16, starting transfers between devices: 53.5 us -> 40 us  [exchange(): return lax.ppermute(x, axis, pairs + [(j, i) for i, j in pairs])]
    all_to_all x1 -> x0, starting transfers between devices: 10.6 us -> none  [per_device(): lax.all_to_all(jnp.broadcast_to(moments[None], (NGX * NGY, 8, 128)), ('gx...]
    ppermute x16, waiting for transfers between devices: 31.5 us -> 21.1 us  [exchange(): return lax.ppermute(x, axis, pairs + [(j, i) for i, j in pairs])]
    pallas_call x2, Pallas kernels: 32.1 us -> 22.4 us  [sort_blocks(): pl.pallas_call(functools.partial(sort_kernel, runs, n), out_shape=tuple(s...]
  transfers between devices with their start and end apart: 17 -> 16, of which waited for: 10 -> 7; matrix products, arithmetic and copies ran while one was open for 1% -> 1% of each run, Pallas kernels for 29% -> 17%
where the time goes in v2:
time: 179 us
  Pallas kernels  94.3 us (53%)
  starting transfers between devices  40 us (22%)
  waiting for transfers between devices  21.1 us (12%)
  blocking collectives  16.9 us (9%)
  local copies, waits for them, and re-layouts  5.31 us (3%)
    ppermute x16, starting transfers between devices, exchange(): return lax.ppermute(x, axis, pairs + [(j, i) for i, j in pairs])  40 us
    pallas_call x2, Pallas kernels, sort_blocks(): pl.pallas_call(functools.partial(sort_kernel, runs, n), out_shape=tuple(s...  22.4 us
    ppermute x16, waiting for transfers between devices, exchange(): return lax.ppermute(x, axis, pairs + [(j, i) for i, j in pairs])  21.1 us
    pallas_call x2, Pallas kernels, deposit(): pl.pallas_call(functools.partial(deposit_kernel, len(arrays), bases, unro...  19.1 us
    pallas_call x2, Pallas kernels, interp(): pl.pallas_call(functools.partial(interp_kernel, len(arrays), bases, unrol...  18.9 us
    all_to_all x1, blocking collectives, per_device(): everyone = lax.all_to_all(moments, ('gx', 'gy'), 0, 0)  16.9 us
    pallas_call x1, Pallas kernels, sweeps(): pl.pallas_call(sweeps_kernel, out_shape=(S((3, 16, 64, 256), f32), S((NGX...  10.8 us
    pallas_call x1, Pallas kernels, place_forces(): pl.pallas_call(functools.partial(place_kernel, len(backs), GROUPS), out_s...  9.69 us
  transfers between devices with their start and end apart: 16, of which 7 were waited for; matrix products, arithmetic and copies ran while one was open for 1% of the time, Pallas kernels for 17%

profile of v2, /device:TPU:10, one launch (start us, length us, event | category | flops | bytes accessed | tf_op | source)
XLA Modules:
  0.0 178.7 jit_solution(3238999945304143213)
XLA Ops:
  0.6 11.2 %sort_blocks.2 = (f32[456,128]{1,0:T(8,128)}, f32[456,128]{1,0:T(8,128)}, f32[304,128]{1,0:T(8,128)}, s32[24,8,128]{2,1,0:T(8,128)}) custom-call(f32[5,1,128,3072]{3,2,1,0:T(8,128)} %data_ref.3, s32[2,1,128,3072]{3,2,1,0:T(8,128)} %cells_ref.3, s32[1,128]{1,0:T(1,128)} %counts_ref.3), custom_call_target="tpu_custom_call" | custom-call | tf_op jit(solution)/shard_map/sort_blocks/pallas_call | solution.py:189
  11.8 4.0 %collective-permute-start = (f32[456,128]{1,0:T(8,128)}, f32[456,128]{1,0:T(8,128)S(1)}, u32[]{:S(2)}, u32[]{:S(2)}) collective-permute-start(f32[456,128]{1,0:T(8,128)} %get-tuple-element.30), channel_id=1, source_target_pairs={{0,16},{8,24},{32,48},{40,56},{64,80},{72,88},{96,112},{104,120},{... | collective-permute-start | bytes 700424 | tf_op jit(solution)/shard_map/ppermute | solution.py:748
  15.8 2.0 %collective-permute-start.1 = (f32[456,128]{1,0:T(8,128)}, f32[456,128]{1,0:T(8,128)S(1)}, u32[]{:S(2)}, u32[]{:S(2)}) collective-permute-start(f32[456,128]{1,0:T(8,128)} %get-tuple-element.31), channel_id=1, source_target_pairs={{16,32},{24,40},{48,64},{56,72},{80,96},{88,104},{32,16},{40,24},{... | collective-permute-start | bytes 700424 | tf_op jit(solution)/shard_map/ppermute | solution.py:748
  17.8 11.2 %sort_blocks.3 = (f32[456,128]{1,0:T(8,128)}, f32[456,128]{1,0:T(8,128)}, f32[152,128]{1,0:T(8,128)}, s32[24,8,128]{2,1,0:T(8,128)}) custom-call(f32[5,1,128,3072]{3,2,1,0:T(8,128)} %data_ref.3, s32[2,1,128,3072]{3,2,1,0:T(8,128)} %cells_ref.3, s32[1,128]{1,0:T(1,128)} %counts_ref.3), custom_call_target="tpu_custom_call" | custom-call | tf_op jit(solution)/shard_map/sort_blocks/pallas_call | solution.py:189
  29.0 1.6 collective-permute-start.2
  30.7 5.3 %collective-permute-start.3 = (f32[456,128]{1,0:T(8,128)}, f32[456,128]{1,0:T(8,128)S(1)}, u32[]{:S(2)}, u32[]{:S(2)}) collective-permute-start(f32[456,128]{1,0:T(8,128)} %get-tuple-element.34), channel_id=1, source_target_pairs={{8,16},{24,32},{40,48},{56,64},{72,80},{88,96},{104,112},{16,8},{3... | collective-permute-start | bytes 700424 | tf_op jit(solution)/shard_map/ppermute | solution.py:748
  36.1 0.9 constant_dynamic-update-slice_fusion
  37.1 4.4 %collective-permute-done.3 = f32[456,128]{1,0:T(8,128)S(1)} collective-permute-done((f32[456,128]{1,0:T(8,128)}, f32[456,128]{1,0:T(8,128)S(1)}, u32[]{:S(2)}, u32[]{:S(2)}) %collective-permute-start.3) | collective-permute-done | bytes 233504 | tf_op jit(solution)/shard_map/ppermute | solution.py:748
  41.5 1.9 %collective-permute-start.5 = (f32[760,128]{1,0:T(8,128)S(1)}, f32[760,128]{1,0:T(8,128)S(1)}, u32[]{:S(2)}, u32[]{:S(2)}) collective-permute-start(f32[760,128]{1,0:T(8,128)S(1)} %get-tuple-element.58), channel_id=1, source_target_pairs={{1,2},{3,4},{5,6},{2,1},{4,3},{6,5},{9,10},{11,12},{13,14},{10,9},... | collective-permute-start | bytes 1167368 | tf_op jit(solution)/shard_map/ppermute | solution.py:748
  43.5 1.8 collective-permute-start.4
  45.2 6.8 %deposit.2.refs_2_ = f32[5,512,128]{2,1,0:T(8,128)} custom-call(f32[760,128]{1,0:T(8,128)} %copy-done.11), custom_call_target="tpu_custom_call" | custom-call | flops 5000000000 | bytes 15000000 | tf_op jit(solution)/shard_map/deposit/pallas_call | solution.py:320
  52.9 12.3 %deposit.3 = (bf16[32,48,256]{2,1,0:T(8,128)(2,1)}, f32[4,4,64,128]{3,2,1,0:T(8,128)}, f32[4,4,64,128]{3,2,1,0:T(8,128)}, f32[8,128]{1,0:T(8,128)}) custom-call(f32[760,128]{1,0:T(8,128)} %copy-done.13, f32[760,128]{1,0:T(8,128)} %copy-done.12, f32[5,512,128]{2,1,0:T(8,128)} %deposit.2.refs_2_, f32[3,512,128]{2,1,0:T(8,128)} %bitcast.2), custom_call_target="tpu_custom_call" | custom-call | flops 10000000000 | bytes 30000000 | tf_op jit(solution)/shard_map/deposit/pallas_call | solution.py:320
  66.0 4.9 %collective-permute-start.7 = (f32[4,4,64,128]{3,2,1,0:T(8,128)}, f32[4,4,64,128]{3,2,1,0:T(8,128)S(1)}, u32[]{:S(2)}, u32[]{:S(2)}) collective-permute-start(f32[4,4,64,128]{3,2,1,0:T(8,128)} %get-tuple-element.37.own_1), channel_id=1, source_target_pairs={{8,16},{24,32},{40,48},{56,64},{72,80},{88,96},{104,112},{16,8},{3... | collective-permute-start | bytes 1572872 | tf_op jit(solution)/shard_map/ppermute | solution.py:748
  70.9 5.1 %inverse.1 = (s32[24,8,128]{2,1,0:T(8,128)}, s32[24,8,128]{2,1,0:T(8,128)}, f32[8,128]{1,0:T(8,128)}) custom-call(s32[24,8,128]{2,1,0:T(8,128)} %get-tuple-element.38.keys_a, s32[24,8,128]{2,1,0:T(8,128)} %get-tuple-element.39.keys_b, f32[8,128]{1,0:T(8,128)} %get-tuple-element.40.after), custom_call_target="tpu_custom_call" | custom-call | flops 1000000000 | bytes 20000000 | tf_op jit(solution)/shard_map/inverse/pallas_call | solution.py:174
  76.0 3.4 %collective-permute-done.6.got_0 = f32[4,4,64,128]{3,2,1,0:T(8,128)S(1)} collective-permute-done((f32[4,4,64,128]{3,2,1,0:T(8,128)}, f32[4,4,64,128]{3,2,1,0:T(8,128)S(1)}, u32[]{:S(2)}, u32[]{:S(2)}) %collective-permute-start.6) | collective-permute-done | bytes 524320 | tf_op jit(solution)/shard_map/ppermute | solution.py:748
  79.4 4.4 %collective-permute-done.7.got_1 = f32[4,4,64,128]{3,2,1,0:T(8,128)S(1)} collective-permute-done((f32[4,4,64,128]{3,2,1,0:T(8,128)}, f32[4,4,64,128]{3,2,1,0:T(8,128)S(1)}, u32[]{:S(2)}, u32[]{:S(2)}) %collective-permute-start.7) | collective-permute-done | bytes 524320 | tf_op jit(solution)/shard_map/ppermute | solution.py:748
  84.6 2.8 %pack_edges.1 = f32[4,64,128]{2,1,0:T(8,128)} custom-call(f32[4,4,64,128]{3,2,1,0:T(8,128)} %get-tuple-element.36.own_0, f32[4,4,64,128]{3,2,1,0:T(8,128)} %get-tuple-element.37.own_1, f32[4,4,64,128]{3,2,1,0:T(8,128)} %copy-done, f32[4,4,64,128]{3,2,1,0:T(8,128)} %copy-done.1, f32[8,128]{1,0:T(8,128)} %get-tuple-element.41.after.refs_4_), custom_call_target="tpu_custom_call" | custom-call | tf_op jit(solution)/shard_map/pack_edges/pallas_call | solution.py:474
  87.3 1.9 %collective-permute-start.9 = (f32[4,64,128]{2,1,0:T(8,128)}, f32[4,64,128]{2,1,0:T(8,128)S(1)}, u32[]{:S(2)}, u32[]{:S(2)}) collective-permute-start(f32[4,64,128]{2,1,0:T(8,128)} %pack_edges.1), channel_id=1, source_target_pairs={{1,2},{3,4},{5,6},{2,1},{4,3},{6,5},{9,10},{11,12},{13,14},{10,9},... | collective-permute-start | bytes 393224 | tf_op jit(solution)/shard_map/ppermute | solution.py:748
  89.2 1.5 collective-permute-start.8
  90.7 3.1 %collective-permute-done.9.edge_1 = f32[4,64,128]{2,1,0:T(8,128)S(1)} collective-permute-done((f32[4,64,128]{2,1,0:T(8,128)}, f32[4,64,128]{2,1,0:T(8,128)S(1)}, u32[]{:S(2)}, u32[]{:S(2)}) %collective-permute-start.9) | collective-permute-done | bytes 131104 | tf_op jit(solution)/shard_map/ppermute | solution.py:748
  95.1 10.8 %sweeps.1 = (f32[3,16,64,256]{3,2,1,0:T(8,128)}, f32[128,1,128]{2,1,0:T(1,128)}) custom-call(f32[4,4,64,128]{3,2,1,0:T(8,128)} %get-tuple-element.36.own_0, f32[4,4,64,128]{3,2,1,0:T(8,128)} %get-tuple-element.37.own_1, f32[4,4,64,128]{3,2,1,0:T(8,128)} %copy-done, f32[4,4,64,128]{3,2,1,0:T(8,128)} %copy-done.1, f32[4,64,128]{2,1,0:T(8,128)} %copy-done.6, ...), custom_call_target="tpu_custom_call" | custom-call | tf_op jit(solution)/shard_map/sweeps/pallas_call | solution.py:570
  105.9 16.9 %all_to_all.5.all_moments = f32[128,1,128]{2,1,0:T(1,128)} all-to-all(f32[128,1,128]{2,1,0:T(1,128)} %get-tuple-element.42), channel_id=1, replica_groups=mesh['gx'=16,'gy'=8] {'gx','gy'}, dimensions={0} | all-to-all | bytes 131072 | tf_op jit(solution)/shard_map/all_to_all | solution.py:770
  122.8 3.6 %gradients.1 = (f32[512,128]{1,0:T(8,128)}, bf16[32,48,256]{2,1,0:T(8,128)(2,1)}) custom-call(f32[128,1,128]{2,1,0:T(1,128)} %all_to_all.5.all_moments, f32[3,16,64,256]{3,2,1,0:T(8,128)} %get-tuple-element.43.vs), custom_call_target="tpu_custom_call" | custom-call | tf_op jit(solution)/shard_map/gradients/pallas_call | solution.py:623
  126.4 11.7 %interp.2 = (f32[360,128]{1,0:T(8,128)}, f32[360,128]{1,0:T(8,128)}, f32[8,128]{1,0:T(8,128)}) custom-call(f32[760,128]{1,0:T(8,128)} %copy-done.13, f32[760,128]{1,0:T(8,128)} %copy-done.12, bf16[32,48,256]{2,1,0:T(8,128)(2,1)} %get-tuple-element.45.refs_2_.refs_1_, bf16[32,48,256]{2,1,0:T(8,128)(2,1)} %get-tuple-element.46.refs_3_.refs_2_, ...), custom_call_target="tpu_custom_call" | custom-call | flops 10000000000 | bytes 30000000 | tf_op jit(solution)/shard_map/interp/pallas_call | solution.py:402
  138.3 4.0 %collective-permute-start.11 = (f32[360,128]{1,0:T(8,128)}, f32[360,128]{1,0:T(8,128)S(1)}, u32[]{:S(2)}, u32[]{:S(2)}) collective-permute-start(f32[360,128]{1,0:T(8,128)} %get-tuple-element.50), channel_id=1, source_target_pairs={{1,2},{3,4},{5,6},{2,1},{4,3},{6,5},{9,10},{11,12},{13,14},{10,9},... | collective-permute-start | bytes 552968 | tf_op jit(solution)/shard_map/ppermute | solution.py:748
  142.3 7.2 %interp.3 = (f32[360,128]{1,0:T(8,128)}, f32[8,128]{1,0:T(8,128)}) custom-call(f32[760,128]{1,0:T(8,128)} %copy-done.11, bf16[32,48,256]{2,1,0:T(8,128)(2,1)} %get-tuple-element.45.refs_2_.refs_1_, bf16[32,48,256]{2,1,0:T(8,128)(2,1)} %get-tuple-element.46.refs_3_.refs_2_, f32[8,128]{1,0:T(8,128)} %get-tuple-element.48.refs_3_), custom_call_target="tpu_custom_call" | custom-call | flops 5000000000 | bytes 15000000 | tf_op jit(solution)/shard_map/interp/pallas_call | solution.py:402
  150.2 1.9 %arrange.1 = (f32[216,128]{1,0:T(8,128)}, f32[216,128]{1,0:T(8,128)}, f32[216,128]{1,0:T(8,128)}, f32[216,128]{1,0:T(8,128)}, f32[216,128]{1,0:T(8,128)}) custom-call(f32[360,128]{1,0:T(8,128)} %copy-done.2, f32[360,128]{1,0:T(8,128)} %get-tuple-element.49.refs_1_, f32[360,128]{1,0:T(8,128)} %copy-done.3), custom_call_target="tpu_custom_call" | custom-call | tf_op jit(solution)/shard_map/arrange/pallas_call | solution.py:641
  152.2 1.3 collective-permute-start.12
  153.5 4.9 %collective-permute-start.13 = (f32[216,128]{1,0:T(8,128)}, f32[216,128]{1,0:T(8,128)S(1)}, u32[]{:S(2)}, u32[]{:S(2)}) collective-permute-start(f32[216,128]{1,0:T(8,128)} %get-tuple-element.52), channel_id=1, source_target_pairs={{16,32},{24,40},{48,64},{56,72},{80,96},{88,104},{32,16},{40,24},{... | collective-permute-start | bytes 331784 | tf_op jit(solution)/shard_map/ppermute | solution.py:748
  159.2 3.1 %collective-permute-start.15 = (f32[216,128]{1,0:T(8,128)}, f32[216,128]{1,0:T(8,128)S(1)}, u32[]{:S(2)}, u32[]{:S(2)}) collective-permute-start(f32[216,128]{1,0:T(8,128)} %get-tuple-element.55), channel_id=1, source_target_pairs={{8,16},{24,32},{40,48},{56,64},{72,80},{88,96},{104,112},{16,8},{3... | collective-permute-start | bytes 331784 | tf_op jit(solution)/shard_map/ppermute | solution.py:748
  163.4 4.7 %collective-permute-done.15.refs_4_ = f32[216,128]{1,0:T(8,128)S(1)} collective-permute-done((f32[216,128]{1,0:T(8,128)}, f32[216,128]{1,0:T(8,128)S(1)}, u32[]{:S(2)}, u32[]{:S(2)}) %collective-permute-start.15) | collective-permute-done | bytes 110624 | tf_op jit(solution)/shard_map/ppermute | solution.py:748
  168.8 9.7 %place_forces.1 = f32[3,1,128,3072]{3,2,1,0:T(8,128)} custom-call(f32[216,128]{1,0:T(8,128)} %copy-done.7, f32[216,128]{1,0:T(8,128)} %copy-done.8, f32[216,128]{1,0:T(8,128)} %get-tuple-element.53.refs_2_, f32[216,128]{1,0:T(8,128)} %copy-done.9, f32[216,128]{1,0:T(8,128)} %copy-done.10, s32[24,8,128]{2,1,0:T(8,128)} %get-tuple-element.56.refs_5_, ...), custom_call_target="tpu_custom_call" | custom-call | tf_op jit(solution)/shard_map/place_forces/pallas_call | solution.py:727
  (48 shorter events, 7.3 us)
Async XLA Ops:
  11.8 24.2 %collective-permute-start = (f32[456,128]{1,0:T(8,128)}, f32[456,128]{1,0:T(8,128)S(1)}, u32[]{:S(2)}, u32[]{:S(2)}) collective-permute-start(f32[456,128]{1,0:T(8,128)} %get-tuple-element.30), channel_id=1, source_target_pairs={{0,16},{8,24},{32,48},{40,56},{64,80},{72,88},{96,112},{104,120},{... | collective-permute-start | bytes 700424 | tf_op jit(solution)/shard_map/ppermute | solution.py:748
  15.8 20.3 %copy-start.4 = (f32[304,128]{1,0:T(8,128)S(1)}, f32[304,128]{1,0:T(8,128)}, u32[]{:S(2)}) copy-start(f32[304,128]{1,0:T(8,128)} %get-tuple-element.35) | copy-start | bytes 466948
  15.8 20.3 %collective-permute-start.1 = (f32[456,128]{1,0:T(8,128)}, f32[456,128]{1,0:T(8,128)S(1)}, u32[]{:S(2)}, u32[]{:S(2)}) collective-permute-start(f32[456,128]{1,0:T(8,128)} %get-tuple-element.31), channel_id=1, source_target_pairs={{16,32},{24,40},{48,64},{56,72},{80,96},{88,104},{32,16},{40,24},{... | collective-permute-start | bytes 700424 | tf_op jit(solution)/shard_map/ppermute | solution.py:748
  29.0 8.0 %collective-permute-start.2 = (f32[456,128]{1,0:T(8,128)}, f32[456,128]{1,0:T(8,128)S(1)}, u32[]{:S(2)}, u32[]{:S(2)}) collective-permute-start(f32[456,128]{1,0:T(8,128)} %get-tuple-element.33), channel_id=1, source_target_pairs={{0,8},{16,24},{32,40},{48,56},{64,72},{80,88},{96,104},{112,120},{... | collective-permute-start | bytes 700424 | tf_op jit(solution)/shard_map/ppermute | solution.py:748
  30.7 10.8 %collective-permute-start.3 = (f32[456,128]{1,0:T(8,128)}, f32[456,128]{1,0:T(8,128)S(1)}, u32[]{:S(2)}, u32[]{:S(2)}) collective-permute-start(f32[456,128]{1,0:T(8,128)} %get-tuple-element.34), channel_id=1, source_target_pairs={{8,16},{24,32},{40,48},{56,64},{72,80},{88,96},{104,112},{16,8},{3... | collective-permute-start | bytes 700424 | tf_op jit(solution)/shard_map/ppermute | solution.py:748
  41.5 3.8 %copy-start.11 = (f32[760,128]{1,0:T(8,128)}, f32[760,128]{1,0:T(8,128)S(1)}, u32[]{:S(2)}) copy-start(f32[760,128]{1,0:T(8,128)S(1)} %get-tuple-element.60.refs_0_) | copy-start | bytes 1167364
  41.5 10.5 %collective-permute-start.5 = (f32[760,128]{1,0:T(8,128)S(1)}, f32[760,128]{1,0:T(8,128)S(1)}, u32[]{:S(2)}, u32[]{:S(2)}) collective-permute-start(f32[760,128]{1,0:T(8,128)S(1)} %get-tuple-element.58), channel_id=1, source_target_pairs={{1,2},{3,4},{5,6},{2,1},{4,3},{6,5},{9,10},{11,12},{13,14},{10,9},... | collective-permute-start | bytes 1167368 | tf_op jit(solution)/shard_map/ppermute | solution.py:748
  43.5 8.6 %collective-permute-start.4 = (f32[760,128]{1,0:T(8,128)S(1)}, f32[760,128]{1,0:T(8,128)S(1)}, u32[]{:S(2)}, u32[]{:S(2)}) collective-permute-start(f32[760,128]{1,0:T(8,128)S(1)} %get-tuple-element.59), channel_id=1, source_target_pairs={{0,1},{2,3},{4,5},{6,7},{1,0},{3,2},{5,4},{7,6},{8,9},{10,11},{12,... | collective-permute-start | bytes 1167368 | tf_op jit(solution)/shard_map/ppermute | solution.py:748
  52.0 0.8 copy-start.12
  52.1 0.9 copy-start.13
  65.2 14.1 %collective-permute-start.6 = (f32[4,4,64,128]{3,2,1,0:T(8,128)}, f32[4,4,64,128]{3,2,1,0:T(8,128)S(1)}, u32[]{:S(2)}, u32[]{:S(2)}) collective-permute-start(f32[4,4,64,128]{3,2,1,0:T(8,128)} %get-tuple-element.36.own_0), channel_id=1, source_target_pairs={{0,8},{16,24},{32,40},{48,56},{64,72},{80,88},{96,104},{112,120},{... | collective-permute-start | bytes 1572872 | tf_op jit(solution)/shard_map/ppermute | solution.py:748
  66.0 17.8 %collective-permute-start.7 = (f32[4,4,64,128]{3,2,1,0:T(8,128)}, f32[4,4,64,128]{3,2,1,0:T(8,128)S(1)}, u32[]{:S(2)}, u32[]{:S(2)}) collective-permute-start(f32[4,4,64,128]{3,2,1,0:T(8,128)} %get-tuple-element.37.own_1), channel_id=1, source_target_pairs={{8,16},{24,32},{40,48},{56,64},{72,80},{88,96},{104,112},{16,8},{3... | collective-permute-start | bytes 1572872 | tf_op jit(solution)/shard_map/ppermute | solution.py:748
  79.4 4.4 %copy-start = (f32[4,4,64,128]{3,2,1,0:T(8,128)}, f32[4,4,64,128]{3,2,1,0:T(8,128)S(1)}, u32[]{:S(2)}) copy-start(f32[4,4,64,128]{3,2,1,0:T(8,128)S(1)} %collective-permute-done.6.got_0) | copy-start | bytes 1572868
  83.7 0.8 copy-start.1
  87.3 6.5 %collective-permute-start.9 = (f32[4,64,128]{2,1,0:T(8,128)}, f32[4,64,128]{2,1,0:T(8,128)S(1)}, u32[]{:S(2)}, u32[]{:S(2)}) collective-permute-start(f32[4,64,128]{2,1,0:T(8,128)} %pack_edges.1), channel_id=1, source_target_pairs={{1,2},{3,4},{5,6},{2,1},{4,3},{6,5},{9,10},{11,12},{13,14},{10,9},... | collective-permute-start | bytes 393224 | tf_op jit(solution)/shard_map/ppermute | solution.py:748
  89.2 4.6 %collective-permute-start.8 = (f32[4,64,128]{2,1,0:T(8,128)}, f32[4,64,128]{2,1,0:T(8,128)S(1)}, u32[]{:S(2)}, u32[]{:S(2)}) collective-permute-start(f32[4,64,128]{2,1,0:T(8,128)} %pack_edges.1), channel_id=1, source_target_pairs={{0,1},{2,3},{4,5},{6,7},{1,0},{3,2},{5,4},{7,6},{8,9},{10,11},{12,... | collective-permute-start | bytes 393224 | tf_op jit(solution)/shard_map/ppermute | solution.py:748
  93.8 0.6 copy-start.5
  94.4 0.7 copy-start.6
  138.2 11.3 %collective-permute-start.10 = (f32[360,128]{1,0:T(8,128)}, f32[360,128]{1,0:T(8,128)S(1)}, u32[]{:S(2)}, u32[]{:S(2)}) collective-permute-start(f32[360,128]{1,0:T(8,128)} %get-tuple-element.47), channel_id=1, source_target_pairs={{0,1},{2,3},{4,5},{6,7},{1,0},{3,2},{5,4},{7,6},{8,9},{10,11},{12,... | collective-permute-start | bytes 552968 | tf_op jit(solution)/shard_map/ppermute | solution.py:748
  138.3 11.2 %collective-permute-start.11 = (f32[360,128]{1,0:T(8,128)}, f32[360,128]{1,0:T(8,128)S(1)}, u32[]{:S(2)}, u32[]{:S(2)}) collective-permute-start(f32[360,128]{1,0:T(8,128)} %get-tuple-element.50), channel_id=1, source_target_pairs={{1,2},{3,4},{5,6},{2,1},{4,3},{6,5},{9,10},{11,12},{13,14},{10,9},... | collective-permute-start | bytes 552968 | tf_op jit(solution)/shard_map/ppermute | solution.py:748
  149.5 0.7 copy-start.2
  149.5 0.7 copy-start.3
  152.2 10.2 %collective-permute-start.12 = (f32[216,128]{1,0:T(8,128)}, f32[216,128]{1,0:T(8,128)S(1)}, u32[]{:S(2)}, u32[]{:S(2)}) collective-permute-start(f32[216,128]{1,0:T(8,128)} %get-tuple-element.51), channel_id=1, source_target_pairs={{0,16},{8,24},{32,48},{40,56},{64,80},{72,88},{96,112},{104,120},{... | collective-permute-start | bytes 331784 | tf_op jit(solution)/shard_map/ppermute | solution.py:748
  153.5 9.3 %collective-permute-start.13 = (f32[216,128]{1,0:T(8,128)}, f32[216,128]{1,0:T(8,128)S(1)}, u32[]{:S(2)}, u32[]{:S(2)}) collective-permute-start(f32[216,128]{1,0:T(8,128)} %get-tuple-element.52), channel_id=1, source_target_pairs={{16,32},{24,40},{48,64},{56,72},{80,96},{88,104},{32,16},{40,24},{... | collective-permute-start | bytes 331784 | tf_op jit(solution)/shard_map/ppermute | solution.py:748
  158.4 5.0 %collective-permute-start.14 = (f32[216,128]{1,0:T(8,128)}, f32[216,128]{1,0:T(8,128)S(1)}, u32[]{:S(2)}, u32[]{:S(2)}) collective-permute-start(f32[216,128]{1,0:T(8,128)} %get-tuple-element.54), channel_id=1, source_target_pairs={{0,8},{16,24},{32,40},{48,56},{64,72},{80,88},{96,104},{112,120},{... | collective-permute-start | bytes 331784 | tf_op jit(solution)/shard_map/ppermute | solution.py:748
  159.2 8.9 %collective-permute-start.15 = (f32[216,128]{1,0:T(8,128)}, f32[216,128]{1,0:T(8,128)S(1)}, u32[]{:S(2)}, u32[]{:S(2)}) collective-permute-start(f32[216,128]{1,0:T(8,128)} %get-tuple-element.55), channel_id=1, source_target_pairs={{8,16},{24,32},{40,48},{56,64},{72,80},{88,96},{104,112},{16,8},{3... | collective-permute-start | bytes 331784 | tf_op jit(solution)/shard_map/ppermute | solution.py:748
  162.4 5.8 %copy-start.7 = (f32[216,128]{1,0:T(8,128)}, f32[216,128]{1,0:T(8,128)S(1)}, u32[]{:S(2)}) copy-start(f32[216,128]{1,0:T(8,128)S(1)} %collective-permute-done.12.refs_0_) | copy-start | bytes 331780
  162.8 5.3 %copy-start.8 = (f32[216,128]{1,0:T(8,128)}, f32[216,128]{1,0:T(8,128)S(1)}, u32[]{:S(2)}) copy-start(f32[216,128]{1,0:T(8,128)S(1)} %collective-permute-done.13.refs_1_) | copy-start | bytes 331780
  163.4 4.8 %copy-start.9 = (f32[216,128]{1,0:T(8,128)}, f32[216,128]{1,0:T(8,128)S(1)}, u32[]{:S(2)}) copy-start(f32[216,128]{1,0:T(8,128)S(1)} %collective-permute-done.14.refs_3_) | copy-start | bytes 331780
  168.2 0.6 copy-start.10

commit v3 on v2

--- a/solution.py
+++ b/solution.py
@@ -74,6 +74,14 @@
 NGX, NGY = 16, 8
 
 
+def unrolled(count, by, body):
+    def several(i, _):
+        for j in range(by):
+            body(i * by + j)
+        return 0
+    lax.fori_loop(0, count // by, several, 0)
+
+
 def row_mask(first, count):
     row = lax.broadcasted_iota(i32, (8, 128), 0)
     return (row >= first) & (row < first + count)
@@ -86,8 +94,10 @@
     copies = []
     for t, (dx, _, _, _) in enumerate(runs):
         tile = pl.ds(pl.multiple_of(jnp.clip(hx + dx, 0, NGX - 1) * 8, 8), 8)
-        copies.append(pltpu.make_async_copy(data_ref.at[:, 0, tile, :], data_v.at[t], sems.at[2 * t]))
-        copies.append(pltpu.make_async_copy(cells_ref.at[:, 0, tile, :], cells_v.at[t], sems.at[2 * t + 1]))
+        copies.append(pltpu.make_async_copy(cells_ref.at[:, 0, tile, :], cells_v.at[t], sems.at[2 * t]))
+    for t, (dx, _, _, _) in enumerate(runs):
+        tile = pl.ds(pl.multiple_of(jnp.clip(hx + dx, 0, NGX - 1) * 8, 8), 8)
+        copies.append(pltpu.make_async_copy(data_ref.at[:, 0, tile, :], data_v.at[t], sems.at[2 * t + 1]))
     for copy in copies:
         copy.start()
     lane = lax.broadcasted_iota(i32, (8, 128), 1)
@@ -101,7 +111,7 @@
             counts = jnp.where(row == first + i, jnp.where(valid, n, 0), counts)
     shifts = [lax.rem(first - (hy + dy0) + 16, 8) for _, dy0, first, _ in runs]
     masks = [row_mask(first, count) for _, _, first, count in runs]
-    for copy in copies:
+    for copy in copies[:len(runs)]:
         copy.wait()
 
     def gathered(ref, f, c):
@@ -119,16 +129,19 @@
             live = slot < counts
             cell = (((col >> 7) * 64 + h) << 7) + (col & 127)
             cell = jnp.where(live, cell, 65536)
-            for f in range(5):
-                pay_s[f, c] = jnp.where(live, gathered(data_v, f, c), 0.0)
             rows.append((cell << 12) + slot)
         else:
             rows.append((1 << 29) + slot)
     keys = lanes_to_chunks(sort_network(jnp.stack(rows, axis=0)))
     key_s[...] = keys[:CH]
     pos_ref[...] = keys[:CH]
-
-    def chunk(c, _):
+    for copy in copies[len(runs):]:
+        copy.wait()
+    for c in range(CH):
+        for f in range(5):
+            pay_s[f, c] = jnp.where(lane + c * 128 < counts, gathered(data_v, f, c), 0.0)
+
+    def chunk(c):
         k = key_s[c]
         slot = k & 4095
         at, src = slot & 127, slot >> 7
@@ -141,8 +154,7 @@
         for f in range(5):
             out_s[pl.ds(f * CH + c, 8, stride=BR), :] = acc[f]
         out_s[pl.ds(5 * CH + c, 8, stride=BR), :] = (k >> 12).astype(f32)
-        return 0
-    lax.fori_loop(0, CH, chunk, 0)
+    unrolled(CH, 4, chunk)
     low = lane < 64
     bound = jnp.where(low, lane, lane - 63) * SPAN
     total = jnp.zeros((8, 128), i32)
@@ -232,7 +244,7 @@
     nb = len(blocks)
     rest = refs[nref:]
     if use_acc:
-        prev, fluid, table, own_0, own_1, token, out, pre, off_v, off_s, sem = rest
+        prev, fluid, table, own, send_0, send_1, token, out, flux, pre, off_v, off_s, sem = rest
     else:
         out, pre, off_v, off_s, sem = rest
     load_offsets(blocks, off_v, off_s, sem)
@@ -300,7 +312,7 @@
 
 
     if use_acc:
-        fields(out, fluid, table, own_0, own_1)
+        fields(out, fluid, table, own, send_0, send_1, flux)
         token[...] = jnp.zeros_like(token)
 
 
@@ -308,7 +320,8 @@
     nb = len(arrays) * len(bases)
     args = list(arrays) + ([] if prev is None else [prev, fluid])
     total = S((5, 512, 128), f32)
-    shapes = (S((NW, 48, 256), bf16), S((4, 4, 64, 128), f32), S((4, 4, 64, 128), f32), TOKEN)
+    sent = S((SENT, 64, 128), f32)
+    shapes = (S((NW, 48, 256), bf16), S((2, 8, 64, 128), f32), sent, sent, TOKEN)
     scratch = [
         pltpu.VMEM((nb, 12, CH, 128), f32),
         pltpu.VMEM((nb, 128), i32),
@@ -316,12 +329,12 @@
         pltpu.SemaphoreType.DMA,
     ]
     if prev is not None:
-        scratch = [pltpu.VMEM((5, 512, 128), f32)] + scratch
+        scratch = [pltpu.VMEM((5, 512, 128), f32), pltpu.VMEM((8, 64, 128), f32)] + scratch
     return pl.pallas_call(
         functools.partial(deposit_kernel, len(arrays), bases, unroll, prev is not None),
         out_shape=total if prev is None else shapes,
         in_specs=[VSPEC] * len(args),
-        out_specs=VSPEC if prev is None else (VSPEC,) * 4,
+        out_specs=VSPEC if prev is None else (VSPEC,) * 5,
         scratch_shapes=scratch,
         compiler_params=VM,
         cost_estimate=pl.CostEstimate(flops=10**9 * nb, bytes_accessed=3 * 10**6 * nb, transcendentals=0),
@@ -428,154 +441,247 @@
         table[4 * x + q, k * 16:k * 16 + 16, 128:256] = lo[16 * q:16 * q + 16]
 
 
-def fields(acc, fluid, table, own_0, own_1):
-    even = lax.rem(lax.axis_index("gx"), 2) == 0
-    for r in range(4):
-        made = []
-        for x in (r, r + 4):
-            at = slice(x * 64, x * 64 + 64)
-            fraction = acc[0, at, :]
-            drag = acc[1, at, :]
-            porosity = 1.0 / (1.0 + fraction)
-            values = [porosity]
-            for d in range(3):
-                fluid_d = fluid[d, pl.ds(x, 64, stride=8), :]
-                predicted = fluid_d + TIME_STEP * (1.0 + fraction) * (acc[2 + d, at, :] - drag * fluid_d)
-                put_table(table, d, x, predicted)
-                values.append(porosity * predicted)
-            made.append(values)
-        for f in range(4):
-            low, high = made[0][f], made[1][f]
-            own_0[f, r] = jnp.where(even, high, low)
-            own_1[f, r] = jnp.where(even, low, high)
-
-
-def extended_row(rows, f, r, even):
-    own_0, own_1, got_0, got_1 = rows
-    first, second = ((got_1, got_0), (own_1, own_0), (own_0, own_1), (got_0, got_1))[r // 4]
-    return jnp.where(even, first[f, r % 4], second[f, r % 4])
-
-
-def pack_kernel(own_0, own_1, got_0, got_1, after, out):
+def up_z(x):
+    return jnp.concatenate([x[1:], jnp.zeros_like(x[:1])], axis=0)
+
+
+def down_z(x):
+    return jnp.concatenate([jnp.zeros_like(x[:1]), x[:-1]], axis=0)
+
+
+def plane_lanes():
+    return lax.broadcasted_iota(i32, (64, 128), 1)
+
+
+def is_even(axis):
+    return lax.rem(lax.axis_index(axis), 2) == 0
+
+
+def turn(x, by):
+    return x if by % 128 == 0 else pltpu.roll(x, by % 128, 1)
+
+
+SENT = 9
+
+
+def fields(acc, fluid, table, own, send_0, send_1, flux):
+    even = is_even("gx")
+    lane = plane_lanes()
+    ends = jnp.zeros((64, 128), f32)
+    for x in range(8):
+        at = slice(x * 64, x * 64 + 64)
+        fraction = acc[0, at, :]
+        drag = acc[1, at, :]
+        porosity = 1.0 / (1.0 + fraction)
+        fluxes = []
+        for d in range(3):
+            fluid_d = fluid[d, pl.ds(x, 64, stride=8), :]
+            predicted = fluid_d + TIME_STEP * (1.0 + fraction) * (acc[2 + d, at, :] - drag * fluid_d)
+            put_table(table, d, x, predicted)
+            fluxes.append(porosity * predicted)
+        flux[x] = fluxes[0]
+        fy, fz = fluxes[1:]
+        along_y = jnp.where(lane < 127, turn(fy, -1), 0.0) - jnp.where(lane > 0, turn(fy, 1), 0.0)
+        own[0, x] = porosity
+        own[1, x] = -0.5 * (along_y + (up_z(fz) - down_z(fz)))
+        mid = 8 * (x + 4)
+        ends = jnp.where((lane == mid) | (lane == mid - 1), turn(fy, mid), ends)
+    for x in range(8):
+        along_x = (flux[x + 1] if x < 7 else 0.0) - (flux[x - 1] if x > 0 else 0.0)
+        own[1, x] = own[1, x] - 0.5 * along_x
+    low = [own[0, x] for x in range(4)] + [own[1, x] for x in range(3)] + [flux[0], ends]
+    high = [own[0, x] for x in range(4, 8)] + [own[1, x] for x in range(5, 8)] + [flux[7], ends]
+    for i in range(SENT):
+        send_0[i] = jnp.where(even, high[i], low[i])
+        send_1[i] = jnp.where(even, low[i], high[i])
+
+
+def extended(refs):
+    own, sent_0, sent_1, got_0, got_1 = refs
+    even = is_even("gx")
+
+    def below(i):
+        return jnp.where(even, got_1[i], got_0[i])
+
+    def above(i):
+        return jnp.where(even, got_0[i], got_1[i])
+
+    def porosity(r):
+        return below(r) if r < 4 else own[0, r - 4] if r < 12 else above(r - 12)
+
+    def source(r):
+        if r == 3:
+            return below(6) - 0.5 * jnp.where(even, sent_1[7], sent_0[7])
+        if r == 4:
+            return own[1, 0] + 0.5 * below(7)
+        if r == 11:
+            return own[1, 7] - 0.5 * above(7)
+        if r == 12:
+            return above(4) + 0.5 * jnp.where(even, sent_0[7], sent_1[7])
+        return below(3 + r) if r < 4 else own[1, r - 4] if r < 12 else above(r - 8)
+
+    def ends():
+        lane = plane_lanes()
+        beside = jnp.where((lane >= 92) & (lane < 124), turn(above(8), 64), turn(below(8), 64))
+        return jnp.where((lane >= 28) & (lane < 92), sent_0[8], beside)
+    return porosity, source, ends
+
+
+def pack_kernel(own, sent_0, sent_1, got_0, got_1, after, out):
     del after
-    even = lax.rem(lax.axis_index("gx"), 2) == 0
-    rows = (own_0, own_1, got_0, got_1)
-    lane = lax.broadcasted_iota(i32, (64, 128), 1)
-    for f in range(4):
+    porosity, source, ends = extended((own, sent_0, sent_1, got_0, got_1))
+    lane = plane_lanes()
+    for f, (rows, get) in enumerate(((range(16), porosity), (range(1, 15), source))):
         got = jnp.zeros((64, 128), f32)
-        for r in range(16):
-            src = extended_row(rows, f, r, even)
-            place = lax.rem(lane + 132 - 8 * r, 128) < 8
-            got = jnp.where(place, src if r == 0 else pltpu.roll(src, 8 * r, 1), got)
+        for r in rows:
+            place = (lax.rem(lane + 132 - 8 * r, 128)) < 8
+            got = jnp.where(place, turn(get(r), 8 * r), got)
         out[f] = got
-
-
-def pack_edges(rows, after):
+    out[2] = ends()
+
+
+def pack_edges(refs, after):
     return pl.pallas_call(
         pack_kernel,
-        out_shape=S((4, 64, 128), f32),
-        in_specs=[VSPEC] * 5,
+        out_shape=S((3, 64, 128), f32),
+        in_specs=[VSPEC] * 6,
         out_specs=VSPEC,
         compiler_params=VM,
         name="pack_edges",
-    )(*rows, after)
-
-
-def up_z(x):
-    return jnp.concatenate([x[1:], jnp.zeros_like(x[:1])], axis=0)
-
-
-def down_z(x):
-    return jnp.concatenate([jnp.zeros_like(x[:1]), x[:-1]], axis=0)
-
-
-def up_y(x):
-    return pltpu.roll(x, x.shape[1] - 1, 1)
-
-
-def down_y(x):
-    return pltpu.roll(x, 1, 1)
+    )(*refs, after)
 
 
 def face(e, n):
     return 2.0 * e * n / jnp.maximum(e + n, 1e-30)
 
 
-def sweeps_kernel(own_0, own_1, got_0, got_1, edge_0, edge_1, vs, moments, ext, wx, wy, wz, diag, inv, src, more):
-    lane = lax.broadcasted_iota(i32, (64, 128), 1)
-    even = (lane & 7) < 4
+def up_pair(pair, last):
+    a, b = (pltpu.roll(x, 127, 1) for x in pair)
+    return jnp.where(last, b, a), jnp.where(last, a, b)
+
+
+def down_pair(pair, first):
+    a, b = (pltpu.roll(x, 1, 1) for x in pair)
+    return jnp.where(first, b, a), jnp.where(first, a, b)
+
+
+MID, UP, DOWN = pl.ds(8, 64), pl.ds(9, 64), pl.ds(7, 64)
+
+
+def sweeps_kernel(own, sent_0, sent_1, got_0, got_1, packed, edge_0, edge_1, core, beside, moments, vs, por, src, wx, wy, wz,
+                  diag, inv):
+    porosity, source, _ = extended((own, sent_0, sent_1, got_0, got_1))
+    lane = plane_lanes()
+    first, last = lane == 0, lane == 127
     keep = (lane < 4) | (lane >= 124)
-    even_x = lax.rem(lax.axis_index("gx"), 2) == 0
-    even_y = lax.rem(lax.axis_index("gy"), 2) == 0
-    rows = (own_0, own_1, got_0, got_1)
-    for f in range(4):
-        both = jnp.where(even == even_y, edge_0[f], edge_1[f])
-        for r in range(16):
-            ext[f, r, :, 0:128] = extended_row(rows, f, r, even_x)
-            ext[f, r, :, 128:256] = jnp.where(keep, both if r == 0 else pltpu.roll(both, 128 - 8 * r, 1), 0.0)
-
-    def faces(r, _):
-        e = ext[0, r]
-        wx[r] = face(e, ext[0, jnp.minimum(r + 1, 15)])
-        wy[r] = face(e, up_y(e))
-        wz[r] = face(e, up_z(e))
-        return 0
-    lax.fori_loop(0, 16, faces, 0)
-
-    def sources(r, _):
-        e = ext[0, r]
-        y, z = wy[r], wz[r]
-        d = SHIFT * e + wz[r] + down_z(z) + wx[r] + wx[r - 1] + y + down_y(y)
-        outside = e == 0.0
-        i = jnp.where(outside, 0.0, 1.0 / jnp.where(outside, 1.0, d))
-        fy, fz = ext[2, r], ext[3, r]
-        b = -0.5 * ((ext[1, r + 1] - ext[1, r - 1]) + (up_y(fy) - down_y(fy)) + (up_z(fz) - down_z(fz)))
-        diag[r] = d
-        inv[r] = i
-        vs[0, r] = b * i
-        return 0
-    lax.fori_loop(1, 15, sources, 0)
-
-    def spread(k, r):
-        v = vs[k, r]
-        y, z = wy[r], wz[r]
-        total = wx[r] * vs[k, r + 1] + wx[r - 1] * vs[k, r - 1]
-        total = total + y * up_y(v) + down_y(y * v)
-        total = total + z * up_z(v) + down_z(z * v)
-        return (diag[r] * v - total) * inv[r]
+    even_y = is_even("gy")
+
+    def above(f):
+        return jnp.where(even_y, edge_0[f], edge_1[f])
+
+    def below(f):
+        return jnp.where(even_y, edge_1[f], edge_0[f])
+    part = lane & 7
+
+    def crossed(from_below, from_above):
+        return jnp.where(part == 0, 0.5 * turn(from_below, 1), jnp.where(part == 7, -0.5 * turn(from_above, -1), 0.0))
+    side_e = jnp.where(part < 4, above(0), below(0))
+    side_b = jnp.where(part < 4, above(1), below(1)) + crossed(packed[2], packed[2])
+    core_b = crossed(below(2), above(2))
+    for ref in (por, wz):
+        for h in range(2):
+            for r in range(16):
+                ref[h, r, 0:8] = jnp.zeros((8, 128), f32)
+                ref[h, r, 72:80] = jnp.zeros((8, 128), f32)
+    for k in range(3):
+        for r in range(1, 15):
+            for h in range(2):
+                vs[k, h, r, 0:8] = jnp.zeros((8, 128), f32)
+                vs[k, h, r, 72:80] = jnp.zeros((8, 128), f32)
+    for r in range(16):
+        por[0, r, MID] = porosity(r)
+        por[1, r, MID] = jnp.where(keep, turn(side_e, -8 * r), 0.0)
+        if 0 < r < 15:
+            src[0, r] = source(r) + jnp.where(first | last, turn(core_b, -8 * r), 0.0)
+            src[1, r] = jnp.where(keep, turn(side_b, -8 * r), 0.0)
+
+    def faces(r):
+        pair = [por[h, r, MID] for h in range(2)]
+        up = up_pair(pair, last)
+        for h in range(2):
+            wx[h, r] = face(pair[h], por[h, r + 1, MID])
+            wy[h, r] = face(pair[h], up[h])
+            wz[h, r, MID] = face(pair[h], por[h, r, UP])
+    for r in range(15):
+        faces(r)
+
+    def keep_plane(k, h, r, v):
+        vs[k, h, r, MID] = v
+        if h == 0 and 3 <= r < 13:
+            core[k, r - 3] = v
+        if h == 1 and 4 <= r < 12:
+            beside[k, r - 4] = v
+
+    def sources(r):
+        y = [wy[h, r] for h in range(2)]
+        y_down = down_pair(y, first)
+        for h in range(2):
+            e = por[h, r, MID]
+            d = SHIFT * e + wx[h, r] + wx[h, r - 1] + y[h] + y_down[h] + wz[h, r, MID] + wz[h, r, DOWN]
+            outside = e == 0.0
+            i = jnp.where(outside, 0.0, 1.0 / jnp.where(outside, 1.0, d))
+            diag[h, r] = d
+            inv[h, r] = i
+            keep_plane(0, h, r, src[h, r] * i)
+    for r in range(1, 15):
+        sources(r)
+
+    def spread(k, r, halves):
+        pair = [vs[k, h, r, MID] for h in range(2)]
+        y = [wy[h, r] for h in range(2)]
+        up = up_pair(pair, last)
+        down = down_pair([a * b for a, b in zip(y, pair)], first)
+        made = []
+        for h in range(halves):
+            total = wx[h, r] * vs[k, h, r + 1, MID] + wx[h, r - 1] * vs[k, h, r - 1, MID]
+            total = total + y[h] * up[h] + down[h]
+            total = total + wz[h, r, MID] * vs[k, h, r, UP] + wz[h, r, DOWN] * vs[k, h, r, DOWN]
+            made.append((diag[h, r] * pair[h] - total) * inv[h, r])
+        return made
 
     for k, (lo, hi) in ((0, (2, 14)), (1, (3, 13))):
-        def image(r, _, k=k):
-            vs[k + 1, r] = spread(k, r)
-            return 0
-        lax.fori_loop(lo, hi, image, 0)
+        for r in range(lo, hi):
+            for h, v in enumerate(spread(k, r, 2)):
+                keep_plane(k + 1, h, r, v)
 
     def sums(r, total):
-        d = diag[r][:, 0:128]
-        v0, v1, v2 = (vs[k, r][:, 0:128] for k in range(3))
-        v3 = spread(2, r)[:, 0:128]
+        d = diag[0, r]
+        v0, v1, v2 = (vs[k, 0, r, MID] for k in range(3))
+        v3, = spread(2, r, 1)
         d0, d1, d2 = d * v0, d * v1, d * v2
         terms = (d0 * v0, d0 * v1, d1 * v1, d1 * v2, d2 * v2, d2 * v3)
         return tuple(t + jnp.sum(x.reshape(8, 8, 128), axis=0) for t, x in zip(total, terms))
-    total = lax.fori_loop(4, 12, sums, tuple(jnp.zeros((8, 128), f32) for _ in range(6)))
+    total = tuple(jnp.zeros((8, 128), f32) for _ in range(6))
+    for r in range(4, 12):
+        total = sums(r, total)
     row = jnp.zeros((1, 128), f32)
-    first = lax.broadcasted_iota(i32, (1, 128), 1)
+    place = lax.broadcasted_iota(i32, (1, 128), 1)
     for k in range(6):
-        row = jnp.where(first == k, jnp.sum(total[k]), row)
+        row = jnp.where(place == k, jnp.sum(total[k]), row)
     moments[...] = jnp.broadcast_to(row[:, None, :], moments.shape)
 
 
-def sweeps(rows, edge_0, edge_1):
-    big = pltpu.VMEM((16, 64, 256), f32)
+def sweeps(refs, packed, edge_0, edge_1):
+    padded, plane = pltpu.VMEM((2, 16, 80, 128), f32), pltpu.VMEM((2, 16, 64, 128), f32)
     return pl.pallas_call(
         sweeps_kernel,
-        out_shape=(S((3, 16, 64, 256), f32), S((NGX * NGY, 1, 128), f32)),
-        in_specs=[VSPEC] * 6,
-        out_specs=(VSPEC,) * 2,
-        scratch_shapes=[pltpu.VMEM((4, 16, 64, 256), f32)] + [big] * 7,
+        out_shape=(S((3, 10, 64, 128), f32), S((3, 8, 64, 128), f32), S((NGX * NGY, 1, 128), f32)),
+        in_specs=[VSPEC] * 8,
+        out_specs=(VSPEC,) * 3,
+        scratch_shapes=[pltpu.VMEM((3, 2, 16, 80, 128), f32), padded, plane, plane, plane, padded, plane, plane],
         compiler_params=VM,
         name="sweeps",
-    )(*rows, edge_0, edge_1)
+    )(*refs, packed, edge_0, edge_1)
 
 
 def coefficients(mu):
@@ -601,34 +707,38 @@
     return pressure
 
 
-def gradient_kernel(all_moments, vs, pressure, table, p):
+def gradient_kernel(all_moments, core, beside, pressure, table, p):
     summed = jnp.sum(all_moments[...], axis=0)
-    mu = [jnp.broadcast_to(summed[:, k:k + 1], (8, 256)) for k in range(6)]
-    coef = [jnp.broadcast_to(c[:1], (64, 256)) for c in coefficients(mu)]
-
-    def combine(r, _):
-        p[r] = coef[0] * vs[0, r] + coef[1] * vs[1, r] + coef[2] * vs[2, r]
-        return 0
-    lax.fori_loop(3, 13, combine, 0)
+    coef = coefficients([jnp.broadcast_to(summed[:, k:k + 1], (8, 128)) for k in range(6)])
+    coef = [jnp.broadcast_to(c[:1], (64, 128)) for c in coef]
+    lane = plane_lanes()
+    first, last = lane == 0, lane == 127
+
+    def combine(ref, r):
+        return coef[0] * ref[0, r] + coef[1] * ref[1, r] + coef[2] * ref[2, r]
+    for r in range(3, 13):
+        p[r, 0:8] = jnp.zeros((8, 128), f32)
+        p[r, 72:80] = jnp.zeros((8, 128), f32)
+        p[r, MID] = combine(core, r - 3)
     for x in range(8):
-        here = p[x + 4]
-        core = here[:, 0:128]
-        pressure[pl.ds(x, 64, stride=8), :] = core
-        put_table(table, 0, x, 0.5 * (p[x + 5][:, 0:128] - p[x + 3][:, 0:128]))
-        put_table(table, 1, x, 0.5 * (up_y(here) - down_y(here))[:, 0:128])
-        put_table(table, 2, x, 0.5 * (up_z(core) - down_z(core)))
-
-
-def gradients(all_moments, vs):
+        r = x + 4
+        pair = (p[r, MID], combine(beside, x))
+        pressure[pl.ds(x, 64, stride=8), :] = pair[0]
+        put_table(table, 0, x, 0.5 * (p[r + 1, MID] - p[r - 1, MID]))
+        put_table(table, 1, x, 0.5 * (up_pair(pair, last)[0] - down_pair(pair, first)[0]))
+        put_table(table, 2, x, 0.5 * (p[r, UP] - p[r, DOWN]))
+
+
+def gradients(all_moments, core, beside):
     return pl.pallas_call(
         gradient_kernel,
         out_shape=(S((512, 128), f32), S((NW, 48, 256), bf16)),
-        in_specs=[VSPEC] * 2,
+        in_specs=[VSPEC] * 3,
         out_specs=(VSPEC,) * 2,
-        scratch_shapes=[pltpu.VMEM((16, 64, 256), f32)],
+        scratch_shapes=[pltpu.VMEM((16, 80, 128), f32)],
         compiler_params=VM,
         name="gradients",
-    )(all_moments, vs)
+    )(all_moments, core, beside)
 
 
 def arrange_kernel(*refs):
@@ -682,7 +792,7 @@
             stage[7 * PR:8 * PR, :] = jnp.zeros((PR, 128), f32)
         pos_ref = (pos_a, pos_b)[g]
 
-        def chunk(c, _):
+        def chunk(c):
             k = pos_ref[c]
             at, src = k & 127, k >> 7
             acc = [jnp.zeros((8, 128), f32) for _ in range(3)]
@@ -693,8 +803,7 @@
                     acc[f] = jnp.where(here, got, acc[f])
             for f in range(3):
                 found[g, f, c] = acc[f]
-            return 0
-        lax.fori_loop(0, CH, chunk, 0)
+        unrolled(CH, 8, chunk)
     row = lax.broadcasted_iota(i32, (8, 128), 0)
     for dx in (-2, -1, 0, 1, 2):
         pieces = [(g, run) for g, runs in enumerate(groups) for run in runs if run[0] == dx]
@@ -762,13 +871,13 @@
     ]
     bases = tuple(range(0, 5 * BR, BR))
     acc = deposit([mine], bases, 8)
-    table, own_0, own_1, token = deposit(sides, bases, 4, acc, fluid_velocity.reshape(3, 512, 128))
-    rows = (own_0, own_1, exchange(own_0, "gx", 1, 0), exchange(own_1, "gx", 1, 1))
+    table, own, send_0, send_1, token = deposit(sides, bases, 4, acc, fluid_velocity.reshape(3, 512, 128))
+    rows = (own, send_0, send_1, exchange(send_0, "gx", 1, 0), exchange(send_1, "gx", 1, 1))
     *pos, token = inverse(keys_a, keys_b, token)
     packed = pack_edges(rows, token)
-    vs, moments = sweeps(rows, exchange(packed, "gy", 1, 0), exchange(packed, "gy", 1, 1))
+    core, beside, moments = sweeps(rows, packed, exchange(packed, "gy", 1, 0), exchange(packed, "gy", 1, 1))
     everyone = lax.all_to_all(moments, ("gx", "gy"), 0, 0)
-    pressure, slopes = gradients(everyone, vs)
+    pressure, slopes = gradients(everyone, core, beside)
     far_0, far_1, token = interp(sides, bases, table, slopes, 4, token, 2)
     back = [exchange(far_0, "gy", 1, 0), exchange(far_1, "gy", 1, 1)]
     near, _ = interp([mine], bases, table, slopes, 8, token, 1)

time: 179 us -> 162 us (0.905)
  Pallas kernels: 94.3 us -> 81.6 us
  waiting for transfers between devices: 21.1 us -> 16 us
    pallas_call x2, Pallas kernels: 13.5 us -> 7.52 us  [the longest x1 5.15 us: sweeps(): pl.pallas_call(sweeps_kernel, out_shape=(S((3, 10, 64, 128), f32), S((3,...]
    ppermute x16, waiting for transfers between devices: 21.1 us -> 16 us  [exchange(): return lax.ppermute(x, axis, pairs + [(j, i) for i, j in pairs])]
    pallas_call x2, Pallas kernels: 22.4 us -> 19 us  [sort_blocks(): pl.pallas_call(functools.partial(sort_kernel, runs, n), out_shape=tuple(s...]
    pallas_call x1, Pallas kernels: 9.69 us -> 6.82 us  [place_forces(): pl.pallas_call(functools.partial(place_kernel, len(backs), GROUPS), out_s...]
  transfers between devices with their start and end apart: 16 -> 16, of which waited for: 7 -> 6; matrix products, arithmetic and copies ran while one was open for 1% -> 1% of each run, Pallas kernels for 17% -> 18%
where the time goes in v3:
time: 162 us; the launch traced here: 161 us
  Pallas kernels  81.6 us (50%)
  starting transfers between devices  40 us (25%)
  blocking collectives  16.9 us (10%)
  waiting for transfers between devices  16 us (10%)
  local copies, waits for them, and re-layouts  5.24 us (3%)
    ppermute x16, starting transfers between devices, exchange(): return lax.ppermute(x, axis, pairs + [(j, i) for i, j in pairs])  40 us
    pallas_call x2, Pallas kernels, deposit(): pl.pallas_call(functools.partial(deposit_kernel, len(arrays), bases, unro...  19.3 us
    pallas_call x2, Pallas kernels, sort_blocks(): pl.pallas_call(functools.partial(sort_kernel, runs, n), out_shape=tuple(s...  19 us
    pallas_call x2, Pallas kernels, interp(): pl.pallas_call(functools.partial(interp_kernel, len(arrays), bases, unrol...  18.9 us
    all_to_all x1, blocking collectives, per_device(): everyone = lax.all_to_all(moments, ('gx', 'gy'), 0, 0)  16.9 us
    ppermute x16, waiting for transfers between devices, exchange(): return lax.ppermute(x, axis, pairs + [(j, i) for i, j in pairs])  16 us
    pallas_call x1, Pallas kernels, place_forces(): pl.pallas_call(functools.partial(place_kernel, len(backs), GROUPS), out_s...  6.82 us
    unnamed x33, local copies, waits for them, and re-layouts  5.22 us
  transfers between devices with their start and end apart: 16, of which 6 were waited for; matrix products, arithmetic and copies ran while one was open for 1% of the time, Pallas kernels for 18%

profile of v3, /device:TPU:10, one launch (start us, length us, event | category | flops | bytes accessed | tf_op | source)
XLA Modules:
  0.0 160.8 jit_solution(11640485937449699980)
XLA Ops:
  0.6 9.5 %sort_blocks.2 = (f32[456,128]{1,0:T(8,128)}, f32[456,128]{1,0:T(8,128)}, f32[304,128]{1,0:T(8,128)}, s32[24,8,128]{2,1,0:T(8,128)}) custom-call(f32[5,1,128,3072]{3,2,1,0:T(8,128)} %data_ref.3, s32[2,1,128,3072]{3,2,1,0:T(8,128)} %cells_ref.3, s32[1,128]{1,0:T(1,128)} %counts_ref.3), custom_call_target="tpu_custom_call" | custom-call | tf_op jit(solution)/shard_map/sort_blocks/pallas_call | solution.py:201
  10.1 4.0 %collective-permute-start = (f32[456,128]{1,0:T(8,128)}, f32[456,128]{1,0:T(8,128)S(1)}, u32[]{:S(2)}, u32[]{:S(2)}) collective-permute-start(f32[456,128]{1,0:T(8,128)} %get-tuple-element.32), channel_id=1, source_target_pairs={{0,16},{8,24},{32,48},{40,56},{64,80},{72,88},{96,112},{104,120},{... | collective-permute-start | bytes 700424 | tf_op jit(solution)/shard_map/ppermute | solution.py:857
  14.1 2.0 %collective-permute-start.1 = (f32[456,128]{1,0:T(8,128)}, f32[456,128]{1,0:T(8,128)S(1)}, u32[]{:S(2)}, u32[]{:S(2)}) collective-permute-start(f32[456,128]{1,0:T(8,128)} %get-tuple-element.33), channel_id=1, source_target_pairs={{16,32},{24,40},{48,64},{56,72},{80,96},{88,104},{32,16},{40,24},{... | collective-permute-start | bytes 700424 | tf_op jit(solution)/shard_map/ppermute | solution.py:857
  16.1 9.5 %sort_blocks.3 = (f32[456,128]{1,0:T(8,128)}, f32[456,128]{1,0:T(8,128)}, f32[152,128]{1,0:T(8,128)}, s32[24,8,128]{2,1,0:T(8,128)}) custom-call(f32[5,1,128,3072]{3,2,1,0:T(8,128)} %data_ref.3, s32[2,1,128,3072]{3,2,1,0:T(8,128)} %cells_ref.3, s32[1,128]{1,0:T(1,128)} %counts_ref.3), custom_call_target="tpu_custom_call" | custom-call | tf_op jit(solution)/shard_map/sort_blocks/pallas_call | solution.py:201
  25.6 1.6 %collective-permute-start.2 = (f32[456,128]{1,0:T(8,128)}, f32[456,128]{1,0:T(8,128)S(1)}, u32[]{:S(2)}, u32[]{:S(2)}) collective-permute-start(f32[456,128]{1,0:T(8,128)} %get-tuple-element.35), channel_id=1, source_target_pairs={{0,8},{16,24},{32,40},{48,56},{64,72},{80,88},{96,104},{112,120},{... | collective-permute-start | bytes 700424 | tf_op jit(solution)/shard_map/ppermute | solution.py:857
  27.2 5.3 %collective-permute-start.3 = (f32[456,128]{1,0:T(8,128)}, f32[456,128]{1,0:T(8,128)S(1)}, u32[]{:S(2)}, u32[]{:S(2)}) collective-permute-start(f32[456,128]{1,0:T(8,128)} %get-tuple-element.36), channel_id=1, source_target_pairs={{8,16},{24,32},{40,48},{56,64},{72,80},{88,96},{104,112},{16,8},{3... | collective-permute-start | bytes 700424 | tf_op jit(solution)/shard_map/ppermute | solution.py:857
  32.7 0.9 constant_dynamic-update-slice_fusion
  33.6 4.4 %collective-permute-done.3 = f32[456,128]{1,0:T(8,128)S(1)} collective-permute-done((f32[456,128]{1,0:T(8,128)}, f32[456,128]{1,0:T(8,128)S(1)}, u32[]{:S(2)}, u32[]{:S(2)}) %collective-permute-start.3) | collective-permute-done | bytes 233504 | tf_op jit(solution)/shard_map/ppermute | solution.py:857
  38.1 1.9 %collective-permute-start.5 = (f32[760,128]{1,0:T(8,128)S(1)}, f32[760,128]{1,0:T(8,128)S(1)}, u32[]{:S(2)}, u32[]{:S(2)}) collective-permute-start(f32[760,128]{1,0:T(8,128)S(1)} %get-tuple-element.62), channel_id=1, source_target_pairs={{1,2},{3,4},{5,6},{2,1},{4,3},{6,5},{9,10},{11,12},{13,14},{10,9},... | collective-permute-start | bytes 1167368 | tf_op jit(solution)/shard_map/ppermute | solution.py:857
  40.0 1.8 %collective-permute-start.4 = (f32[760,128]{1,0:T(8,128)S(1)}, f32[760,128]{1,0:T(8,128)S(1)}, u32[]{:S(2)}, u32[]{:S(2)}) collective-permute-start(f32[760,128]{1,0:T(8,128)S(1)} %get-tuple-element.63), channel_id=1, source_target_pairs={{0,1},{2,3},{4,5},{6,7},{1,0},{3,2},{5,4},{7,6},{8,9},{10,11},{12,... | collective-permute-start | bytes 1167368 | tf_op jit(solution)/shard_map/ppermute | solution.py:857
  41.8 6.8 %deposit.2.refs_2_ = f32[5,512,128]{2,1,0:T(8,128)} custom-call(f32[760,128]{1,0:T(8,128)} %copy-done.11), custom_call_target="tpu_custom_call" | custom-call | flops 5000000000 | bytes 15000000 | tf_op jit(solution)/shard_map/deposit/pallas_call | solution.py:333
  49.5 12.5 %deposit.3 = (bf16[32,48,256]{2,1,0:T(8,128)(2,1)}, f32[2,8,64,128]{3,2,1,0:T(8,128)}, f32[9,64,128]{2,1,0:T(8,128)}, f32[9,64,128]{2,1,0:T(8,128)}, f32[8,128]{1,0:T(8,128)}) custom-call(f32[760,128]{1,0:T(8,128)} %copy-done.13, f32[760,128]{1,0:T(8,128)} %copy-done.12, f32[5,512,128]{2,1,0:T(8,128)} %deposit.2.refs_2_, f32[3,512,128]{2,1,0:T(8,128)} %bitcast.2), custom_call_target="tpu_custom_call" | custom-call | flops 10000000000 | bytes 30000000 | tf_op jit(solution)/shard_map/deposit/pallas_call | solution.py:333
  62.8 4.9 %collective-permute-start.7 = (f32[9,64,128]{2,1,0:T(8,128)}, f32[9,64,128]{2,1,0:T(8,128)S(1)}, u32[]{:S(2)}, u32[]{:S(2)}) collective-permute-start(f32[9,64,128]{2,1,0:T(8,128)} %get-tuple-element.40.sent_1), channel_id=1, source_target_pairs={{8,16},{24,32},{40,48},{56,64},{72,80},{88,96},{104,112},{16,8},{3... | collective-permute-start | bytes 884744 | tf_op jit(solution)/shard_map/ppermute | solution.py:857
  67.7 5.1 %inverse.1 = (s32[24,8,128]{2,1,0:T(8,128)}, s32[24,8,128]{2,1,0:T(8,128)}, f32[8,128]{1,0:T(8,128)}) custom-call(s32[24,8,128]{2,1,0:T(8,128)} %get-tuple-element.41.keys_a, s32[24,8,128]{2,1,0:T(8,128)} %get-tuple-element.42.keys_b, f32[8,128]{1,0:T(8,128)} %get-tuple-element.43.after), custom_call_target="tpu_custom_call" | custom-call | flops 1000000000 | bytes 20000000 | tf_op jit(solution)/shard_map/inverse/pallas_call | solution.py:186
  72.8 2.8 %collective-permute-done.7.got_1 = f32[9,64,128]{2,1,0:T(8,128)S(1)} collective-permute-done((f32[9,64,128]{2,1,0:T(8,128)}, f32[9,64,128]{2,1,0:T(8,128)S(1)}, u32[]{:S(2)}, u32[]{:S(2)}) %collective-permute-start.7) | collective-permute-done | bytes 294944 | tf_op jit(solution)/shard_map/ppermute | solution.py:857
  76.4 2.4 %pack_edges.1.packed = f32[3,64,128]{2,1,0:T(8,128)} custom-call(f32[2,8,64,128]{3,2,1,0:T(8,128)} %get-tuple-element.38.own, f32[9,64,128]{2,1,0:T(8,128)} %get-tuple-element.39.sent_0, f32[9,64,128]{2,1,0:T(8,128)} %get-tuple-element.40.sent_1, f32[9,64,128]{2,1,0:T(8,128)} %copy-done, f32[9,64,128]{2,1,0:T(8,128)} %copy-done.1, ...), custom_call_target="tpu_custom_call" | custom-call | tf_op jit(solution)/shard_map/pack_edges/pallas_call | solution.py:544
  78.7 1.9 %collective-permute-start.9 = (f32[3,64,128]{2,1,0:T(8,128)}, f32[3,64,128]{2,1,0:T(8,128)S(1)}, u32[]{:S(2)}, u32[]{:S(2)}) collective-permute-start(f32[3,64,128]{2,1,0:T(8,128)} %pack_edges.1.packed), channel_id=1, source_target_pairs={{1,2},{3,4},{5,6},{2,1},{4,3},{6,5},{9,10},{11,12},{13,14},{10,9},... | collective-permute-start | bytes 294920 | tf_op jit(solution)/shard_map/ppermute | solution.py:857
  80.6 1.5 collective-permute-start.8
  82.1 2.8 %collective-permute-done.9.edge_1 = f32[3,64,128]{2,1,0:T(8,128)S(1)} collective-permute-done((f32[3,64,128]{2,1,0:T(8,128)}, f32[3,64,128]{2,1,0:T(8,128)S(1)}, u32[]{:S(2)}, u32[]{:S(2)}) %collective-permute-start.9) | collective-permute-done | bytes 98336 | tf_op jit(solution)/shard_map/ppermute | solution.py:857
  86.1 5.2 %sweeps.1 = (f32[3,10,64,128]{3,2,1,0:T(8,128)}, f32[3,8,64,128]{3,2,1,0:T(8,128)}, f32[128,1,128]{2,1,0:T(1,128)}) custom-call(f32[2,8,64,128]{3,2,1,0:T(8,128)} %get-tuple-element.38.own, f32[9,64,128]{2,1,0:T(8,128)} %get-tuple-element.39.sent_0, f32[9,64,128]{2,1,0:T(8,128)} %get-tuple-element.40.sent_1, f32[9,64,128]{2,1,0:T(8,128)} %copy-done, ...), custom_call_target="tpu_custom_call" | custom-call | tf_op jit(solution)/shard_map/sweeps/pallas_call | solution.py:676
  91.3 16.9 %all_to_all.5.all_moments = f32[128,1,128]{2,1,0:T(1,128)} all-to-all(f32[128,1,128]{2,1,0:T(1,128)} %get-tuple-element.45), channel_id=1, replica_groups=mesh['gx'=16,'gy'=8] {'gx','gy'}, dimensions={0} | all-to-all | bytes 131072 | tf_op jit(solution)/shard_map/all_to_all | solution.py:879
  108.2 3.0 %gradients.1 = (f32[512,128]{1,0:T(8,128)}, bf16[32,48,256]{2,1,0:T(8,128)(2,1)}) custom-call(f32[128,1,128]{2,1,0:T(1,128)} %all_to_all.5.all_moments, f32[3,10,64,128]{3,2,1,0:T(8,128)} %get-tuple-element.46.core, f32[3,8,64,128]{3,2,1,0:T(8,128)} %get-tuple-element.47.beside), custom_call_target="tpu_custom_call" | custom-call | tf_op jit(solution)/shard_map/gradients/pallas_call | solution.py:733
  111.3 11.7 %interp.2 = (f32[360,128]{1,0:T(8,128)}, f32[360,128]{1,0:T(8,128)}, f32[8,128]{1,0:T(8,128)}) custom-call(f32[760,128]{1,0:T(8,128)} %copy-done.13, f32[760,128]{1,0:T(8,128)} %copy-done.12, bf16[32,48,256]{2,1,0:T(8,128)(2,1)} %get-tuple-element.49.refs_2_.refs_1_, bf16[32,48,256]{2,1,0:T(8,128)(2,1)} %get-tuple-element.50.refs_3_.refs_2_, ...), custom_call_target="tpu_custom_call" | custom-call | flops 10000000000 | bytes 30000000 | tf_op jit(solution)/shard_map/interp/pallas_call | solution.py:415
  123.2 3.8 %collective-permute-start.11 = (f32[360,128]{1,0:T(8,128)}, f32[360,128]{1,0:T(8,128)S(1)}, u32[]{:S(2)}, u32[]{:S(2)}) collective-permute-start(f32[360,128]{1,0:T(8,128)} %get-tuple-element.54), channel_id=1, source_target_pairs={{1,2},{3,4},{5,6},{2,1},{4,3},{6,5},{9,10},{11,12},{13,14},{10,9},... | collective-permute-start | bytes 552968 | tf_op jit(solution)/shard_map/ppermute | solution.py:857
  127.0 7.2 %interp.3 = (f32[360,128]{1,0:T(8,128)}, f32[8,128]{1,0:T(8,128)}) custom-call(f32[760,128]{1,0:T(8,128)} %copy-done.11, bf16[32,48,256]{2,1,0:T(8,128)(2,1)} %get-tuple-element.49.refs_2_.refs_1_, bf16[32,48,256]{2,1,0:T(8,128)(2,1)} %get-tuple-element.50.refs_3_.refs_2_, f32[8,128]{1,0:T(8,128)} %get-tuple-element.52.refs_3_), custom_call_target="tpu_custom_call" | custom-call | flops 5000000000 | bytes 15000000 | tf_op jit(solution)/shard_map/interp/pallas_call | solution.py:415
  134.9 1.9 %arrange.1 = (f32[216,128]{1,0:T(8,128)}, f32[216,128]{1,0:T(8,128)}, f32[216,128]{1,0:T(8,128)}, f32[216,128]{1,0:T(8,128)}, f32[216,128]{1,0:T(8,128)}) custom-call(f32[360,128]{1,0:T(8,128)} %copy-done.2, f32[360,128]{1,0:T(8,128)} %get-tuple-element.53.refs_1_, f32[360,128]{1,0:T(8,128)} %copy-done.3), custom_call_target="tpu_custom_call" | custom-call | tf_op jit(solution)/shard_map/arrange/pallas_call | solution.py:751
  136.9 1.5 collective-permute-start.12
  138.3 4.8 %collective-permute-start.13 = (f32[216,128]{1,0:T(8,128)}, f32[216,128]{1,0:T(8,128)S(1)}, u32[]{:S(2)}, u32[]{:S(2)}) collective-permute-start(f32[216,128]{1,0:T(8,128)} %get-tuple-element.56), channel_id=1, source_target_pairs={{16,32},{24,40},{48,64},{56,72},{80,96},{88,104},{32,16},{40,24},{... | collective-permute-start | bytes 331784 | tf_op jit(solution)/shard_map/ppermute | solution.py:857
  143.2 1.1 collective-permute-start.14
  144.2 3.0 %collective-permute-start.15 = (f32[216,128]{1,0:T(8,128)}, f32[216,128]{1,0:T(8,128)S(1)}, u32[]{:S(2)}, u32[]{:S(2)}) collective-permute-start(f32[216,128]{1,0:T(8,128)} %get-tuple-element.59), channel_id=1, source_target_pairs={{8,16},{24,32},{40,48},{56,64},{72,80},{88,96},{104,112},{16,8},{3... | collective-permute-start | bytes 331784 | tf_op jit(solution)/shard_map/ppermute | solution.py:857
  148.2 5.0 %collective-permute-done.15.refs_4_ = f32[216,128]{1,0:T(8,128)S(1)} collective-permute-done((f32[216,128]{1,0:T(8,128)}, f32[216,128]{1,0:T(8,128)S(1)}, u32[]{:S(2)}, u32[]{:S(2)}) %collective-permute-start.15) | collective-permute-done | bytes 110624 | tf_op jit(solution)/shard_map/ppermute | solution.py:857
  153.8 6.8 %place_forces.1 = f32[3,1,128,3072]{3,2,1,0:T(8,128)} custom-call(f32[216,128]{1,0:T(8,128)} %copy-done.5, f32[216,128]{1,0:T(8,128)} %copy-done.6, f32[216,128]{1,0:T(8,128)} %get-tuple-element.57.refs_2_, f32[216,128]{1,0:T(8,128)} %copy-done.7, f32[216,128]{1,0:T(8,128)} %copy-done.8, s32[24,8,128]{2,1,0:T(8,128)} %get-tuple-element.60.refs_5_, ...), custom_call_target="tpu_custom_call" | custom-call | tf_op jit(solution)/shard_map/place_forces/pallas_call | solution.py:836
  (48 shorter events, 6.3 us)
Async XLA Ops:
  10.1 22.5 %collective-permute-start = (f32[456,128]{1,0:T(8,128)}, f32[456,128]{1,0:T(8,128)S(1)}, u32[]{:S(2)}, u32[]{:S(2)}) collective-permute-start(f32[456,128]{1,0:T(8,128)} %get-tuple-element.32), channel_id=1, source_target_pairs={{0,16},{8,24},{32,48},{40,56},{64,80},{72,88},{96,112},{104,120},{... | collective-permute-start | bytes 700424 | tf_op jit(solution)/shard_map/ppermute | solution.py:857
  14.1 18.6 %copy-start.4 = (f32[304,128]{1,0:T(8,128)S(1)}, f32[304,128]{1,0:T(8,128)}, u32[]{:S(2)}) copy-start(f32[304,128]{1,0:T(8,128)} %get-tuple-element.37) | copy-start | bytes 466948
  14.1 18.5 %collective-permute-start.1 = (f32[456,128]{1,0:T(8,128)}, f32[456,128]{1,0:T(8,128)S(1)}, u32[]{:S(2)}, u32[]{:S(2)}) collective-permute-start(f32[456,128]{1,0:T(8,128)} %get-tuple-element.33), channel_id=1, source_target_pairs={{16,32},{24,40},{48,64},{56,72},{80,96},{88,104},{32,16},{40,24},{... | collective-permute-start | bytes 700424 | tf_op jit(solution)/shard_map/ppermute | solution.py:857
  25.6 8.0 %collective-permute-start.2 = (f32[456,128]{1,0:T(8,128)}, f32[456,128]{1,0:T(8,128)S(1)}, u32[]{:S(2)}, u32[]{:S(2)}) collective-permute-start(f32[456,128]{1,0:T(8,128)} %get-tuple-element.35), channel_id=1, source_target_pairs={{0,8},{16,24},{32,40},{48,56},{64,72},{80,88},{96,104},{112,120},{... | collective-permute-start | bytes 700424 | tf_op jit(solution)/shard_map/ppermute | solution.py:857
  27.2 10.8 %collective-permute-start.3 = (f32[456,128]{1,0:T(8,128)}, f32[456,128]{1,0:T(8,128)S(1)}, u32[]{:S(2)}, u32[]{:S(2)}) collective-permute-start(f32[456,128]{1,0:T(8,128)} %get-tuple-element.36), channel_id=1, source_target_pairs={{8,16},{24,32},{40,48},{56,64},{72,80},{88,96},{104,112},{16,8},{3... | collective-permute-start | bytes 700424 | tf_op jit(solution)/shard_map/ppermute | solution.py:857
  38.0 3.8 %copy-start.11 = (f32[760,128]{1,0:T(8,128)}, f32[760,128]{1,0:T(8,128)S(1)}, u32[]{:S(2)}) copy-start(f32[760,128]{1,0:T(8,128)S(1)} %get-tuple-element.64.refs_0_) | copy-start | bytes 1167364
  38.1 10.5 %collective-permute-start.5 = (f32[760,128]{1,0:T(8,128)S(1)}, f32[760,128]{1,0:T(8,128)S(1)}, u32[]{:S(2)}, u32[]{:S(2)}) collective-permute-start(f32[760,128]{1,0:T(8,128)S(1)} %get-tuple-element.62), channel_id=1, source_target_pairs={{1,2},{3,4},{5,6},{2,1},{4,3},{6,5},{9,10},{11,12},{13,14},{10,9},... | collective-permute-start | bytes 1167368 | tf_op jit(solution)/shard_map/ppermute | solution.py:857
  40.0 8.6 %collective-permute-start.4 = (f32[760,128]{1,0:T(8,128)S(1)}, f32[760,128]{1,0:T(8,128)S(1)}, u32[]{:S(2)}, u32[]{:S(2)}) collective-permute-start(f32[760,128]{1,0:T(8,128)S(1)} %get-tuple-element.63), channel_id=1, source_target_pairs={{0,1},{2,3},{4,5},{6,7},{1,0},{3,2},{5,4},{7,6},{8,9},{10,11},{12,... | collective-permute-start | bytes 1167368 | tf_op jit(solution)/shard_map/ppermute | solution.py:857
  48.6 0.7 copy-start.12
  48.6 0.9 copy-start.13
  62.1 10.7 %collective-permute-start.6 = (f32[9,64,128]{2,1,0:T(8,128)}, f32[9,64,128]{2,1,0:T(8,128)S(1)}, u32[]{:S(2)}, u32[]{:S(2)}) collective-permute-start(f32[9,64,128]{2,1,0:T(8,128)} %get-tuple-element.39.sent_0), channel_id=1, source_target_pairs={{0,8},{16,24},{32,40},{48,56},{64,72},{80,88},{96,104},{112,120},{... | collective-permute-start | bytes 884744 | tf_op jit(solution)/shard_map/ppermute | solution.py:857
  62.8 12.9 %collective-permute-start.7 = (f32[9,64,128]{2,1,0:T(8,128)}, f32[9,64,128]{2,1,0:T(8,128)S(1)}, u32[]{:S(2)}, u32[]{:S(2)}) collective-permute-start(f32[9,64,128]{2,1,0:T(8,128)} %get-tuple-element.40.sent_1), channel_id=1, source_target_pairs={{8,16},{24,32},{40,48},{56,64},{72,80},{88,96},{104,112},{16,8},{3... | collective-permute-start | bytes 884744 | tf_op jit(solution)/shard_map/ppermute | solution.py:857
  72.8 2.9 %copy-start = (f32[9,64,128]{2,1,0:T(8,128)}, f32[9,64,128]{2,1,0:T(8,128)S(1)}, u32[]{:S(2)}) copy-start(f32[9,64,128]{2,1,0:T(8,128)S(1)} %collective-permute-done.6.got_0) | copy-start | bytes 884740
  75.7 0.7 copy-start.1
  78.7 6.1 %collective-permute-start.9 = (f32[3,64,128]{2,1,0:T(8,128)}, f32[3,64,128]{2,1,0:T(8,128)S(1)}, u32[]{:S(2)}, u32[]{:S(2)}) collective-permute-start(f32[3,64,128]{2,1,0:T(8,128)} %pack_edges.1.packed), channel_id=1, source_target_pairs={{1,2},{3,4},{5,6},{2,1},{4,3},{6,5},{9,10},{11,12},{13,14},{10,9},... | collective-permute-start | bytes 294920 | tf_op jit(solution)/shard_map/ppermute | solution.py:857
  80.6 4.2 %collective-permute-start.8 = (f32[3,64,128]{2,1,0:T(8,128)}, f32[3,64,128]{2,1,0:T(8,128)S(1)}, u32[]{:S(2)}, u32[]{:S(2)}) collective-permute-start(f32[3,64,128]{2,1,0:T(8,128)} %pack_edges.1.packed), channel_id=1, source_target_pairs={{0,1},{2,3},{4,5},{6,7},{1,0},{3,2},{5,4},{7,6},{8,9},{10,11},{12,... | collective-permute-start | bytes 294920 | tf_op jit(solution)/shard_map/ppermute | solution.py:857
  84.9 0.6 copy-start.9
  85.5 0.6 copy-start.10
  123.0 11.2 %collective-permute-start.10 = (f32[360,128]{1,0:T(8,128)}, f32[360,128]{1,0:T(8,128)S(1)}, u32[]{:S(2)}, u32[]{:S(2)}) collective-permute-start(f32[360,128]{1,0:T(8,128)} %get-tuple-element.51), channel_id=1, source_target_pairs={{0,1},{2,3},{4,5},{6,7},{1,0},{3,2},{5,4},{7,6},{8,9},{10,11},{12,... | collective-permute-start | bytes 552968 | tf_op jit(solution)/shard_map/ppermute | solution.py:857
  123.2 11.0 %collective-permute-start.11 = (f32[360,128]{1,0:T(8,128)}, f32[360,128]{1,0:T(8,128)S(1)}, u32[]{:S(2)}, u32[]{:S(2)}) collective-permute-start(f32[360,128]{1,0:T(8,128)} %get-tuple-element.54), channel_id=1, source_target_pairs={{1,2},{3,4},{5,6},{2,1},{4,3},{6,5},{9,10},{11,12},{13,14},{10,9},... | collective-permute-start | bytes 552968 | tf_op jit(solution)/shard_map/ppermute | solution.py:857
  134.2 0.7 copy-start.2
  134.2 0.7 copy-start.3
  136.9 10.4 %collective-permute-start.12 = (f32[216,128]{1,0:T(8,128)}, f32[216,128]{1,0:T(8,128)S(1)}, u32[]{:S(2)}, u32[]{:S(2)}) collective-permute-start(f32[216,128]{1,0:T(8,128)} %get-tuple-element.55), channel_id=1, source_target_pairs={{0,16},{8,24},{32,48},{40,56},{64,80},{72,88},{96,112},{104,120},{... | collective-permute-start | bytes 331784 | tf_op jit(solution)/shard_map/ppermute | solution.py:857
  138.3 9.3 %collective-permute-start.13 = (f32[216,128]{1,0:T(8,128)}, f32[216,128]{1,0:T(8,128)S(1)}, u32[]{:S(2)}, u32[]{:S(2)}) collective-permute-start(f32[216,128]{1,0:T(8,128)} %get-tuple-element.56), channel_id=1, source_target_pairs={{16,32},{24,40},{48,64},{56,72},{80,96},{88,104},{32,16},{40,24},{... | collective-permute-start | bytes 331784 | tf_op jit(solution)/shard_map/ppermute | solution.py:857
  143.2 5.0 %collective-permute-start.14 = (f32[216,128]{1,0:T(8,128)}, f32[216,128]{1,0:T(8,128)S(1)}, u32[]{:S(2)}, u32[]{:S(2)}) collective-permute-start(f32[216,128]{1,0:T(8,128)} %get-tuple-element.58), channel_id=1, source_target_pairs={{0,8},{16,24},{32,40},{48,56},{64,72},{80,88},{96,104},{112,120},{... | collective-permute-start | bytes 331784 | tf_op jit(solution)/shard_map/ppermute | solution.py:857
  144.2 8.9 %collective-permute-start.15 = (f32[216,128]{1,0:T(8,128)}, f32[216,128]{1,0:T(8,128)S(1)}, u32[]{:S(2)}, u32[]{:S(2)}) collective-permute-start(f32[216,128]{1,0:T(8,128)} %get-tuple-element.59), channel_id=1, source_target_pairs={{8,16},{24,32},{40,48},{56,64},{72,80},{88,96},{104,112},{16,8},{3... | collective-permute-start | bytes 331784 | tf_op jit(solution)/shard_map/ppermute | solution.py:857
  147.2 5.9 %copy-start.5 = (f32[216,128]{1,0:T(8,128)}, f32[216,128]{1,0:T(8,128)S(1)}, u32[]{:S(2)}) copy-start(f32[216,128]{1,0:T(8,128)S(1)} %collective-permute-done.12.refs_0_) | copy-start | bytes 331780
  147.7 5.5 %copy-start.6 = (f32[216,128]{1,0:T(8,128)}, f32[216,128]{1,0:T(8,128)S(1)}, u32[]{:S(2)}) copy-start(f32[216,128]{1,0:T(8,128)S(1)} %collective-permute-done.13.refs_1_) | copy-start | bytes 331780
  148.2 5.0 %copy-start.7 = (f32[216,128]{1,0:T(8,128)}, f32[216,128]{1,0:T(8,128)S(1)}, u32[]{:S(2)}) copy-start(f32[216,128]{1,0:T(8,128)S(1)} %collective-permute-done.14.refs_3_) | copy-start | bytes 331780
  153.2 0.6 copy-start.8

commit v4 on v3

--- a/solution.py
+++ b/solution.py
@@ -13,7 +13,7 @@
 NW = 32
 SPAN = WL * 128
 PR = 3 * CH
-VM = pltpu.CompilerParams(vmem_limit_bytes=56 * 1024 * 1024)
+VM = pltpu.CompilerParams(vmem_limit_bytes=24 * 1024 * 1024)
 VSPEC = pl.BlockSpec(memory_space=pltpu.VMEM)
 S = jax.ShapeDtypeStruct
 TOKEN = S((8, 128), f32)
@@ -201,7 +201,7 @@
     return pl.pallas_call(
         functools.partial(sort_kernel, runs, n),
         out_shape=tuple(shapes),
-        in_specs=[pl.BlockSpec(memory_space=pl.ANY)] * 2 + [pl.BlockSpec(memory_space=pltpu.SMEM)],
+        in_specs=[pl.BlockSpec(memory_space=pltpu.HBM)] * 2 + [pl.BlockSpec(memory_space=pltpu.SMEM)],
         out_specs=(pl.BlockSpec(memory_space=pltpu.VMEM),) * (n + 1),
         scratch_shapes=[
             pltpu.VMEM((n, 5, 8, 3072), f32),
@@ -211,7 +211,7 @@
             pltpu.VMEM((8 * BR, 128), f32),
             pltpu.SemaphoreType.DMA((2 * n,)),
         ],
-        compiler_params=VM,
+        compiler_params=pltpu.CompilerParams(vmem_limit_bytes=56 * 1024 * 1024),
         name="sort_blocks",
     )(data, cells, counts)
 

time: 162 us -> 138 us (0.85)
  Pallas kernels: 81.6 us -> 61.7 us
  local copies, waits for them, and re-layouts: 5.24 us -> 0.99 us
    pallas_call x2, Pallas kernels: 19.3 us -> 14.2 us  [deposit(): pl.pallas_call(functools.partial(deposit_kernel, len(arrays), bases, unro...]
    unnamed x33 -> x13, local copies, waits for them, and re-layouts: 5.22 us -> 0.98 us
    pallas_call x2, Pallas kernels: 18.9 us -> 14.7 us  [interp(): pl.pallas_call(functools.partial(interp_kernel, len(arrays), bases, unrol...]
    pallas_call x1, Pallas kernels: 5.15 us -> 3.03 us  [sweeps(): pl.pallas_call(sweeps_kernel, out_shape=(S((3, 10, 64, 128), f32), S((3,...]
    pallas_call x1, Pallas kernels: 2.37 us -> 0.34 us  [pack_edges(): pl.pallas_call(pack_kernel, out_shape=S((3, 64, 128), f32), in_specs=[VSP...]
    pallas_call x1, Pallas kernels: 1.92 us -> 0.04 us  [arrange(): pl.pallas_call(arrange_kernel, out_shape=(S((3 * PR, 128), f32),) * 5, in...]
    pallas_call x1, Pallas kernels: 3.04 us -> 1.26 us  [gradients(): pl.pallas_call(gradient_kernel, out_shape=(S((512, 128), f32), S((NW, 48,...]
  transfers between devices with their start and end apart: 16 -> 16, of which waited for: 6 -> 7; matrix products, arithmetic and copies ran while one was open for 1% -> 1% of each run, Pallas kernels for 18% -> 17%
where the time goes in v4:
time: 138 us
  Pallas kernels  61.7 us (45%)
  starting transfers between devices  39.9 us (29%)
  waiting for transfers between devices  17.4 us (13%)
  blocking collectives  16.7 us (12%)
    ppermute x16, starting transfers between devices, exchange(): return lax.ppermute(x, axis, pairs + [(j, i) for i, j in pairs])  39.9 us
    pallas_call x2, Pallas kernels, sort_blocks(): pl.pallas_call(functools.partial(sort_kernel, runs, n), out_shape=tuple(s...  19 us
    ppermute x16, waiting for transfers between devices, exchange(): return lax.ppermute(x, axis, pairs + [(j, i) for i, j in pairs])  17.4 us
    all_to_all x1, blocking collectives, per_device(): everyone = lax.all_to_all(moments, ('gx', 'gy'), 0, 0)  16.7 us
    pallas_call x2, Pallas kernels, interp(): pl.pallas_call(functools.partial(interp_kernel, len(arrays), bases, unrol...  14.7 us
    pallas_call x2, Pallas kernels, deposit(): pl.pallas_call(functools.partial(deposit_kernel, len(arrays), bases, unro...  14.2 us
    pallas_call x1, Pallas kernels, place_forces(): pl.pallas_call(functools.partial(place_kernel, len(backs), GROUPS), out_s...  5.63 us
    pallas_call x1, Pallas kernels, inverse(): pl.pallas_call(inverse_kernel, out_shape=(shape, shape, TOKEN), in_specs=...  3.47 us
  transfers between devices with their start and end apart: 16, of which 7 were waited for; matrix products, arithmetic and copies ran while one was open for 1% of the time, Pallas kernels for 17%

profile of v4, /device:TPU:10, one launch (start us, length us, event | category | flops | bytes accessed | tf_op | source)
XLA Modules:
  0.0 137.8 jit_solution(8065822596302558129)
XLA Ops:
  0.6 9.5 %sort_blocks.2 = (f32[456,128]{1,0:T(8,128)}, f32[456,128]{1,0:T(8,128)}, f32[304,128]{1,0:T(8,128)}, s32[24,8,128]{2,1,0:T(8,128)}) custom-call(f32[5,1,128,3072]{3,2,1,0:T(8,128)} %data_ref.3, s32[2,1,128,3072]{3,2,1,0:T(8,128)} %cells_ref.3, s32[1,128]{1,0:T(1,128)} %counts_ref.3), custom_call_target="tpu_custom_call" | custom-call | tf_op jit(solution)/shard_map/sort_blocks/pallas_call | solution.py:201
  10.1 4.0 %collective-permute-start = (f32[456,128]{1,0:T(8,128)}, f32[456,128]{1,0:T(8,128)S(1)}, u32[]{:S(2)}, u32[]{:S(2)}) collective-permute-start(f32[456,128]{1,0:T(8,128)} %get-tuple-element.32), channel_id=1, source_target_pairs={{0,16},{8,24},{32,48},{40,56},{64,80},{72,88},{96,112},{104,120},{... | collective-permute-start | bytes 700424 | tf_op jit(solution)/shard_map/ppermute | solution.py:857
  14.1 2.0 %collective-permute-start.1 = (f32[456,128]{1,0:T(8,128)}, f32[456,128]{1,0:T(8,128)S(1)}, u32[]{:S(2)}, u32[]{:S(2)}) collective-permute-start(f32[456,128]{1,0:T(8,128)} %get-tuple-element.33), channel_id=1, source_target_pairs={{16,32},{24,40},{48,64},{56,72},{80,96},{88,104},{32,16},{40,24},{... | collective-permute-start | bytes 700424 | tf_op jit(solution)/shard_map/ppermute | solution.py:857
  16.1 9.5 %sort_blocks.3 = (f32[456,128]{1,0:T(8,128)}, f32[456,128]{1,0:T(8,128)}, f32[152,128]{1,0:T(8,128)}, s32[24,8,128]{2,1,0:T(8,128)}) custom-call(f32[5,1,128,3072]{3,2,1,0:T(8,128)} %data_ref.3, s32[2,1,128,3072]{3,2,1,0:T(8,128)} %cells_ref.3, s32[1,128]{1,0:T(1,128)} %counts_ref.3), custom_call_target="tpu_custom_call" | custom-call | tf_op jit(solution)/shard_map/sort_blocks/pallas_call | solution.py:201
  25.6 1.6 %collective-permute-start.2 = (f32[456,128]{1,0:T(8,128)}, f32[456,128]{1,0:T(8,128)S(1)}, u32[]{:S(2)}, u32[]{:S(2)}) collective-permute-start(f32[456,128]{1,0:T(8,128)} %get-tuple-element.35), channel_id=1, source_target_pairs={{0,8},{16,24},{32,40},{48,56},{64,72},{80,88},{96,104},{112,120},{... | collective-permute-start | bytes 700424 | tf_op jit(solution)/shard_map/ppermute | solution.py:857
  27.2 5.3 %collective-permute-start.3 = (f32[456,128]{1,0:T(8,128)}, f32[456,128]{1,0:T(8,128)S(1)}, u32[]{:S(2)}, u32[]{:S(2)}) collective-permute-start(f32[456,128]{1,0:T(8,128)} %get-tuple-element.36), channel_id=1, source_target_pairs={{8,16},{24,32},{40,48},{56,64},{72,80},{88,96},{104,112},{16,8},{3... | collective-permute-start | bytes 700424 | tf_op jit(solution)/shard_map/ppermute | solution.py:857
  32.7 0.9 constant_dynamic-update-slice_fusion
  33.6 4.4 %collective-permute-done.3 = f32[456,128]{1,0:T(8,128)S(1)} collective-permute-done((f32[456,128]{1,0:T(8,128)}, f32[456,128]{1,0:T(8,128)S(1)}, u32[]{:S(2)}, u32[]{:S(2)}) %collective-permute-start.3) | collective-permute-done | bytes 233504 | tf_op jit(solution)/shard_map/ppermute | solution.py:857
  38.1 1.9 %collective-permute-start.5 = (f32[760,128]{1,0:T(8,128)S(1)}, f32[760,128]{1,0:T(8,128)S(1)}, u32[]{:S(2)}, u32[]{:S(2)}) collective-permute-start(f32[760,128]{1,0:T(8,128)S(1)} %get-tuple-element.62), channel_id=1, source_target_pairs={{1,2},{3,4},{5,6},{2,1},{4,3},{6,5},{9,10},{11,12},{13,14},{10,9},... | collective-permute-start | bytes 1167368 | tf_op jit(solution)/shard_map/ppermute | solution.py:857
  40.0 1.8 %collective-permute-start.4 = (f32[760,128]{1,0:T(8,128)S(1)}, f32[760,128]{1,0:T(8,128)S(1)}, u32[]{:S(2)}, u32[]{:S(2)}) collective-permute-start(f32[760,128]{1,0:T(8,128)S(1)} %get-tuple-element.63), channel_id=1, source_target_pairs={{0,1},{2,3},{4,5},{6,7},{1,0},{3,2},{5,4},{7,6},{8,9},{10,11},{12,... | collective-permute-start | bytes 1167368 | tf_op jit(solution)/shard_map/ppermute | solution.py:857
  41.8 4.7 %deposit.2.refs_2_ = f32[5,512,128]{2,1,0:T(8,128)S(1)} custom-call(f32[760,128]{1,0:T(8,128)S(1)} %get-tuple-element.64.refs_0_), custom_call_target="tpu_custom_call" | custom-call | flops 5000000000 | bytes 15000000 | tf_op jit(solution)/shard_map/deposit/pallas_call | solution.py:333
  46.6 0.6 collective-permute-done.5.refs_1_
  47.2 9.4 %deposit.3 = (bf16[32,48,256]{2,1,0:T(8,128)(2,1)S(1)}, f32[2,8,64,128]{3,2,1,0:T(8,128)S(1)}, f32[9,64,128]{2,1,0:T(8,128)S(1)}, f32[9,64,128]{2,1,0:T(8,128)S(1)}, f32[8,128]{1,0:T(8,128)S(1)}) custom-call(f32[760,128]{1,0:T(8,128)S(1)} %collective-permute-done.4.refs_0_, f32[760,128]{1,0:T(8,128)S(1)} %collective-permute-done.5.refs_1_, ...), custom_call_target="tpu_custom_call" | custom-call | flops 10000000000 | bytes 30000000 | tf_op jit(solution)/shard_map/deposit/pallas_call | solution.py:333
  56.6 0.8 collective-permute-start.6
  57.4 4.9 %collective-permute-start.7 = (f32[9,64,128]{2,1,0:T(8,128)S(1)}, f32[9,64,128]{2,1,0:T(8,128)S(1)}, u32[]{:S(2)}, u32[]{:S(2)}) collective-permute-start(f32[9,64,128]{2,1,0:T(8,128)S(1)} %get-tuple-element.40.sent_1), channel_id=1, source_target_pairs={{8,16},{24,32},{40,48},{56,64},{72,80},{88,96},{104,112},{16,8},{3... | collective-permute-start | bytes 884744 | tf_op jit(solution)/shard_map/ppermute | solution.py:857
  62.3 3.5 %inverse.1 = (s32[24,8,128]{2,1,0:T(8,128)S(1)}, s32[24,8,128]{2,1,0:T(8,128)S(1)}, f32[8,128]{1,0:T(8,128)S(1)}) custom-call(s32[24,8,128]{2,1,0:T(8,128)S(1)} %copy-done.1, s32[24,8,128]{2,1,0:T(8,128)S(1)} %copy-done.2, f32[8,128]{1,0:T(8,128)S(1)} %get-tuple-element.43.after), custom_call_target="tpu_custom_call" | custom-call | flops 1000000000 | bytes 20000000 | tf_op jit(solution)/shard_map/inverse/pallas_call | solution.py:186
  65.8 4.3 %collective-permute-done.7.got_1 = f32[9,64,128]{2,1,0:T(8,128)S(1)} collective-permute-done((f32[9,64,128]{2,1,0:T(8,128)S(1)}, f32[9,64,128]{2,1,0:T(8,128)S(1)}, u32[]{:S(2)}, u32[]{:S(2)}) %collective-permute-start.7) | collective-permute-done | bytes 294944 | tf_op jit(solution)/shard_map/ppermute | solution.py:857
  70.5 1.9 %collective-permute-start.9 = (f32[3,64,128]{2,1,0:T(8,128)S(1)}, f32[3,64,128]{2,1,0:T(8,128)S(1)}, u32[]{:S(2)}, u32[]{:S(2)}) collective-permute-start(f32[3,64,128]{2,1,0:T(8,128)S(1)} %pack_edges.1.packed), channel_id=1, source_target_pairs={{1,2},{3,4},{5,6},{2,1},{4,3},{6,5},{9,10},{11,12},{13,14},{10,9},... | collective-permute-start | bytes 294920 | tf_op jit(solution)/shard_map/ppermute | solution.py:857
  72.4 1.6 %collective-permute-start.8 = (f32[3,64,128]{2,1,0:T(8,128)S(1)}, f32[3,64,128]{2,1,0:T(8,128)S(1)}, u32[]{:S(2)}, u32[]{:S(2)}) collective-permute-start(f32[3,64,128]{2,1,0:T(8,128)S(1)} %pack_edges.1.packed), channel_id=1, source_target_pairs={{0,1},{2,3},{4,5},{6,7},{1,0},{3,2},{5,4},{7,6},{8,9},{10,11},{12,... | collective-permute-start | bytes 294920 | tf_op jit(solution)/shard_map/ppermute | solution.py:857
  74.0 2.4 %collective-permute-done.9.edge_1 = f32[3,64,128]{2,1,0:T(8,128)S(1)} collective-permute-done((f32[3,64,128]{2,1,0:T(8,128)S(1)}, f32[3,64,128]{2,1,0:T(8,128)S(1)}, u32[]{:S(2)}, u32[]{:S(2)}) %collective-permute-start.9) | collective-permute-done | bytes 98336 | tf_op jit(solution)/shard_map/ppermute | solution.py:857
  76.4 3.0 %sweeps.1 = (f32[3,10,64,128]{3,2,1,0:T(8,128)S(1)}, f32[3,8,64,128]{3,2,1,0:T(8,128)S(1)}, f32[128,1,128]{2,1,0:T(1,128)S(1)}) custom-call(f32[2,8,64,128]{3,2,1,0:T(8,128)S(1)} %get-tuple-element.38.own, f32[9,64,128]{2,1,0:T(8,128)S(1)} %get-tuple-element.39.sent_0, f32[9,64,128]{2,1,0:T(8,128)S(1)} %get-tuple-element.40.sent_1, ...), custom_call_target="tpu_custom_call" | custom-call | tf_op jit(solution)/shard_map/sweeps/pallas_call | solution.py:676
  79.5 16.7 %all_to_all.5.all_moments = f32[128,1,128]{2,1,0:T(1,128)S(1)} all-to-all(f32[128,1,128]{2,1,0:T(1,128)S(1)} %get-tuple-element.45), channel_id=1, replica_groups=mesh['gx'=16,'gy'=8] {'gx','gy'}, dimensions={0} | all-to-all | bytes 131072 | tf_op jit(solution)/shard_map/all_to_all | solution.py:879
  96.2 1.3 gradients.1
  97.4 9.5 %interp.2 = (f32[360,128]{1,0:T(8,128)S(1)}, f32[360,128]{1,0:T(8,128)S(1)}, f32[8,128]{1,0:T(8,128)S(1)}) custom-call(f32[760,128]{1,0:T(8,128)S(1)} %collective-permute-done.4.refs_0_, f32[760,128]{1,0:T(8,128)S(1)} %collective-permute-done.5.refs_1_, bf16[32,48,256]{2,1,0:T(8,128)(2,1)S(1)} %get-tuple-element.49.refs_2_.refs_1_, ...), custom_call_target="tpu_custom_call" | custom-call | flops 10000000000 | bytes 30000000 | tf_op jit(solution)/shard_map/interp/pallas_call | solution.py:415
  107.0 3.6 %collective-permute-start.11 = (f32[360,128]{1,0:T(8,128)S(1)}, f32[360,128]{1,0:T(8,128)S(1)}, u32[]{:S(2)}, u32[]{:S(2)}) collective-permute-start(f32[360,128]{1,0:T(8,128)S(1)} %get-tuple-element.54), channel_id=1, source_target_pairs={{1,2},{3,4},{5,6},{2,1},{4,3},{6,5},{9,10},{11,12},{13,14},{10,9},... | collective-permute-start | bytes 552968 | tf_op jit(solution)/shard_map/ppermute | solution.py:857
  110.6 5.3 %interp.3 = (f32[360,128]{1,0:T(8,128)S(1)}, f32[8,128]{1,0:T(8,128)}) custom-call(f32[760,128]{1,0:T(8,128)S(1)} %get-tuple-element.64.refs_0_, bf16[32,48,256]{2,1,0:T(8,128)(2,1)S(1)} %get-tuple-element.49.refs_2_.refs_1_, bf16[32,48,256]{2,1,0:T(8,128)(2,1)S(1)} %get-tuple-element.50.refs_3_.refs_2_, f32[8,128]{1,0:T(8,128)S(1)} %get-tuple-element.52.refs_3_), custom_call_target="tpu_custom_call" | custom-call | flops 5000000000 | bytes 15000000 | tf_op jit(solution)/shard_map/interp/pallas_call | solution.py:415
  116.0 1.5 %collective-permute-start.12 = (f32[216,128]{1,0:T(8,128)S(1)}, f32[216,128]{1,0:T(8,128)S(1)}, u32[]{:S(2)}, u32[]{:S(2)}) collective-permute-start(f32[216,128]{1,0:T(8,128)S(1)} %get-tuple-element.55), channel_id=1, source_target_pairs={{0,16},{8,24},{32,48},{40,56},{64,80},{72,88},{96,112},{104,120},{... | collective-permute-start | bytes 331784 | tf_op jit(solution)/shard_map/ppermute | solution.py:857
  117.5 4.8 %collective-permute-start.13 = (f32[216,128]{1,0:T(8,128)S(1)}, f32[216,128]{1,0:T(8,128)S(1)}, u32[]{:S(2)}, u32[]{:S(2)}) collective-permute-start(f32[216,128]{1,0:T(8,128)S(1)} %get-tuple-element.56), channel_id=1, source_target_pairs={{16,32},{24,40},{48,64},{56,72},{80,96},{88,104},{32,16},{40,24},{... | collective-permute-start | bytes 331784 | tf_op jit(solution)/shard_map/ppermute | solution.py:857
  122.3 0.9 collective-permute-start.14
  123.3 3.1 %collective-permute-start.15 = (f32[216,128]{1,0:T(8,128)S(1)}, f32[216,128]{1,0:T(8,128)S(1)}, u32[]{:S(2)}, u32[]{:S(2)}) collective-permute-start(f32[216,128]{1,0:T(8,128)S(1)} %get-tuple-element.59), channel_id=1, source_target_pairs={{8,16},{24,32},{40,48},{56,64},{72,80},{88,96},{104,112},{16,8},{3... | collective-permute-start | bytes 331784 | tf_op jit(solution)/shard_map/ppermute | solution.py:857
  127.2 4.8 %collective-permute-done.15.refs_4_ = f32[216,128]{1,0:T(8,128)S(1)} collective-permute-done((f32[216,128]{1,0:T(8,128)S(1)}, f32[216,128]{1,0:T(8,128)S(1)}, u32[]{:S(2)}, u32[]{:S(2)}) %collective-permute-start.15) | collective-permute-done | bytes 110624 | tf_op jit(solution)/shard_map/ppermute | solution.py:857
  132.0 5.6 %place_forces.1 = f32[3,1,128,3072]{3,2,1,0:T(8,128)} custom-call(f32[216,128]{1,0:T(8,128)S(1)} %collective-permute-done.12.refs_0_, f32[216,128]{1,0:T(8,128)S(1)} %collective-permute-done.13.refs_1_, f32[216,128]{1,0:T(8,128)S(1)} %get-tuple-element.57.refs_2_, f32[216,128]{1,0:T(8,128)S(1)} %collective-permute-done.14.refs_3_, ...), custom_call_target="tpu_custom_call" | custom-call | tf_op jit(solution)/shard_map/place_forces/pallas_call | solution.py:836
  (28 shorter events, 1.4 us)
Async XLA Ops:
  10.1 22.5 %collective-permute-start = (f32[456,128]{1,0:T(8,128)}, f32[456,128]{1,0:T(8,128)S(1)}, u32[]{:S(2)}, u32[]{:S(2)}) collective-permute-start(f32[456,128]{1,0:T(8,128)} %get-tuple-element.32), channel_id=1, source_target_pairs={{0,16},{8,24},{32,48},{40,56},{64,80},{72,88},{96,112},{104,120},{... | collective-permute-start | bytes 700424 | tf_op jit(solution)/shard_map/ppermute | solution.py:857
  14.1 18.6 %copy-start.3 = (f32[304,128]{1,0:T(8,128)S(1)}, f32[304,128]{1,0:T(8,128)}, u32[]{:S(2)}) copy-start(f32[304,128]{1,0:T(8,128)} %get-tuple-element.37) | copy-start | bytes 466948
  14.1 18.6 %collective-permute-start.1 = (f32[456,128]{1,0:T(8,128)}, f32[456,128]{1,0:T(8,128)S(1)}, u32[]{:S(2)}, u32[]{:S(2)}) collective-permute-start(f32[456,128]{1,0:T(8,128)} %get-tuple-element.33), channel_id=1, source_target_pairs={{16,32},{24,40},{48,64},{56,72},{80,96},{88,104},{32,16},{40,24},{... | collective-permute-start | bytes 700424 | tf_op jit(solution)/shard_map/ppermute | solution.py:857
  25.6 8.0 %collective-permute-start.2 = (f32[456,128]{1,0:T(8,128)}, f32[456,128]{1,0:T(8,128)S(1)}, u32[]{:S(2)}, u32[]{:S(2)}) collective-permute-start(f32[456,128]{1,0:T(8,128)} %get-tuple-element.35), channel_id=1, source_target_pairs={{0,8},{16,24},{32,40},{48,56},{64,72},{80,88},{96,104},{112,120},{... | collective-permute-start | bytes 700424 | tf_op jit(solution)/shard_map/ppermute | solution.py:857
  27.2 10.8 %collective-permute-start.3 = (f32[456,128]{1,0:T(8,128)}, f32[456,128]{1,0:T(8,128)S(1)}, u32[]{:S(2)}, u32[]{:S(2)}) collective-permute-start(f32[456,128]{1,0:T(8,128)} %get-tuple-element.36), channel_id=1, source_target_pairs={{8,16},{24,32},{40,48},{56,64},{72,80},{88,96},{104,112},{16,8},{3... | collective-permute-start | bytes 700424 | tf_op jit(solution)/shard_map/ppermute | solution.py:857
  38.1 9.1 %collective-permute-start.5 = (f32[760,128]{1,0:T(8,128)S(1)}, f32[760,128]{1,0:T(8,128)S(1)}, u32[]{:S(2)}, u32[]{:S(2)}) collective-permute-start(f32[760,128]{1,0:T(8,128)S(1)} %get-tuple-element.62), channel_id=1, source_target_pairs={{1,2},{3,4},{5,6},{2,1},{4,3},{6,5},{9,10},{11,12},{13,14},{10,9},... | collective-permute-start | bytes 1167368 | tf_op jit(solution)/shard_map/ppermute | solution.py:857
  40.0 7.1 %collective-permute-start.4 = (f32[760,128]{1,0:T(8,128)S(1)}, f32[760,128]{1,0:T(8,128)S(1)}, u32[]{:S(2)}, u32[]{:S(2)}) collective-permute-start(f32[760,128]{1,0:T(8,128)S(1)} %get-tuple-element.63), channel_id=1, source_target_pairs={{0,1},{2,3},{4,5},{6,7},{1,0},{3,2},{5,4},{7,6},{8,9},{10,11},{12,... | collective-permute-start | bytes 1167368 | tf_op jit(solution)/shard_map/ppermute | solution.py:857
  41.8 5.4 %copy-start = (f32[3,64,8,128]{3,2,1,0:T(8,128)S(1)}, f32[3,64,8,128]{3,2,1,0:T(8,128)}, u32[]{:S(2)}) copy-start(f32[3,64,8,128]{3,2,1,0:T(8,128)} %param.7) | copy-start | bytes 2359300
  47.2 15.1 %copy-start.1 = (s32[24,8,128]{2,1,0:T(8,128)S(1)}, s32[24,8,128]{2,1,0:T(8,128)}, u32[]{:S(2)}) copy-start(s32[24,8,128]{2,1,0:T(8,128)} %get-tuple-element.41.keys_a) | copy-start | bytes 294916
  47.2 15.1 %copy-start.2 = (s32[24,8,128]{2,1,0:T(8,128)S(1)}, s32[24,8,128]{2,1,0:T(8,128)}, u32[]{:S(2)}) copy-start(s32[24,8,128]{2,1,0:T(8,128)} %get-tuple-element.42.keys_b) | copy-start | bytes 294916
  56.6 9.2 %collective-permute-start.6 = (f32[9,64,128]{2,1,0:T(8,128)S(1)}, f32[9,64,128]{2,1,0:T(8,128)S(1)}, u32[]{:S(2)}, u32[]{:S(2)}) collective-permute-start(f32[9,64,128]{2,1,0:T(8,128)S(1)} %get-tuple-element.39.sent_0), channel_id=1, source_target_pairs={{0,8},{16,24},{32,40},{48,56},{64,72},{80,88},{96,104},{112,120},{... | collective-permute-start | bytes 884744 | tf_op jit(solution)/shard_map/ppermute | solution.py:857
  57.4 12.7 %collective-permute-start.7 = (f32[9,64,128]{2,1,0:T(8,128)S(1)}, f32[9,64,128]{2,1,0:T(8,128)S(1)}, u32[]{:S(2)}, u32[]{:S(2)}) collective-permute-start(f32[9,64,128]{2,1,0:T(8,128)S(1)} %get-tuple-element.40.sent_1), channel_id=1, source_target_pairs={{8,16},{24,32},{40,48},{56,64},{72,80},{88,96},{104,112},{16,8},{3... | collective-permute-start | bytes 884744 | tf_op jit(solution)/shard_map/ppermute | solution.py:857
  70.5 5.9 %collective-permute-start.9 = (f32[3,64,128]{2,1,0:T(8,128)S(1)}, f32[3,64,128]{2,1,0:T(8,128)S(1)}, u32[]{:S(2)}, u32[]{:S(2)}) collective-permute-start(f32[3,64,128]{2,1,0:T(8,128)S(1)} %pack_edges.1.packed), channel_id=1, source_target_pairs={{1,2},{3,4},{5,6},{2,1},{4,3},{6,5},{9,10},{11,12},{13,14},{10,9},... | collective-permute-start | bytes 294920 | tf_op jit(solution)/shard_map/ppermute | solution.py:857
  72.4 4.0 %collective-permute-start.8 = (f32[3,64,128]{2,1,0:T(8,128)S(1)}, f32[3,64,128]{2,1,0:T(8,128)S(1)}, u32[]{:S(2)}, u32[]{:S(2)}) collective-permute-start(f32[3,64,128]{2,1,0:T(8,128)S(1)} %pack_edges.1.packed), channel_id=1, source_target_pairs={{0,1},{2,3},{4,5},{6,7},{1,0},{3,2},{5,4},{7,6},{8,9},{10,11},{12,... | collective-permute-start | bytes 294920 | tf_op jit(solution)/shard_map/ppermute | solution.py:857
  106.9 9.0 %collective-permute-start.10 = (f32[360,128]{1,0:T(8,128)S(1)}, f32[360,128]{1,0:T(8,128)S(1)}, u32[]{:S(2)}, u32[]{:S(2)}) collective-permute-start(f32[360,128]{1,0:T(8,128)S(1)} %get-tuple-element.51), channel_id=1, source_target_pairs={{0,1},{2,3},{4,5},{6,7},{1,0},{3,2},{5,4},{7,6},{8,9},{10,11},{12,... | collective-permute-start | bytes 552968 | tf_op jit(solution)/shard_map/ppermute | solution.py:857
  107.0 8.9 %collective-permute-start.11 = (f32[360,128]{1,0:T(8,128)S(1)}, f32[360,128]{1,0:T(8,128)S(1)}, u32[]{:S(2)}, u32[]{:S(2)}) collective-permute-start(f32[360,128]{1,0:T(8,128)S(1)} %get-tuple-element.54), channel_id=1, source_target_pairs={{1,2},{3,4},{5,6},{2,1},{4,3},{6,5},{9,10},{11,12},{13,14},{10,9},... | collective-permute-start | bytes 552968 | tf_op jit(solution)/shard_map/ppermute | solution.py:857
  116.0 10.4 %collective-permute-start.12 = (f32[216,128]{1,0:T(8,128)S(1)}, f32[216,128]{1,0:T(8,128)S(1)}, u32[]{:S(2)}, u32[]{:S(2)}) collective-permute-start(f32[216,128]{1,0:T(8,128)S(1)} %get-tuple-element.55), channel_id=1, source_target_pairs={{0,16},{8,24},{32,48},{40,56},{64,80},{72,88},{96,112},{104,120},{... | collective-permute-start | bytes 331784 | tf_op jit(solution)/shard_map/ppermute | solution.py:857
  117.5 9.1 %collective-permute-start.13 = (f32[216,128]{1,0:T(8,128)S(1)}, f32[216,128]{1,0:T(8,128)S(1)}, u32[]{:S(2)}, u32[]{:S(2)}) collective-permute-start(f32[216,128]{1,0:T(8,128)S(1)} %get-tuple-element.56), channel_id=1, source_target_pairs={{16,32},{24,40},{48,64},{56,72},{80,96},{88,104},{32,16},{40,24},{... | collective-permute-start | bytes 331784 | tf_op jit(solution)/shard_map/ppermute | solution.py:857
  122.3 4.8 %collective-permute-start.14 = (f32[216,128]{1,0:T(8,128)S(1)}, f32[216,128]{1,0:T(8,128)S(1)}, u32[]{:S(2)}, u32[]{:S(2)}) collective-permute-start(f32[216,128]{1,0:T(8,128)S(1)} %get-tuple-element.58), channel_id=1, source_target_pairs={{0,8},{16,24},{32,40},{48,56},{64,72},{80,88},{96,104},{112,120},{... | collective-permute-start | bytes 331784 | tf_op jit(solution)/shard_map/ppermute | solution.py:857
  123.3 8.7 %collective-permute-start.15 = (f32[216,128]{1,0:T(8,128)S(1)}, f32[216,128]{1,0:T(8,128)S(1)}, u32[]{:S(2)}, u32[]{:S(2)}) collective-permute-start(f32[216,128]{1,0:T(8,128)S(1)} %get-tuple-element.59), channel_id=1, source_target_pairs={{8,16},{24,32},{40,48},{56,64},{72,80},{88,96},{104,112},{16,8},{3... | collective-permute-start | bytes 331784 | tf_op jit(solution)/shard_map/ppermute | solution.py:857

commit v5 on v4

--- a/solution.py
+++ b/solution.py
@@ -154,7 +154,7 @@
         for f in range(5):
             out_s[pl.ds(f * CH + c, 8, stride=BR), :] = acc[f]
         out_s[pl.ds(5 * CH + c, 8, stride=BR), :] = (k >> 12).astype(f32)
-    unrolled(CH, 4, chunk)
+    unrolled(CH, 12, chunk)
     low = lane < 64
     bound = jnp.where(low, lane, lane - 63) * SPAN
     total = jnp.zeros((8, 128), i32)
@@ -211,7 +211,7 @@
             pltpu.VMEM((8 * BR, 128), f32),
             pltpu.SemaphoreType.DMA((2 * n,)),
         ],
-        compiler_params=pltpu.CompilerParams(vmem_limit_bytes=56 * 1024 * 1024),
+        compiler_params=pltpu.CompilerParams(vmem_limit_bytes=50 * 1024 * 1024),
         name="sort_blocks",
     )(data, cells, counts)
 
@@ -803,7 +803,7 @@
                     acc[f] = jnp.where(here, got, acc[f])
             for f in range(3):
                 found[g, f, c] = acc[f]
-        unrolled(CH, 8, chunk)
+        unrolled(CH, 24, chunk)
     row = lax.broadcasted_iota(i32, (8, 128), 0)
     for dx in (-2, -1, 0, 1, 2):
         pieces = [(g, run) for g, runs in enumerate(groups) for run in runs if run[0] == dx]
@@ -871,14 +871,14 @@
     ]
     bases = tuple(range(0, 5 * BR, BR))
     acc = deposit([mine], bases, 8)
-    table, own, send_0, send_1, token = deposit(sides, bases, 4, acc, fluid_velocity.reshape(3, 512, 128))
+    table, own, send_0, send_1, token = deposit(sides, bases, 8, acc, fluid_velocity.reshape(3, 512, 128))
     rows = (own, send_0, send_1, exchange(send_0, "gx", 1, 0), exchange(send_1, "gx", 1, 1))
     *pos, token = inverse(keys_a, keys_b, token)
     packed = pack_edges(rows, token)
     core, beside, moments = sweeps(rows, packed, exchange(packed, "gy", 1, 0), exchange(packed, "gy", 1, 1))
     everyone = lax.all_to_all(moments, ("gx", "gy"), 0, 0)
     pressure, slopes = gradients(everyone, core, beside)
-    far_0, far_1, token = interp(sides, bases, table, slopes, 4, token, 2)
+    far_0, far_1, token = interp(sides, bases, table, slopes, 8, token, 2)
     back = [exchange(far_0, "gy", 1, 0), exchange(far_1, "gy", 1, 1)]
     near, _ = interp([mine], bases, table, slopes, 8, token, 1)
     blocks = list(arrange(back[0], near, back[1]))

time: 138 us -> 135 us (0.978)
  Pallas kernels: 61.7 us -> 56 us
  local copies, waits for them, and re-layouts: 0.99 us -> 2.63 us
    pallas_call x2, Pallas kernels: 19 us -> 15.1 us  [sort_blocks(): pl.pallas_call(functools.partial(sort_kernel, runs, n), out_shape=tuple(s...]
    unnamed x13 -> x11, local copies, waits for them, and re-layouts: 0.98 us -> 2.62 us
  transfers between devices with their start and end apart: 16 -> 16, of which waited for: 7 -> 8; matrix products, arithmetic and copies ran while one was open for 1% -> 0% of each run, Pallas kernels for 17% -> 16%
where the time goes in v5:
time: 135 us
  Pallas kernels  56 us (41%)
  starting transfers between devices  40 us (30%)
  waiting for transfers between devices  18.3 us (14%)
  blocking collectives  16.7 us (12%)
  local copies, waits for them, and re-layouts  2.63 us (2%)
    ppermute x16, starting transfers between devices, exchange(): return lax.ppermute(x, axis, pairs + [(j, i) for i, j in pairs])  40 us
    ppermute x16, waiting for transfers between devices, exchange(): return lax.ppermute(x, axis, pairs + [(j, i) for i, j in pairs])  18.3 us
    all_to_all x1, blocking collectives, per_device(): everyone = lax.all_to_all(moments, ('gx', 'gy'), 0, 0)  16.7 us
    pallas_call x2, Pallas kernels, sort_blocks(): pl.pallas_call(functools.partial(sort_kernel, runs, n), out_shape=tuple(s...  15.1 us
    pallas_call x2, Pallas kernels, interp(): pl.pallas_call(functools.partial(interp_kernel, len(arrays), bases, unrol...  14.1 us
    pallas_call x2, Pallas kernels, deposit(): pl.pallas_call(functools.partial(deposit_kernel, len(arrays), bases, unro...  13.5 us
    pallas_call x1, Pallas kernels, place_forces(): pl.pallas_call(functools.partial(place_kernel, len(backs), GROUPS), out_s...  5.16 us
    pallas_call x1, Pallas kernels, inverse(): pl.pallas_call(inverse_kernel, out_shape=(shape, shape, TOKEN), in_specs=...  3.47 us
  transfers between devices with their start and end apart: 16, of which 8 were waited for; matrix products, arithmetic and copies ran while one was open for 0% of the time, Pallas kernels for 16%

profile of v5, /device:TPU:10, one launch (start us, length us, event | category | flops | bytes accessed | tf_op | source)
XLA Modules:
  0.0 134.8 jit_solution(3148991449583569896)
XLA Ops:
  0.6 1.9 %copy-done = s32[2,1,128,3072]{3,2,1,0:T(8,128)S(1)} copy-done((s32[2,1,128,3072]{3,2,1,0:T(8,128)S(1)}, s32[2,1,128,3072]{3,2,1,0:T(8,128)}, u32[]{:S(2)}) %copy-start) | copy-done | bytes 3145752
  2.5 0.7 copy-done.1
  3.2 7.6 %sort_blocks.2 = (f32[456,128]{1,0:T(8,128)S(1)}, f32[456,128]{1,0:T(8,128)S(1)}, f32[304,128]{1,0:T(8,128)S(1)}, s32[24,8,128]{2,1,0:T(8,128)S(1)}) custom-call(f32[5,1,128,3072]{3,2,1,0:T(8,128)} %data_ref.3, s32[2,1,128,3072]{3,2,1,0:T(8,128)S(1)} %copy-done, s32[1,128]{1,0:T(1,128)S(1)} %copy-done.1), custom_call_target="tpu_custom_call" | custom-call | tf_op jit(solution)/shard_map/sort_blocks/pallas_call | solution.py:201
  10.7 4.0 %collective-permute-start = (f32[456,128]{1,0:T(8,128)S(1)}, f32[456,128]{1,0:T(8,128)S(1)}, u32[]{:S(2)}, u32[]{:S(2)}) collective-permute-start(f32[456,128]{1,0:T(8,128)S(1)} %get-tuple-element.32), channel_id=1, source_target_pairs={{0,16},{8,24},{32,48},{40,56},{64,80},{72,88},{96,112},{104,120},{... | collective-permute-start | bytes 700424 | tf_op jit(solution)/shard_map/ppermute | solution.py:857
  14.7 1.9 %collective-permute-start.1 = (f32[456,128]{1,0:T(8,128)S(1)}, f32[456,128]{1,0:T(8,128)S(1)}, u32[]{:S(2)}, u32[]{:S(2)}) collective-permute-start(f32[456,128]{1,0:T(8,128)S(1)} %get-tuple-element.33), channel_id=1, source_target_pairs={{16,32},{24,40},{48,64},{56,72},{80,96},{88,104},{32,16},{40,24},{... | collective-permute-start | bytes 700424 | tf_op jit(solution)/shard_map/ppermute | solution.py:857
  16.6 7.6 %sort_blocks.3 = (f32[456,128]{1,0:T(8,128)S(1)}, f32[456,128]{1,0:T(8,128)S(1)}, f32[152,128]{1,0:T(8,128)S(1)}, s32[24,8,128]{2,1,0:T(8,128)S(1)}) custom-call(f32[5,1,128,3072]{3,2,1,0:T(8,128)} %data_ref.3, s32[2,1,128,3072]{3,2,1,0:T(8,128)S(1)} %copy-done, s32[1,128]{1,0:T(1,128)S(1)} %copy-done.1), custom_call_target="tpu_custom_call" | custom-call | tf_op jit(solution)/shard_map/sort_blocks/pallas_call | solution.py:201
  24.2 1.6 %collective-permute-start.2 = (f32[456,128]{1,0:T(8,128)S(1)}, f32[456,128]{1,0:T(8,128)S(1)}, u32[]{:S(2)}, u32[]{:S(2)}) collective-permute-start(f32[456,128]{1,0:T(8,128)S(1)} %get-tuple-element.35), channel_id=1, source_target_pairs={{0,8},{16,24},{32,40},{48,56},{64,72},{80,88},{96,104},{112,120},{... | collective-permute-start | bytes 700424 | tf_op jit(solution)/shard_map/ppermute | solution.py:857
  25.8 5.3 %collective-permute-start.3 = (f32[456,128]{1,0:T(8,128)S(1)}, f32[456,128]{1,0:T(8,128)S(1)}, u32[]{:S(2)}, u32[]{:S(2)}) collective-permute-start(f32[456,128]{1,0:T(8,128)S(1)} %get-tuple-element.36), channel_id=1, source_target_pairs={{8,16},{24,32},{40,48},{56,64},{72,80},{88,96},{104,112},{16,8},{3... | collective-permute-start | bytes 700424 | tf_op jit(solution)/shard_map/ppermute | solution.py:857
  31.4 4.9 %collective-permute-done.3 = f32[456,128]{1,0:T(8,128)S(1)} collective-permute-done((f32[456,128]{1,0:T(8,128)S(1)}, f32[456,128]{1,0:T(8,128)S(1)}, u32[]{:S(2)}, u32[]{:S(2)}) %collective-permute-start.3) | collective-permute-done | bytes 233504 | tf_op jit(solution)/shard_map/ppermute | solution.py:857
  36.5 1.9 %collective-permute-start.5 = (f32[760,128]{1,0:T(8,128)S(1)}, f32[760,128]{1,0:T(8,128)S(1)}, u32[]{:S(2)}, u32[]{:S(2)}) collective-permute-start(f32[760,128]{1,0:T(8,128)S(1)} %get-tuple-element.62), channel_id=1, source_target_pairs={{1,2},{3,4},{5,6},{2,1},{4,3},{6,5},{9,10},{11,12},{13,14},{10,9},... | collective-permute-start | bytes 1167368 | tf_op jit(solution)/shard_map/ppermute | solution.py:857
  38.4 1.8 %collective-permute-start.4 = (f32[760,128]{1,0:T(8,128)S(1)}, f32[760,128]{1,0:T(8,128)S(1)}, u32[]{:S(2)}, u32[]{:S(2)}) collective-permute-start(f32[760,128]{1,0:T(8,128)S(1)} %get-tuple-element.63), channel_id=1, source_target_pairs={{0,1},{2,3},{4,5},{6,7},{1,0},{3,2},{5,4},{7,6},{8,9},{10,11},{12,... | collective-permute-start | bytes 1167368 | tf_op jit(solution)/shard_map/ppermute | solution.py:857
  40.2 4.7 %deposit.2.refs_2_ = f32[5,512,128]{2,1,0:T(8,128)S(1)} custom-call(f32[760,128]{1,0:T(8,128)S(1)} %get-tuple-element.64.refs_0_), custom_call_target="tpu_custom_call" | custom-call | flops 5000000000 | bytes 15000000 | tf_op jit(solution)/shard_map/deposit/pallas_call | solution.py:333
  45.5 8.7 %deposit.3 = (bf16[32,48,256]{2,1,0:T(8,128)(2,1)S(1)}, f32[2,8,64,128]{3,2,1,0:T(8,128)S(1)}, f32[9,64,128]{2,1,0:T(8,128)S(1)}, f32[9,64,128]{2,1,0:T(8,128)S(1)}, f32[8,128]{1,0:T(8,128)S(1)}) custom-call(f32[760,128]{1,0:T(8,128)S(1)} %collective-permute-done.4.refs_0_, f32[760,128]{1,0:T(8,128)S(1)} %collective-permute-done.5.refs_1_, ...), custom_call_target="tpu_custom_call" | custom-call | flops 10000000000 | bytes 30000000 | tf_op jit(solution)/shard_map/deposit/pallas_call | solution.py:333
  54.3 0.8 collective-permute-start.6
  55.0 4.9 %collective-permute-start.7 = (f32[9,64,128]{2,1,0:T(8,128)S(1)}, f32[9,64,128]{2,1,0:T(8,128)S(1)}, u32[]{:S(2)}, u32[]{:S(2)}) collective-permute-start(f32[9,64,128]{2,1,0:T(8,128)S(1)} %get-tuple-element.40.sent_1), channel_id=1, source_target_pairs={{8,16},{24,32},{40,48},{56,64},{72,80},{88,96},{104,112},{16,8},{3... | collective-permute-start | bytes 884744 | tf_op jit(solution)/shard_map/ppermute | solution.py:857
  59.9 3.5 %inverse.1 = (s32[24,8,128]{2,1,0:T(8,128)S(1)}, s32[24,8,128]{2,1,0:T(8,128)S(1)}, f32[8,128]{1,0:T(8,128)S(1)}) custom-call(s32[24,8,128]{2,1,0:T(8,128)S(1)} %get-tuple-element.41.keys_a, s32[24,8,128]{2,1,0:T(8,128)S(1)} %get-tuple-element.42.keys_b, f32[8,128]{1,0:T(8,128)S(1)} %get-tuple-element.43.after), custom_call_target="tpu_custom_call" | custom-call | flops 1000000000 | bytes 20000000 | tf_op jit(solution)/shard_map/inverse/pallas_call | solution.py:186
  63.4 4.5 %collective-permute-done.7.got_1 = f32[9,64,128]{2,1,0:T(8,128)S(1)} collective-permute-done((f32[9,64,128]{2,1,0:T(8,128)S(1)}, f32[9,64,128]{2,1,0:T(8,128)S(1)}, u32[]{:S(2)}, u32[]{:S(2)}) %collective-permute-start.7) | collective-permute-done | bytes 294944 | tf_op jit(solution)/shard_map/ppermute | solution.py:857
  68.3 1.9 %collective-permute-start.9 = (f32[3,64,128]{2,1,0:T(8,128)S(1)}, f32[3,64,128]{2,1,0:T(8,128)S(1)}, u32[]{:S(2)}, u32[]{:S(2)}) collective-permute-start(f32[3,64,128]{2,1,0:T(8,128)S(1)} %pack_edges.1.packed), channel_id=1, source_target_pairs={{1,2},{3,4},{5,6},{2,1},{4,3},{6,5},{9,10},{11,12},{13,14},{10,9},... | collective-permute-start | bytes 294920 | tf_op jit(solution)/shard_map/ppermute | solution.py:857
  70.2 1.6 %collective-permute-start.8 = (f32[3,64,128]{2,1,0:T(8,128)S(1)}, f32[3,64,128]{2,1,0:T(8,128)S(1)}, u32[]{:S(2)}, u32[]{:S(2)}) collective-permute-start(f32[3,64,128]{2,1,0:T(8,128)S(1)} %pack_edges.1.packed), channel_id=1, source_target_pairs={{0,1},{2,3},{4,5},{6,7},{1,0},{3,2},{5,4},{7,6},{8,9},{10,11},{12,... | collective-permute-start | bytes 294920 | tf_op jit(solution)/shard_map/ppermute | solution.py:857
  71.8 2.4 %collective-permute-done.9.edge_1 = f32[3,64,128]{2,1,0:T(8,128)S(1)} collective-permute-done((f32[3,64,128]{2,1,0:T(8,128)S(1)}, f32[3,64,128]{2,1,0:T(8,128)S(1)}, u32[]{:S(2)}, u32[]{:S(2)}) %collective-permute-start.9) | collective-permute-done | bytes 98336 | tf_op jit(solution)/shard_map/ppermute | solution.py:857
  74.2 3.0 %sweeps.1 = (f32[3,10,64,128]{3,2,1,0:T(8,128)S(1)}, f32[3,8,64,128]{3,2,1,0:T(8,128)S(1)}, f32[128,1,128]{2,1,0:T(1,128)S(1)}) custom-call(f32[2,8,64,128]{3,2,1,0:T(8,128)S(1)} %get-tuple-element.38.own, f32[9,64,128]{2,1,0:T(8,128)S(1)} %get-tuple-element.39.sent_0, f32[9,64,128]{2,1,0:T(8,128)S(1)} %get-tuple-element.40.sent_1, ...), custom_call_target="tpu_custom_call" | custom-call | tf_op jit(solution)/shard_map/sweeps/pallas_call | solution.py:676
  77.3 16.7 %all_to_all.5.all_moments = f32[128,1,128]{2,1,0:T(1,128)S(1)} all-to-all(f32[128,1,128]{2,1,0:T(1,128)S(1)} %get-tuple-element.45), channel_id=1, replica_groups=mesh['gx'=16,'gy'=8] {'gx','gy'}, dimensions={0} | all-to-all | bytes 131072 | tf_op jit(solution)/shard_map/all_to_all | solution.py:879
  94.0 1.3 gradients.1
  95.2 8.9 %interp.2 = (f32[360,128]{1,0:T(8,128)S(1)}, f32[360,128]{1,0:T(8,128)S(1)}, f32[8,128]{1,0:T(8,128)S(1)}) custom-call(f32[760,128]{1,0:T(8,128)S(1)} %collective-permute-done.4.refs_0_, f32[760,128]{1,0:T(8,128)S(1)} %collective-permute-done.5.refs_1_, bf16[32,48,256]{2,1,0:T(8,128)(2,1)S(1)} %get-tuple-element.49.refs_2_.refs_1_, ...), custom_call_target="tpu_custom_call" | custom-call | flops 10000000000 | bytes 30000000 | tf_op jit(solution)/shard_map/interp/pallas_call | solution.py:415
  104.2 3.8 %collective-permute-start.11 = (f32[360,128]{1,0:T(8,128)S(1)}, f32[360,128]{1,0:T(8,128)S(1)}, u32[]{:S(2)}, u32[]{:S(2)}) collective-permute-start(f32[360,128]{1,0:T(8,128)S(1)} %get-tuple-element.54), channel_id=1, source_target_pairs={{1,2},{3,4},{5,6},{2,1},{4,3},{6,5},{9,10},{11,12},{13,14},{10,9},... | collective-permute-start | bytes 552968 | tf_op jit(solution)/shard_map/ppermute | solution.py:857
  108.0 5.3 %interp.3 = (f32[360,128]{1,0:T(8,128)S(1)}, f32[8,128]{1,0:T(8,128)}) custom-call(f32[760,128]{1,0:T(8,128)S(1)} %get-tuple-element.64.refs_0_, bf16[32,48,256]{2,1,0:T(8,128)(2,1)S(1)} %get-tuple-element.49.refs_2_.refs_1_, bf16[32,48,256]{2,1,0:T(8,128)(2,1)S(1)} %get-tuple-element.50.refs_3_.refs_2_, f32[8,128]{1,0:T(8,128)S(1)} %get-tuple-element.52.refs_3_), custom_call_target="tpu_custom_call" | custom-call | flops 5000000000 | bytes 15000000 | tf_op jit(solution)/shard_map/interp/pallas_call | solution.py:415
  113.4 1.5 %collective-permute-start.12 = (f32[216,128]{1,0:T(8,128)S(1)}, f32[216,128]{1,0:T(8,128)S(1)}, u32[]{:S(2)}, u32[]{:S(2)}) collective-permute-start(f32[216,128]{1,0:T(8,128)S(1)} %get-tuple-element.55), channel_id=1, source_target_pairs={{0,16},{8,24},{32,48},{40,56},{64,80},{72,88},{96,112},{104,120},{... | collective-permute-start | bytes 331784 | tf_op jit(solution)/shard_map/ppermute | solution.py:857
  114.9 4.8 %collective-permute-start.13 = (f32[216,128]{1,0:T(8,128)S(1)}, f32[216,128]{1,0:T(8,128)S(1)}, u32[]{:S(2)}, u32[]{:S(2)}) collective-permute-start(f32[216,128]{1,0:T(8,128)S(1)} %get-tuple-element.56), channel_id=1, source_target_pairs={{16,32},{24,40},{48,64},{56,72},{80,96},{88,104},{32,16},{40,24},{... | collective-permute-start | bytes 331784 | tf_op jit(solution)/shard_map/ppermute | solution.py:857
  119.7 0.9 collective-permute-start.14
  120.7 3.1 %collective-permute-start.15 = (f32[216,128]{1,0:T(8,128)S(1)}, f32[216,128]{1,0:T(8,128)S(1)}, u32[]{:S(2)}, u32[]{:S(2)}) collective-permute-start(f32[216,128]{1,0:T(8,128)S(1)} %get-tuple-element.59), channel_id=1, source_target_pairs={{8,16},{24,32},{40,48},{56,64},{72,80},{88,96},{104,112},{16,8},{3... | collective-permute-start | bytes 331784 | tf_op jit(solution)/shard_map/ppermute | solution.py:857
  124.6 4.8 %collective-permute-done.15.refs_4_ = f32[216,128]{1,0:T(8,128)S(1)} collective-permute-done((f32[216,128]{1,0:T(8,128)S(1)}, f32[216,128]{1,0:T(8,128)S(1)}, u32[]{:S(2)}, u32[]{:S(2)}) %collective-permute-start.15) | collective-permute-done | bytes 110624 | tf_op jit(solution)/shard_map/ppermute | solution.py:857
  129.4 5.2 %place_forces.1 = f32[3,1,128,3072]{3,2,1,0:T(8,128)} custom-call(f32[216,128]{1,0:T(8,128)S(1)} %collective-permute-done.12.refs_0_, f32[216,128]{1,0:T(8,128)S(1)} %collective-permute-done.13.refs_1_, f32[216,128]{1,0:T(8,128)S(1)} %get-tuple-element.57.refs_2_, f32[216,128]{1,0:T(8,128)S(1)} %collective-permute-done.14.refs_3_, ...), custom_call_target="tpu_custom_call" | custom-call | tf_op jit(solution)/shard_map/place_forces/pallas_call | solution.py:836
  (26 shorter events, 2.2 us)
Async XLA Ops:
  0.6 1.9 %copy-start = (s32[2,1,128,3072]{3,2,1,0:T(8,128)S(1)}, s32[2,1,128,3072]{3,2,1,0:T(8,128)}, u32[]{:S(2)}) copy-start(s32[2,1,128,3072]{3,2,1,0:T(8,128)} %cells_ref.3) | copy-start | bytes 9437188
  2.5 0.7 copy-start.1
  10.7 20.4 %collective-permute-start = (f32[456,128]{1,0:T(8,128)S(1)}, f32[456,128]{1,0:T(8,128)S(1)}, u32[]{:S(2)}, u32[]{:S(2)}) collective-permute-start(f32[456,128]{1,0:T(8,128)S(1)} %get-tuple-element.32), channel_id=1, source_target_pairs={{0,16},{8,24},{32,48},{40,56},{64,80},{72,88},{96,112},{104,120},{... | collective-permute-start | bytes 700424 | tf_op jit(solution)/shard_map/ppermute | solution.py:857
  14.7 16.5 %collective-permute-start.1 = (f32[456,128]{1,0:T(8,128)S(1)}, f32[456,128]{1,0:T(8,128)S(1)}, u32[]{:S(2)}, u32[]{:S(2)}) collective-permute-start(f32[456,128]{1,0:T(8,128)S(1)} %get-tuple-element.33), channel_id=1, source_target_pairs={{16,32},{24,40},{48,64},{56,72},{80,96},{88,104},{32,16},{40,24},{... | collective-permute-start | bytes 700424 | tf_op jit(solution)/shard_map/ppermute | solution.py:857
  24.2 7.2 %collective-permute-start.2 = (f32[456,128]{1,0:T(8,128)S(1)}, f32[456,128]{1,0:T(8,128)S(1)}, u32[]{:S(2)}, u32[]{:S(2)}) collective-permute-start(f32[456,128]{1,0:T(8,128)S(1)} %get-tuple-element.35), channel_id=1, source_target_pairs={{0,8},{16,24},{32,40},{48,56},{64,72},{80,88},{96,104},{112,120},{... | collective-permute-start | bytes 700424 | tf_op jit(solution)/shard_map/ppermute | solution.py:857
  25.8 10.6 %collective-permute-start.3 = (f32[456,128]{1,0:T(8,128)S(1)}, f32[456,128]{1,0:T(8,128)S(1)}, u32[]{:S(2)}, u32[]{:S(2)}) collective-permute-start(f32[456,128]{1,0:T(8,128)S(1)} %get-tuple-element.36), channel_id=1, source_target_pairs={{8,16},{24,32},{40,48},{56,64},{72,80},{88,96},{104,112},{16,8},{3... | collective-permute-start | bytes 700424 | tf_op jit(solution)/shard_map/ppermute | solution.py:857
  36.5 9.1 %collective-permute-start.5 = (f32[760,128]{1,0:T(8,128)S(1)}, f32[760,128]{1,0:T(8,128)S(1)}, u32[]{:S(2)}, u32[]{:S(2)}) collective-permute-start(f32[760,128]{1,0:T(8,128)S(1)} %get-tuple-element.62), channel_id=1, source_target_pairs={{1,2},{3,4},{5,6},{2,1},{4,3},{6,5},{9,10},{11,12},{13,14},{10,9},... | collective-permute-start | bytes 1167368 | tf_op jit(solution)/shard_map/ppermute | solution.py:857
  38.4 7.1 %collective-permute-start.4 = (f32[760,128]{1,0:T(8,128)S(1)}, f32[760,128]{1,0:T(8,128)S(1)}, u32[]{:S(2)}, u32[]{:S(2)}) collective-permute-start(f32[760,128]{1,0:T(8,128)S(1)} %get-tuple-element.63), channel_id=1, source_target_pairs={{0,1},{2,3},{4,5},{6,7},{1,0},{3,2},{5,4},{7,6},{8,9},{10,11},{12,... | collective-permute-start | bytes 1167368 | tf_op jit(solution)/shard_map/ppermute | solution.py:857
  40.2 5.4 %copy-start.2 = (f32[3,64,8,128]{3,2,1,0:T(8,128)S(1)}, f32[3,64,8,128]{3,2,1,0:T(8,128)}, u32[]{:S(2)}) copy-start(f32[3,64,8,128]{3,2,1,0:T(8,128)} %param.7) | copy-start | bytes 2359300
  54.3 9.1 %collective-permute-start.6 = (f32[9,64,128]{2,1,0:T(8,128)S(1)}, f32[9,64,128]{2,1,0:T(8,128)S(1)}, u32[]{:S(2)}, u32[]{:S(2)}) collective-permute-start(f32[9,64,128]{2,1,0:T(8,128)S(1)} %get-tuple-element.39.sent_0), channel_id=1, source_target_pairs={{0,8},{16,24},{32,40},{48,56},{64,72},{80,88},{96,104},{112,120},{... | collective-permute-start | bytes 884744 | tf_op jit(solution)/shard_map/ppermute | solution.py:857
  55.0 12.9 %collective-permute-start.7 = (f32[9,64,128]{2,1,0:T(8,128)S(1)}, f32[9,64,128]{2,1,0:T(8,128)S(1)}, u32[]{:S(2)}, u32[]{:S(2)}) collective-permute-start(f32[9,64,128]{2,1,0:T(8,128)S(1)} %get-tuple-element.40.sent_1), channel_id=1, source_target_pairs={{8,16},{24,32},{40,48},{56,64},{72,80},{88,96},{104,112},{16,8},{3... | collective-permute-start | bytes 884744 | tf_op jit(solution)/shard_map/ppermute | solution.py:857
  68.3 5.9 %collective-permute-start.9 = (f32[3,64,128]{2,1,0:T(8,128)S(1)}, f32[3,64,128]{2,1,0:T(8,128)S(1)}, u32[]{:S(2)}, u32[]{:S(2)}) collective-permute-start(f32[3,64,128]{2,1,0:T(8,128)S(1)} %pack_edges.1.packed), channel_id=1, source_target_pairs={{1,2},{3,4},{5,6},{2,1},{4,3},{6,5},{9,10},{11,12},{13,14},{10,9},... | collective-permute-start | bytes 294920 | tf_op jit(solution)/shard_map/ppermute | solution.py:857
  70.2 4.0 %collective-permute-start.8 = (f32[3,64,128]{2,1,0:T(8,128)S(1)}, f32[3,64,128]{2,1,0:T(8,128)S(1)}, u32[]{:S(2)}, u32[]{:S(2)}) collective-permute-start(f32[3,64,128]{2,1,0:T(8,128)S(1)} %pack_edges.1.packed), channel_id=1, source_target_pairs={{0,1},{2,3},{4,5},{6,7},{1,0},{3,2},{5,4},{7,6},{8,9},{10,11},{12,... | collective-permute-start | bytes 294920 | tf_op jit(solution)/shard_map/ppermute | solution.py:857
  104.1 9.2 %collective-permute-start.10 = (f32[360,128]{1,0:T(8,128)S(1)}, f32[360,128]{1,0:T(8,128)S(1)}, u32[]{:S(2)}, u32[]{:S(2)}) collective-permute-start(f32[360,128]{1,0:T(8,128)S(1)} %get-tuple-element.51), channel_id=1, source_target_pairs={{0,1},{2,3},{4,5},{6,7},{1,0},{3,2},{5,4},{7,6},{8,9},{10,11},{12,... | collective-permute-start | bytes 552968 | tf_op jit(solution)/shard_map/ppermute | solution.py:857
  104.2 9.1 %collective-permute-start.11 = (f32[360,128]{1,0:T(8,128)S(1)}, f32[360,128]{1,0:T(8,128)S(1)}, u32[]{:S(2)}, u32[]{:S(2)}) collective-permute-start(f32[360,128]{1,0:T(8,128)S(1)} %get-tuple-element.54), channel_id=1, source_target_pairs={{1,2},{3,4},{5,6},{2,1},{4,3},{6,5},{9,10},{11,12},{13,14},{10,9},... | collective-permute-start | bytes 552968 | tf_op jit(solution)/shard_map/ppermute | solution.py:857
  113.4 10.4 %collective-permute-start.12 = (f32[216,128]{1,0:T(8,128)S(1)}, f32[216,128]{1,0:T(8,128)S(1)}, u32[]{:S(2)}, u32[]{:S(2)}) collective-permute-start(f32[216,128]{1,0:T(8,128)S(1)} %get-tuple-element.55), channel_id=1, source_target_pairs={{0,16},{8,24},{32,48},{40,56},{64,80},{72,88},{96,112},{104,120},{... | collective-permute-start | bytes 331784 | tf_op jit(solution)/shard_map/ppermute | solution.py:857
  114.9 9.1 %collective-permute-start.13 = (f32[216,128]{1,0:T(8,128)S(1)}, f32[216,128]{1,0:T(8,128)S(1)}, u32[]{:S(2)}, u32[]{:S(2)}) collective-permute-start(f32[216,128]{1,0:T(8,128)S(1)} %get-tuple-element.56), channel_id=1, source_target_pairs={{16,32},{24,40},{48,64},{56,72},{80,96},{88,104},{32,16},{40,24},{... | collective-permute-start | bytes 331784 | tf_op jit(solution)/shard_map/ppermute | solution.py:857
  119.7 4.8 %collective-permute-start.14 = (f32[216,128]{1,0:T(8,128)S(1)}, f32[216,128]{1,0:T(8,128)S(1)}, u32[]{:S(2)}, u32[]{:S(2)}) collective-permute-start(f32[216,128]{1,0:T(8,128)S(1)} %get-tuple-element.58), channel_id=1, source_target_pairs={{0,8},{16,24},{32,40},{48,56},{64,72},{80,88},{96,104},{112,120},{... | collective-permute-start | bytes 331784 | tf_op jit(solution)/shard_map/ppermute | solution.py:857
  120.7 8.7 %collective-permute-start.15 = (f32[216,128]{1,0:T(8,128)S(1)}, f32[216,128]{1,0:T(8,128)S(1)}, u32[]{:S(2)}, u32[]{:S(2)}) collective-permute-start(f32[216,128]{1,0:T(8,128)S(1)} %get-tuple-element.59), channel_id=1, source_target_pairs={{8,16},{24,32},{40,48},{56,64},{72,80},{88,96},{104,112},{16,8},{3... | collective-permute-start | bytes 331784 | tf_op jit(solution)/shard_map/ppermute | solution.py:857
